TPU v7x, 256 devices: a whole 4x4x8 slice. The times are simulated.
256 devices in a mesh: rep: 4 (over z_lo), exp: 64 (over z_hi, y, x, core).
Axes of the slice: x: 4, y: 4, z: 8 (z_hi: 2, z_lo: 4; z = z_hi * 4 + z_lo), core: 2. Of those that a mesh axis runs over, the one named last changes fastest.
Arguments:
- tokens: bfloat16 [32768, 4096], P(('rep', 'exp')), may hold values from -6 to 6
- cotangent: bfloat16 [32768, 4096], P(('rep', 'exp')), may hold values from -6 to 6
- gates: bfloat16 [32768, 4, 2], P(('rep', 'exp')), may hold values from 0.099609375 to 1
- expert_ids: int32 [32768, 4, 2], P(('rep', 'exp')), may hold values from 0 to 127, as said below
- slots: int32 [32768, 4, 2], P(('rep', 'exp')), may hold values from 0 to 7, as said below
- w_gate: bfloat16 [128, 1024, 1024], P('exp', None, 'rep'), may hold values from -0.1875 to 0.1875
- w_up: bfloat16 [128, 1024, 1024], P('exp', None, 'rep'), may hold values from -0.1875 to 0.1875
- w_down: bfloat16 [128, 1024, 1024], P('exp', 'rep'), may hold values from -0.1875 to 0.1875
Outputs:
- token_grads: bfloat16 [32768, 4096], P(('rep', 'exp'))
- grad_gate: bfloat16 [128, 1024, 1024], P('exp', None, 'rep')
- grad_up: bfloat16 [128, 1024, 1024], P('exp', None, 'rep')
- grad_down: bfloat16 [128, 1024, 1024], P('exp', 'rep')
Inputs may be any that keep to these rules, and one draw needn't show every extreme that they name: `expert_ids`: the two experts of a sub-token differ. Every device's block holds more than 7 assignments to one expert. slots is the number of earlier assignments to the same expert among the 128 tokens of the same device (in the order of token, sub-token, choice), or 7 if that number is 7 or more, meaning the assignment is dropped.
All inputs are finite; a program needn't handle non-finite values.
Results may differ from a plain program's by a relative error of at most 0.015.
Values may be sent and summed in bfloat16 or wider, within the bound.
No kernel may reach another device: no remote copies, remote signals or barrier semaphores. Data moves between devices by JAX's collectives and lax.ppermute only.
A program may use at most 128 MiB of HBM per device.

v0:
```python
import jax
import jax.numpy as jnp
from jax import lax
from jax.experimental import pallas as pl
from jax.experimental.pallas import tpu as pltpu
from jax.sharding import Mesh
from jax.sharding import PartitionSpec as P

HEADS = 4
CAP = 7
EXPERTS = 128
SUB = 1024
PART = 256
STEP = 448
ROWS = EXPERTS * CAP
AXES = ("rep", "zh", "y", "x", "core")
EXP = ("zh", "y", "x", "core")
HOST = ("zh", "y", "x", "rep")
PAIR = ("rep", "core")
SWAP = [(0, 1), (1, 0)]
F32, BF16 = jnp.float32, jnp.bfloat16


def to_host(q):
    return [
        (h * 2 + k, (2 * k + (h + q) % 2) * 2 + h // 2) for h in range(4) for k in range(2)
    ]


def from_host(q):
    return [(b, a) for a, b in to_host(q)]


def tall(down):
    return jnp.concatenate([down[:, i * PART : (i + 1) * PART] for i in range(SUB // PART)], 0)


def wide(stack):
    return jnp.concatenate([stack[i * PART : (i + 1) * PART] for i in range(SUB // PART)], 1)


def dot(a, b, over):
    return lax.dot_general(a, b, ((over[:1], over[1:]), ((), ())), preferred_element_type=F32)


def expert_kernel(x_ref, dy_ref, own_ref, other_ref, dx_ref, dg_ref, du_ref, hid_ref, sum_ref):
    j = pl.program_id(0)

    def part(w_ref):
        def step(i, _):
            at = pl.ds(pl.multiple_of(i * STEP, STEP), STEP)
            x = x_ref[at, :]
            g = dot(x, w_ref[0, :SUB, :], (1, 0))
            u = dot(x, w_ref[0, SUB : 2 * SUB, :], (1, 0))
            dh = jnp.zeros((STEP, PART), F32)
            for f in range(SUB // PART):
                low = 2 * SUB + f * PART
                dh += dot(
                    dy_ref[at, f * PART : (f + 1) * PART], w_ref[0, low : low + PART, :], (1, 1)
                )
            sig = jax.nn.sigmoid(g)
            act = g * sig
            hid_ref[at, :] = (act * u).astype(BF16)
            d_up = (dh * act).astype(BF16)
            d_gate = (dh * u * sig * (1.0 + g * (1.0 - sig))).astype(BF16)
            du_ref[at, :] = d_up
            dg_ref[at, :] = d_gate
            term = dot(d_gate, w_ref[0, :SUB, :], (1, 1)) + dot(
                d_up, w_ref[0, SUB : 2 * SUB, :], (1, 1)
            )

            @pl.when(j == 0)
            def _():
                sum_ref[at, :] = term

            @pl.when(j > 0)
            def _():
                sum_ref[at, :] += term

            return 0

        lax.fori_loop(0, ROWS // STEP, step, 0)

    @pl.when(j < 2)
    def _():
        part(own_ref)

    @pl.when(j >= 2)
    def _():
        part(other_ref)

    @pl.when(j == 3)
    def _():
        dx_ref[...] = sum_ref[...].astype(BF16)


def expert(x, dy, own, other):
    whole = pl.BlockSpec((ROWS, SUB), lambda j: (0, 0))
    columns = pl.BlockSpec((ROWS, PART), lambda j: (0, j))
    out = jax.ShapeDtypeStruct((ROWS, SUB), BF16)
    return pl.pallas_call(
        expert_kernel,
        grid=(4,),
        in_specs=[
            whole,
            whole,
            pl.BlockSpec((1, 3 * SUB, PART), lambda j: (jnp.minimum(j, 1), 0, 0)),
            pl.BlockSpec((1, 3 * SUB, PART), lambda j: (jnp.maximum(j - 2, 0), 0, 0)),
        ],
        out_specs=[whole, columns, columns, columns],
        out_shape=[out] * 4,
        scratch_shapes=[pltpu.VMEM((ROWS, SUB), F32)],
        compiler_params=pltpu.CompilerParams(
            dimension_semantics=("arbitrary",), vmem_limit_bytes=48 * 1024 * 1024
        ),
        cost_estimate=pl.CostEstimate(
            flops=10 * ROWS * SUB * SUB, bytes_accessed=18 * 2**20, transcendentals=ROWS * SUB
        ),
    )(x, dy, own, other)


def on_device(tokens, cotangent, gates, expert_ids, slots, w_gate, w_up, w_down):
    toks = tokens.shape[0]
    rows = toks * HEADS
    h = lax.axis_index("rep")

    packed = jnp.stack(
        [jnp.concatenate([w_gate[p], w_up[p], tall(w_down[p])], 0) for p in range(2)], 0
    )
    own = jnp.stack(
        [
            lax.ppermute(
                lax.dynamic_index_in_dim(packed, (h + q) % 2, 0, keepdims=False), PAIR, to_host(q)
            )
            for q in range(2)
        ],
        0,
    )
    other = lax.ppermute(own, "core", SWAP)

    def heads_first(a):
        return jnp.transpose(a, (1, 0, 2)).reshape(rows, 2)

    ids = heads_first(expert_ids)
    slot = heads_first(slots)
    gate = heads_first(gates)
    target = jnp.where(slot < CAP, ids * CAP + slot, ROWS)
    place = lax.broadcasted_iota(jnp.int32, (ROWS, rows), 0)
    hit0 = target[:, 0][None, :] == place
    hit1 = target[:, 1][None, :] == place
    zero = jnp.zeros((), BF16)
    pick = (hit0 | hit1).astype(BF16)
    pick_gate = jnp.where(hit0, gate[:, 0][None, :], jnp.where(hit1, gate[:, 1][None, :], zero))

    def cut(a):
        return jnp.concatenate([a[:, i * SUB : (i + 1) * SUB] for i in range(HEADS)], 0)

    x_slot = dot(pick, cut(tokens), (1, 0)).astype(BF16)
    dy_slot = dot(pick_gate, cut(cotangent), (1, 0)).astype(BF16)

    lanes = CAP * SUB // 128
    sent = jnp.concatenate(
        [x_slot.reshape(EXPERTS, lanes, 128), dy_slot.reshape(EXPERTS, lanes, 128)], 1
    )
    got = lax.all_to_all(sent, HOST, 0, 0, tiled=True)
    x = got[:, :lanes].reshape(ROWS, SUB)
    dy = got[:, lanes:].reshape(ROWS, SUB)

    dx, d_gate, d_up, hidden = expert(x, dy, own, other)
    returned = lax.all_to_all(dx.reshape(EXPERTS, lanes, 128), HOST, 0, 0, tiled=True)
    returned = returned.reshape(ROWS, SUB)

    whole = (dot(x, d_gate, (0, 0)), dot(x, d_up, (0, 0)), dot(hidden, dy, (0, 0)))

    def pack(q):
        low, high = q * PART, (q + 1) * PART
        return jnp.concatenate(
            [whole[0][:, low:high], whole[1][:, low:high], tall(whole[2][low:high])], 0
        )

    theirs = lax.ppermute(jnp.stack([pack(2), pack(3)], 0).astype(BF16), "core", SWAP)
    back = [
        lax.ppermute((pack(q) + theirs[q].astype(F32)).astype(BF16), PAIR, from_host(q))
        for q in range(2)
    ]
    even = h % 2 == 0
    both = [jnp.where(even, back[0], back[1]), jnp.where(even, back[1], back[0])]
    grad_gate = jnp.stack([a[:SUB] for a in both], 0)
    grad_up = jnp.stack([a[SUB : 2 * SUB] for a in both], 0)
    grad_down = jnp.stack([wide(a[2 * SUB :]) for a in both], 0)

    summed = dot(pick, returned, (0, 0)).astype(BF16)
    token_grads = jnp.concatenate([summed[i * toks : (i + 1) * toks] for i in range(HEADS)], 1)
    return (token_grads, grad_gate, grad_up, grad_down)


def solution(mesh):
    fine = Mesh(mesh.devices.reshape(4, 2, 4, 4, 2), AXES)
    by_token = ("rep",) + EXP
    return jax.shard_map(
        on_device,
        mesh=fine,
        in_specs=(
            P(by_token, None),
            P(by_token, None),
            P(by_token, None, None),
            P(by_token, None, None),
            P(by_token, None, None),
            P(EXP, None, "rep"),
            P(EXP, None, "rep"),
            P(EXP, "rep", None),
        ),
        out_specs=(
            P(by_token, None),
            P(EXP, None, "rep"),
            P(EXP, None, "rep"),
            P(EXP, "rep", None),
        ),
        check_vma=False,
    )
```

profile of v0, /device:TPU:35, one launch (start us, length us, event | category | flops | bytes accessed | tf_op | source)
XLA Modules:
  0.0 361.8 jit_solution(2452741719020416322)
XLA Ops:
  2.1 1.3 fusion.44
  3.4 2.4 convolution_convert_fusion
  5.8 2.8 reshape.46
  8.7 2.4 convolution_convert_fusion.1
  11.0 3.9 %reshape.48 = bf16[128,56,128]{2,1,0:T(8,128)(2,1)} reshape(bf16[896,1024]{1,0:T(8,128)(2,1)} %convolution_convert_fusion.1) | data formatting | bytes 3670016 | tf_op jit(solution)/shard_map/reshape | solution.py:163
  14.9 3.6 pad_maximum_fusion
  18.5 14.9 %all-to-all-start = ((bf16[128,112,128]{2,1,0:T(8,128)(2,1)}), bf16[128,112,128]{2,1,0:T(8,128)(2,1)}, u32[]{:S(2)}, u32[]{:S(2)}) async-start(bf16[128,112,128]{2,1,0:T(8,128)(2,1)} %pad_maximum_fusion), calls=%async_computation | async-start | bytes 7340032 | tf_op jit(solution)/shard_map/all_to_all | solution.py:165
  35.3 1.1 fusion.8
  36.4 5.1 %collective-permute-start = (bf16[3072,256]{1,0:T(8,128)(2,1)S(1)}, bf16[3072,256]{1,0:T(8,128)(2,1)S(1)}, u32[]{:S(2)}, u32[]{:S(2)}) collective-permute-start(bf16[3072,256]{1,0:T(8,128)(2,1)S(1)} %get-tuple-element.32), channel_id=1, source_target_pairs={{0,0},{1,128},{64,64},{65,192},{128,1},{129,129},{192,65},{193,193... | collective-permute-start | bytes 4718600 | tf_op jit(solution)/shard_map/ppermute | solution.py:132
  41.7 106.2 %collective-permute-done = bf16[3072,256]{1,0:T(8,128)(2,1)S(1)} collective-permute-done((bf16[3072,256]{1,0:T(8,128)(2,1)S(1)}, bf16[3072,256]{1,0:T(8,128)(2,1)S(1)}, u32[]{:S(2)}, u32[]{:S(2)}) %collective-permute-start) | collective-permute-done | bytes 1572896 | tf_op jit(solution)/shard_map/ppermute | solution.py:132
  147.8 32.8 %collective-permute-done.1 = bf16[3072,256]{1,0:T(8,128)(2,1)S(1)} collective-permute-done((bf16[3072,256]{1,0:T(8,128)(2,1)S(1)}, bf16[3072,256]{1,0:T(8,128)(2,1)S(1)}, u32[]{:S(2)}, u32[]{:S(2)}) %collective-permute-start.1) | collective-permute-done | bytes 1572896 | tf_op jit(solution)/shard_map/ppermute | solution.py:132
  180.6 2.0 pad_maximum_fusion.1.own_ref
  182.6 4.0 %fusion.40 = (bf16[128,56,128]{2,1,0:T(8,128)(2,1)}, bf16[128,56,128]{2,1,0:T(8,128)(2,1)S(1)}) fusion(bf16[128,112,128]{2,1,0:T(8,128)(2,1)} %all-to-all-done), kind=kLoop, calls=%fused_computation.105 | loop fusion | bytes 7340032 | tf_op jit(solution)/shard_map/slice | solution.py:167
  186.6 3.9 %reshape.50.dy_ref = bf16[896,1024]{1,0:T(8,128)(2,1)} reshape(bf16[128,56,128]{2,1,0:T(8,128)(2,1)} %get-tuple-element.26) | data formatting | bytes 3670016 | tf_op jit(solution)/shard_map/reshape | solution.py:167
  190.4 1.7 reshape.49.x_ref
  192.1 24.6 %shard_map.111 = (bf16[896,1024]{1,0:T(8,128)(2,1)S(1)}, bf16[896,1024]{1,0:T(8,128)(2,1)S(1)}, bf16[896,1024]{1,0:T(8,128)(2,1)S(1)}, bf16[896,1024]{1,0:T(8,128)(2,1)}) custom-call(bf16[896,1024]{1,0:T(8,128)(2,1)} %reshape.49.x_ref, bf16[896,1024]{1,0:T(8,128)(2,1)} %reshape.50.dy_ref, bf16[2,3072,256]{2,1,0:T(8,128)(2,1)} %pad_maximum_fusion.1.own_ref, ...), custom_call_target="tpu_custom_call" | custom-call | flops 9395240960 | bytes 18874368 | tf_op jit(solution)/shard_map/pallas_call | solution.py:101
  216.8 6.0 %fusion.49 = (bf16[1024,1024]{1,0:T(8,128)(2,1)S(1)}, f32[1024,1024]{1,0:T(8,128)}) fusion(bf16[896,1024]{1,0:T(8,128)(2,1)} %get-tuple-element.11, bf16[896,1024]{1,0:T(8,128)(2,1)S(1)} %copy-done.1), kind=kOutput, calls=%fused_computation.114 | convolution fusion | flops 1880096768 | bytes 9961472 | tf_op jit(solution)/shard_map/dot_general | solution.py:43
  222.8 4.4 %fusion.47 = (bf16[1024,1024]{1,0:T(8,128)(2,1)S(1)}, f32[1024,1024]{1,0:T(8,128)}) fusion(bf16[896,1024]{1,0:T(8,128)(2,1)S(1)} %copy-done, bf16[896,1024]{1,0:T(8,128)(2,1)S(1)} %get-tuple-element.9), kind=kOutput, calls=%fused_computation.112 | convolution fusion | flops 1880096768 | bytes 9961472 | tf_op jit(solution)/shard_map/dot_general | solution.py:43
  227.3 4.4 %fusion.48 = (bf16[1024,1024]{1,0:T(8,128)(2,1)S(1)}, f32[1024,1024]{1,0:T(8,128)}) fusion(bf16[896,1024]{1,0:T(8,128)(2,1)S(1)} %copy-done, bf16[896,1024]{1,0:T(8,128)(2,1)S(1)} %get-tuple-element.10), kind=kOutput, calls=%fused_computation.113 | convolution fusion | flops 1880096768 | bytes 9961472 | tf_op jit(solution)/shard_map/dot_general | solution.py:43
  231.9 1.9 pad_maximum_fusion.2
  234.4 1.7 reshape.51
  236.1 11.8 %all-to-all-start.1 = ((bf16[128,56,128]{2,1,0:T(8,128)(2,1)}), bf16[128,56,128]{2,1,0:T(8,128)(2,1)S(1)}, u32[]{:S(2)}, u32[]{:S(2)}) async-start(bf16[128,56,128]{2,1,0:T(8,128)(2,1)} %reshape.51), calls=%async_computation.1 | async-start | bytes 3670016 | tf_op jit(solution)/shard_map/all_to_all | solution.py:170
  247.9 1.8 slice_dynamic-update-slice_fusion.3
  250.9 2.0 copy-done.2
  253.1 4.0 %fusion.1 = (bf16[3072,256]{1,0:T(8,128)(2,1)}, bf16[3072,256]{1,0:T(8,128)(2,1)S(1)}) fusion(f32[3072,256]{1,0:T(8,128)S(1)} %get-tuple-element.14, bf16[2,3072,256]{2,1,0:T(8,128)(2,1)} %collective-permute-done.3, f32[3072,256]{1,0:T(8,128)S(1)} %get-tuple-element.15), kind=kLoop, calls=%fused_computation.10 | loop fusion | flops 4718592 | bytes 12582912 | tf_op jit(solution)/shard_map/convert_element_type | solution.py:183
  257.0 4.9 %collective-permute-start.4 = (bf16[3072,256]{1,0:T(8,128)(2,1)}, bf16[3072,256]{1,0:T(8,128)(2,1)}, u32[]{:S(2)}, u32[]{:S(2)}) collective-permute-start(bf16[3072,256]{1,0:T(8,128)(2,1)} %get-tuple-element.30), channel_id=1, source_target_pairs={{0,0},{128,1},{64,64},{192,65},{1,128},{129,129},{65,192},{193,193... | collective-permute-start | bytes 4718600 | tf_op jit(solution)/shard_map/ppermute | solution.py:183
  262.1 31.0 %all-to-all-done.1 = bf16[128,56,128]{2,1,0:T(8,128)(2,1)S(1)} async-done(((bf16[128,56,128]{2,1,0:T(8,128)(2,1)}), bf16[128,56,128]{2,1,0:T(8,128)(2,1)S(1)}, u32[]{:S(2)}, u32[]{:S(2)}) %all-to-all-start.1) | async-done | bytes 1835040 | tf_op jit(solution)/shard_map/all_to_all | solution.py:170
  293.0 1.7 reshape.52
  294.8 2.8 convolution_convert_fusion.2
  298.7 24.7 %collective-permute-done.4 = bf16[3072,256]{1,0:T(8,128)(2,1)} collective-permute-done((bf16[3072,256]{1,0:T(8,128)(2,1)}, bf16[3072,256]{1,0:T(8,128)(2,1)}, u32[]{:S(2)}, u32[]{:S(2)}) %collective-permute-start.4) | collective-permute-done | bytes 1572896 | tf_op jit(solution)/shard_map/ppermute | solution.py:183
  323.4 32.8 %collective-permute-done.5 = bf16[3072,256]{1,0:T(8,128)(2,1)} collective-permute-done((bf16[3072,256]{1,0:T(8,128)(2,1)S(1)}, bf16[3072,256]{1,0:T(8,128)(2,1)}, u32[]{:S(2)}, u32[]{:S(2)}) %collective-permute-start.5) | collective-permute-done | bytes 1572896 | tf_op jit(solution)/shard_map/ppermute | solution.py:183
  356.2 2.1 broadcast_select_fusion.1
  (58 shorter events, 10.2 us)
Async XLA Ops:
  5.8 2.8 copy-start.4
  18.5 15.0 %copy-start.5 = (bf16[2,256,1024]{2,1,0:T(8,128)(2,1)S(1)}, bf16[2,256,1024]{2,1,0:T(8,128)(2,1)}, u32[]{:S(2)}) copy-start(bf16[2,256,1024]{2,1,0:T(8,128)(2,1)} %param.15) | copy-start | bytes 3145732
  18.5 164.1 %all-to-all-start = ((bf16[128,112,128]{2,1,0:T(8,128)(2,1)}), bf16[128,112,128]{2,1,0:T(8,128)(2,1)}, u32[]{:S(2)}, u32[]{:S(2)}) async-start(bf16[128,112,128]{2,1,0:T(8,128)(2,1)} %pad_maximum_fusion), calls=%async_computation | async-start | bytes 7340032 | tf_op jit(solution)/shard_map/all_to_all | solution.py:165
  33.4 1.2 copy-start.6
  33.6 1.4 copy-start.7
  36.4 111.4 %collective-permute-start = (bf16[3072,256]{1,0:T(8,128)(2,1)S(1)}, bf16[3072,256]{1,0:T(8,128)(2,1)S(1)}, u32[]{:S(2)}, u32[]{:S(2)}) collective-permute-start(bf16[3072,256]{1,0:T(8,128)(2,1)S(1)} %get-tuple-element.32), channel_id=1, source_target_pairs={{0,0},{1,128},{64,64},{65,192},{128,1},{129,129},{192,65},{193,193... | collective-permute-start | bytes 4718600 | tf_op jit(solution)/shard_map/ppermute | solution.py:132
  41.6 139.0 %collective-permute-start.1 = (bf16[3072,256]{1,0:T(8,128)(2,1)S(1)}, bf16[3072,256]{1,0:T(8,128)(2,1)S(1)}, u32[]{:S(2)}, u32[]{:S(2)}) collective-permute-start(bf16[3072,256]{1,0:T(8,128)(2,1)S(1)} %get-tuple-element.33), channel_id=1, source_target_pairs={{0,64},{1,192},{64,0},{65,128},{128,65},{129,193},{192,1},{193,129... | collective-permute-start | bytes 4718600 | tf_op jit(solution)/shard_map/ppermute | solution.py:132
  182.6 9.6 %collective-permute-start.2 = (bf16[2,3072,256]{2,1,0:T(8,128)(2,1)}, bf16[2,3072,256]{2,1,0:T(8,128)(2,1)}, u32[]{:S(2)}, u32[]{:S(2)}) collective-permute-start(bf16[2,3072,256]{2,1,0:T(8,128)(2,1)} %pad_maximum_fusion.1.own_ref), channel_id=1, source_target_pairs={{0,1},{1,0},{2,3},{3,2},{4,5},{5,4},{6,7},{7,6},{8,9},{9,8},{10,11... | collective-permute-start | bytes 9437192 | tf_op jit(solution)/shard_map/ppermute | solution.py:139
  192.1 24.6 %copy-start.1 = (bf16[896,1024]{1,0:T(8,128)(2,1)S(1)}, bf16[896,1024]{1,0:T(8,128)(2,1)}, u32[]{:S(2)}) copy-start(bf16[896,1024]{1,0:T(8,128)(2,1)} %reshape.50.dy_ref) | copy-start | bytes 5505028
  216.8 6.0 %copy-start = (bf16[896,1024]{1,0:T(8,128)(2,1)S(1)}, bf16[896,1024]{1,0:T(8,128)(2,1)}, u32[]{:S(2)}) copy-start(bf16[896,1024]{1,0:T(8,128)(2,1)} %reshape.49.x_ref) | copy-start | bytes 5505028
  233.9 19.2 %collective-permute-start.3 = (bf16[2,3072,256]{2,1,0:T(8,128)(2,1)}, bf16[2,3072,256]{2,1,0:T(8,128)(2,1)}, u32[]{:S(2)}, u32[]{:S(2)}) collective-permute-start(bf16[2,3072,256]{2,1,0:T(8,128)(2,1)} %pad_maximum_fusion.2), channel_id=1, source_target_pairs={{0,1},{1,0},{2,3},{3,2},{4,5},{5,4},{6,7},{7,6},{8,9},{9,8},{10,11... | collective-permute-start | bytes 9437192 | tf_op jit(solution)/shard_map/ppermute | solution.py:181
  236.1 57.0 %all-to-all-start.1 = ((bf16[128,56,128]{2,1,0:T(8,128)(2,1)}), bf16[128,56,128]{2,1,0:T(8,128)(2,1)S(1)}, u32[]{:S(2)}, u32[]{:S(2)}) async-start(bf16[128,56,128]{2,1,0:T(8,128)(2,1)} %reshape.51), calls=%async_computation.1 | async-start | bytes 3670016 | tf_op jit(solution)/shard_map/all_to_all | solution.py:170
  247.8 2.8 copy-start.3
  250.7 2.2 copy-start.2
  257.0 66.4 %collective-permute-start.4 = (bf16[3072,256]{1,0:T(8,128)(2,1)}, bf16[3072,256]{1,0:T(8,128)(2,1)}, u32[]{:S(2)}, u32[]{:S(2)}) collective-permute-start(bf16[3072,256]{1,0:T(8,128)(2,1)} %get-tuple-element.30), channel_id=1, source_target_pairs={{0,0},{128,1},{64,64},{192,65},{1,128},{129,129},{65,192},{193,193... | collective-permute-start | bytes 4718600 | tf_op jit(solution)/shard_map/ppermute | solution.py:183
  262.0 94.2 %collective-permute-start.5 = (bf16[3072,256]{1,0:T(8,128)(2,1)S(1)}, bf16[3072,256]{1,0:T(8,128)(2,1)}, u32[]{:S(2)}, u32[]{:S(2)}) collective-permute-start(bf16[3072,256]{1,0:T(8,128)(2,1)S(1)} %get-tuple-element.31), channel_id=1, source_target_pairs={{64,0},{192,1},{0,64},{128,65},{65,128},{193,129},{1,192},{129,193... | collective-permute-start | bytes 4718600 | tf_op jit(solution)/shard_map/ppermute | solution.py:183
where the time goes:
time: 363 us; the launch traced here: 362 us
  waiting for transfers between devices  227 us (63%)
  starting transfers between devices  37.5 us (10%)
  local copies, waits for them, and re-layouts  29.2 us (8%)
  Pallas kernels  24.6 us (7%)
  matrix products  22.3 us (6%)
  other arithmetic  19.8 us (5%)
    ppermute x2, waiting for transfers between devices, on_device(): lax.ppermute(lax.dynamic_index_in_dim(packed, (h + q) % 2, 0, keepdims=Fa...  139 us
    ppermute x2, waiting for transfers between devices, on_device(): lax.ppermute((pack(q) + theirs[q].astype(F32)).astype(BF16), PAIR, from_h...  57.5 us
    all_to_all x1, waiting for transfers between devices, on_device(): lax.all_to_all(dx.reshape(EXPERTS, lanes, 128), HOST, 0, 0, tiled=True)  31 us
    pallas_call x1, Pallas kernels, expert(): pl.pallas_call(expert_kernel, grid=(4,), in_specs=[whole, whole, pl.Block...  24.6 us
    dot_general x6, matrix products, dot(): lax.dot_general(a, b, ((over[:1], over[1:]), ((), ())), preferred_element...  22.3 us
    all_to_all x1, starting transfers between devices, on_device(): got = lax.all_to_all(sent, HOST, 0, 0, tiled=True)  14.9 us
    all_to_all x1, starting transfers between devices, on_device(): lax.all_to_all(dx.reshape(EXPERTS, lanes, 128), HOST, 0, 0, tiled=True)  11.8 us
  transfers between devices with their start and end apart: 8, of which 5 were waited for; matrix products, arithmetic and copies ran while one was open for 7% of the time, Pallas kernels for 0%

commit v1 on v0

--- a/solution.py
+++ b/solution.py
@@ -15,8 +15,9 @@
 ROWS = EXPERTS * CAP
 AXES = ("rep", "zh", "y", "x", "core")
 EXP = ("zh", "y", "x", "core")
-HOST = ("zh", "y", "x", "rep")
 PAIR = ("rep", "core")
+PLANES = 8
+YX = 16
 SWAP = [(0, 1), (1, 0)]
 F32, BF16 = jnp.float32, jnp.bfloat16
 
@@ -43,7 +44,7 @@
     return lax.dot_general(a, b, ((over[:1], over[1:]), ((), ())), preferred_element_type=F32)
 
 
-def expert_kernel(x_ref, dy_ref, own_ref, other_ref, dx_ref, dg_ref, du_ref, hid_ref, sum_ref):
+def forward_kernel(x_ref, own_ref, other_ref, act_ref, fac_ref, hid_ref, gt_ref, ut_ref, dt_ref):
     j = pl.program_id(0)
 
     def part(w_ref):
@@ -52,34 +53,19 @@
             x = x_ref[at, :]
             g = dot(x, w_ref[0, :SUB, :], (1, 0))
             u = dot(x, w_ref[0, SUB : 2 * SUB, :], (1, 0))
-            dh = jnp.zeros((STEP, PART), F32)
-            for f in range(SUB // PART):
-                low = 2 * SUB + f * PART
-                dh += dot(
-                    dy_ref[at, f * PART : (f + 1) * PART], w_ref[0, low : low + PART, :], (1, 1)
-                )
             sig = jax.nn.sigmoid(g)
             act = g * sig
+            act_ref[at, :] = act
+            fac_ref[at, :] = u * sig * (1.0 + g * (1.0 - sig))
             hid_ref[at, :] = (act * u).astype(BF16)
-            d_up = (dh * act).astype(BF16)
-            d_gate = (dh * u * sig * (1.0 + g * (1.0 - sig))).astype(BF16)
-            du_ref[at, :] = d_up
-            dg_ref[at, :] = d_gate
-            term = dot(d_gate, w_ref[0, :SUB, :], (1, 1)) + dot(
-                d_up, w_ref[0, SUB : 2 * SUB, :], (1, 1)
-            )
-
-            @pl.when(j == 0)
-            def _():
-                sum_ref[at, :] = term
-
-            @pl.when(j > 0)
-            def _():
-                sum_ref[at, :] += term
-
             return 0
 
         lax.fori_loop(0, ROWS // STEP, step, 0)
+        gt_ref[...] = w_ref[0, :SUB, :].T
+        ut_ref[...] = w_ref[0, SUB : 2 * SUB, :].T
+        for f in range(SUB // PART):
+            low = 2 * SUB + f * PART
+            dt_ref[f * PART : (f + 1) * PART, :] = w_ref[0, low : low + PART, :].T
 
     @pl.when(j < 2)
     def _():
@@ -89,34 +75,58 @@
     def _():
         part(other_ref)
 
-    @pl.when(j == 3)
-    def _():
-        dx_ref[...] = sum_ref[...].astype(BF16)
-
-
-def expert(x, dy, own, other):
-    whole = pl.BlockSpec((ROWS, SUB), lambda j: (0, 0))
+
+def backward_kernel(dy_ref, act_ref, fac_ref, gt_ref, ut_ref, dt_ref, dg_ref, du_ref, dx_ref):
+    dh = dot(dy_ref[...], dt_ref[...], (1, 0))
+    du_ref[...] = (dh * act_ref[...]).astype(BF16)
+    dg_ref[...] = (dh * fac_ref[...]).astype(BF16)
+    dx = dot(dg_ref[...], gt_ref[...], (1, 0)) + dot(du_ref[...], ut_ref[...], (1, 0))
+    dx_ref[...] = dx.astype(BF16)
+
+
+def params():
+    return pltpu.CompilerParams(
+        dimension_semantics=("arbitrary",), vmem_limit_bytes=48 * 1024 * 1024
+    )
+
+
+def forward(x, own, other):
     columns = pl.BlockSpec((ROWS, PART), lambda j: (0, j))
-    out = jax.ShapeDtypeStruct((ROWS, SUB), BF16)
+    float_out = jax.ShapeDtypeStruct((ROWS, SUB), F32)
+    square = jax.ShapeDtypeStruct((SUB, SUB), BF16)
     return pl.pallas_call(
-        expert_kernel,
+        forward_kernel,
         grid=(4,),
         in_specs=[
-            whole,
-            whole,
+            pl.BlockSpec((ROWS, SUB), lambda j: (0, 0)),
             pl.BlockSpec((1, 3 * SUB, PART), lambda j: (jnp.minimum(j, 1), 0, 0)),
             pl.BlockSpec((1, 3 * SUB, PART), lambda j: (jnp.maximum(j - 2, 0), 0, 0)),
         ],
-        out_specs=[whole, columns, columns, columns],
-        out_shape=[out] * 4,
-        scratch_shapes=[pltpu.VMEM((ROWS, SUB), F32)],
-        compiler_params=pltpu.CompilerParams(
-            dimension_semantics=("arbitrary",), vmem_limit_bytes=48 * 1024 * 1024
-        ),
+        out_specs=[columns] * 3
+        + [pl.BlockSpec((PART, SUB), lambda j: (j, 0))] * 2
+        + [pl.BlockSpec((SUB, PART), lambda j: (0, j))],
+        out_shape=[float_out, float_out, jax.ShapeDtypeStruct((ROWS, SUB), BF16)] + [square] * 3,
+        compiler_params=params(),
         cost_estimate=pl.CostEstimate(
-            flops=10 * ROWS * SUB * SUB, bytes_accessed=18 * 2**20, transcendentals=ROWS * SUB
-        ),
-    )(x, dy, own, other)
+            flops=4 * ROWS * SUB * SUB, bytes_accessed=24 * 2**20, transcendentals=ROWS * SUB
+        ),
+    )(x, own, other)
+
+
+def backward(dy, act, fac, gate_t, up_t, down_t):
+    some = pl.BlockSpec((STEP, SUB), lambda i: (i, 0))
+    square = pl.BlockSpec((SUB, SUB), lambda i: (0, 0))
+    return pl.pallas_call(
+        backward_kernel,
+        grid=(ROWS // STEP,),
+        in_specs=[some] * 3 + [square] * 3,
+        out_specs=[some] * 3,
+        out_shape=[jax.ShapeDtypeStruct((ROWS, SUB), BF16)] * 3,
+        compiler_params=params(),
+        cost_estimate=pl.CostEstimate(
+            flops=6 * ROWS * SUB * SUB, bytes_accessed=20 * 2**20, transcendentals=0
+        ),
+    )(dy, act, fac, gate_t, up_t, down_t)
 
 
 def on_device(tokens, cotangent, gates, expert_ids, slots, w_gate, w_up, w_down):
@@ -144,7 +154,8 @@
     ids = heads_first(expert_ids)
     slot = heads_first(slots)
     gate = heads_first(gates)
-    target = jnp.where(slot < CAP, ids * CAP + slot, ROWS)
+    first = (((ids >> 2) & 15) * PLANES + (ids >> 6) * 4 + (ids & 3)) * CAP
+    target = jnp.where(slot < CAP, first + slot, ROWS)
     place = lax.broadcasted_iota(jnp.int32, (ROWS, rows), 0)
     hit0 = target[:, 0][None, :] == place
     hit1 = target[:, 1][None, :] == place
@@ -155,20 +166,30 @@
     def cut(a):
         return jnp.concatenate([a[:, i * SUB : (i + 1) * SUB] for i in range(HEADS)], 0)
 
+    def in_plane(a):
+        a = a.reshape(YX, PLANES * CAP, SUB)
+        return lax.all_to_all(a, ("y", "x"), 0, 0, tiled=True).reshape(ROWS, SUB)
+
+    def along_z(a):
+        a = a.reshape(PLANES, YX * CAP, SUB)
+        return lax.all_to_all(a, ("zh", "rep"), 0, 0, tiled=True).reshape(ROWS, SUB)
+
+    row = jnp.arange(ROWS, dtype=jnp.int32)
+    plane, rest = row // (YX * CAP), row % (YX * CAP)
+    source = (rest // CAP) * (PLANES * CAP) + plane * CAP + rest % CAP
+    regroup = (source[:, None] == row[None, :]).astype(BF16)
+
     x_slot = dot(pick, cut(tokens), (1, 0)).astype(BF16)
     dy_slot = dot(pick_gate, cut(cotangent), (1, 0)).astype(BF16)
-
-    lanes = CAP * SUB // 128
-    sent = jnp.concatenate(
-        [x_slot.reshape(EXPERTS, lanes, 128), dy_slot.reshape(EXPERTS, lanes, 128)], 1
-    )
-    got = lax.all_to_all(sent, HOST, 0, 0, tiled=True)
-    x = got[:, :lanes].reshape(ROWS, SUB)
-    dy = got[:, lanes:].reshape(ROWS, SUB)
-
-    dx, d_gate, d_up, hidden = expert(x, dy, own, other)
-    returned = lax.all_to_all(dx.reshape(EXPERTS, lanes, 128), HOST, 0, 0, tiled=True)
-    returned = returned.reshape(ROWS, SUB)
+    x_rows = dot(regroup, in_plane(x_slot), (1, 0)).astype(BF16)
+    dy_rows = dot(regroup, in_plane(dy_slot), (1, 0)).astype(BF16)
+    x_rows, dy_rows, own = lax.optimization_barrier((x_rows, dy_rows, own))
+    other = lax.ppermute(own, "core", SWAP)
+    x = along_z(x_rows)
+    act, fac, hidden, gate_t, up_t, down_t = forward(x, own, other)
+    dy = along_z(dy_rows)
+    d_gate, d_up, dx = backward(dy, act, fac, gate_t, up_t, down_t)
+    dx = along_z(dx)
 
     whole = (dot(x, d_gate, (0, 0)), dot(x, d_up, (0, 0)), dot(hidden, dy, (0, 0)))
 
@@ -179,10 +200,12 @@
         )
 
     theirs = lax.ppermute(jnp.stack([pack(2), pack(3)], 0).astype(BF16), "core", SWAP)
+    dx, theirs = lax.optimization_barrier((dx, theirs))
     back = [
         lax.ppermute((pack(q) + theirs[q].astype(F32)).astype(BF16), PAIR, from_host(q))
         for q in range(2)
     ]
+    returned = in_plane(dot(regroup, dx, (0, 0)).astype(BF16))
     even = h % 2 == 0
     both = [jnp.where(even, back[0], back[1]), jnp.where(even, back[1], back[0])]
     grad_gate = jnp.stack([a[:SUB] for a in both], 0)

time: 363 us -> 354 us (0.975)
  starting transfers between devices: 37.5 us -> 52.3 us
  local copies, waits for them, and re-layouts: 29.2 us -> 15.3 us
  waiting for transfers between devices: 227 us -> 214 us
  matrix products: 22.3 us -> 28.6 us
    ppermute x2, waiting for transfers between devices: 139 us -> 50.3 us  [on_device(): lax.ppermute(lax.dynamic_index_in_dim(packed, (h + q) % 2, 0, keepdims=Fa...]
    all_to_all x2 -> x6, waiting for transfers between devices: 31 us -> 104 us  [the longest x3 96.3 us: along_z(): return lax.all_to_all(a, ('zh', 'rep'), 0, 0, tiled=True).reshape(ROWS, SUB)]
    reshape x6 -> x0, local copies, waits for them, and re-layouts: 15.6 us -> none  [the longest x1 3.86 us: on_device(): dy = got[:, lanes:].reshape(ROWS, SUB)]
    all_to_all x2 -> x6, starting transfers between devices: 26.7 us -> 39.3 us  [the longest x3 21.5 us: in_plane(): return lax.all_to_all(a, ('y', 'x'), 0, 0, tiled=True).reshape(ROWS, SUB)]
    dot_general x6 -> x9, matrix products: 22.3 us -> 28.6 us  [dot(): lax.dot_general(a, b, ((over[:1], over[1:]), ((), ())), preferred_element...]
    unnamed x33 -> x41, local copies, waits for them, and re-layouts: 6.99 us -> 12.5 us
    slice x1 -> x0, local copies, waits for them, and re-layouts: 3.96 us -> none  [on_device(): dy = got[:, lanes:].reshape(ROWS, SUB)]
    pallas_call x1 -> x2, Pallas kernels: 24.6 us -> 23.4 us  [the longest x1 11.7 us: backward(): pl.pallas_call(backward_kernel, grid=(ROWS // STEP,), in_specs=[some] * 3...]
  transfers between devices with their start and end apart: 8 -> 12, of which waited for: 5 -> 9; matrix products, arithmetic and copies ran while one was open for 7% -> 11% of each run, Pallas kernels for 0% -> 3%
where the time goes in v1:
time: 354 us; the launch traced here: 353 us
  waiting for transfers between devices  214 us (60%)
  starting transfers between devices  52.3 us (15%)
  matrix products  28.6 us (8%)
  Pallas kernels  23.4 us (7%)
  other arithmetic  18.5 us (5%)
  local copies, waits for them, and re-layouts  15.3 us (4%)
    all_to_all x3, waiting for transfers between devices, along_z(): return lax.all_to_all(a, ('zh', 'rep'), 0, 0, tiled=True).reshape(ROWS, SUB)  96.3 us
    ppermute x2, waiting for transfers between devices, on_device(): lax.ppermute((pack(q) + theirs[q].astype(F32)).astype(BF16), PAIR, from_h...  57.3 us
    ppermute x2, waiting for transfers between devices, on_device(): lax.ppermute(lax.dynamic_index_in_dim(packed, (h + q) % 2, 0, keepdims=Fa...  50.3 us
    dot_general x9, matrix products, dot(): lax.dot_general(a, b, ((over[:1], over[1:]), ((), ())), preferred_element...  28.6 us
    all_to_all x3, starting transfers between devices, in_plane(): return lax.all_to_all(a, ('y', 'x'), 0, 0, tiled=True).reshape(ROWS, SUB)  21.5 us
    all_to_all x3, starting transfers between devices, along_z(): return lax.all_to_all(a, ('zh', 'rep'), 0, 0, tiled=True).reshape(ROWS, SUB)  17.8 us
    unnamed x41, local copies, waits for them, and re-layouts  12.5 us
    pallas_call x1, Pallas kernels, backward(): pl.pallas_call(backward_kernel, grid=(ROWS // STEP,), in_specs=[some] * 3...  11.7 us
  transfers between devices with their start and end apart: 12, of which 9 were waited for; matrix products, arithmetic and copies ran while one was open for 11% of the time, Pallas kernels for 3%

profile of v1, /device:TPU:35, one launch (start us, length us, event | category | flops | bytes accessed | tf_op | source)
XLA Modules:
  0.0 353.5 jit_solution(12888306526332182008)
XLA Ops:
  2.6 2.4 convolution_convert_fusion
  5.0 7.0 %all-to-all-start = ((bf16[16,56,1024]{2,1,0:T(8,128)(2,1)}), bf16[16,56,1024]{2,1,0:T(8,128)(2,1)}, u32[]{:S(2)}, u32[]{:S(2)}) async-start(bf16[16,56,1024]{2,1,0:T(8,128)(2,1)} %bitcast.5), calls=%async_computation | async-start | bytes 3670016 | tf_op jit(solution)/shard_map/all_to_all | solution.py:171
  16.8 2.9 fusion.17
  19.7 6.0 %collective-permute-start = (bf16[3072,256]{1,0:T(8,128)(2,1)}, bf16[3072,256]{1,0:T(8,128)(2,1)S(1)}, u32[]{:S(2)}, u32[]{:S(2)}) collective-permute-start(bf16[3072,256]{1,0:T(8,128)(2,1)} %get-tuple-element.50), channel_id=1, source_target_pairs={{0,0},{1,128},{64,64},{65,192},{128,1},{129,129},{192,65},{193,193... | collective-permute-start | bytes 4718600 | tf_op jit(solution)/shard_map/ppermute | solution.py:142
  26.0 2.4 convolution_convert_fusion.1
  28.3 7.2 %all-to-all-done = bf16[16,56,1024]{2,1,0:T(8,128)(2,1)} async-done(((bf16[16,56,1024]{2,1,0:T(8,128)(2,1)}), bf16[16,56,1024]{2,1,0:T(8,128)(2,1)}, u32[]{:S(2)}, u32[]{:S(2)}) %all-to-all-start) | async-done | bytes 1835040 | tf_op jit(solution)/shard_map/all_to_all | solution.py:171
  35.5 7.8 %all-to-all-start.1 = ((bf16[16,56,1024]{2,1,0:T(8,128)(2,1)}), bf16[16,56,1024]{2,1,0:T(8,128)(2,1)S(1)}, u32[]{:S(2)}, u32[]{:S(2)}) async-start(bf16[16,56,1024]{2,1,0:T(8,128)(2,1)} %bitcast.10), calls=%async_computation.1 | async-start | bytes 3670016 | tf_op jit(solution)/shard_map/all_to_all | solution.py:171
  43.4 33.4 %collective-permute-done = bf16[3072,256]{1,0:T(8,128)(2,1)S(1)} collective-permute-done((bf16[3072,256]{1,0:T(8,128)(2,1)}, bf16[3072,256]{1,0:T(8,128)(2,1)S(1)}, u32[]{:S(2)}, u32[]{:S(2)}) %collective-permute-start) | collective-permute-done | bytes 1572896 | tf_op jit(solution)/shard_map/ppermute | solution.py:142
  76.8 16.9 %collective-permute-done.1 = bf16[3072,256]{1,0:T(8,128)(2,1)} collective-permute-done((bf16[3072,256]{1,0:T(8,128)(2,1)}, bf16[3072,256]{1,0:T(8,128)(2,1)}, u32[]{:S(2)}, u32[]{:S(2)}) %collective-permute-start.1) | collective-permute-done | bytes 1572896 | tf_op jit(solution)/shard_map/ppermute | solution.py:142
  93.7 3.5 pad_maximum_fusion.own_ref
  97.1 4.8 %fusion.8 = bf16[896,1024]{1,0:T(8,128)(2,1)} fusion(bf16[896,1024]{1,0:T(8,128)(2,1)} %bitcast.6, s32[896]{0:T(1024)S(1)} %fusion.53), kind=kOutput, calls=%fused_computation.19 | convolution fusion | flops 1645887488 | bytes 3673600 | tf_op jit(solution)/shard_map/dot_general | solution.py:44
  102.0 3.4 fusion.9
  105.4 6.6 %all-to-all-start.3 = ((bf16[8,112,1024]{2,1,0:T(8,128)(2,1)}), bf16[8,112,1024]{2,1,0:T(8,128)(2,1)S(1)}, u32[]{:S(2)}, u32[]{:S(2)}) async-start(bf16[8,112,1024]{2,1,0:T(8,128)(2,1)} %bitcast.82), calls=%async_computation.3 | async-start | bytes 3670016 | tf_op jit(solution)/shard_map/all_to_all | solution.py:175
  113.4 42.0 %all-to-all-done.3 = bf16[8,112,1024]{2,1,0:T(8,128)(2,1)S(1)} async-done(((bf16[8,112,1024]{2,1,0:T(8,128)(2,1)}), bf16[8,112,1024]{2,1,0:T(8,128)(2,1)S(1)}, u32[]{:S(2)}, u32[]{:S(2)}) %all-to-all-start.3) | async-done | bytes 1835040 | tf_op jit(solution)/shard_map/all_to_all | solution.py:175
  155.4 6.9 %all-to-all-start.2 = ((bf16[8,112,1024]{2,1,0:T(8,128)(2,1)}), bf16[8,112,1024]{2,1,0:T(8,128)(2,1)}, u32[]{:S(2)}, u32[]{:S(2)}) async-start(bf16[8,112,1024]{2,1,0:T(8,128)(2,1)} %bitcast.80), calls=%async_computation.2 | async-start | bytes 3670016 | tf_op jit(solution)/shard_map/all_to_all | solution.py:175
  162.2 11.7 %shard_map.111 = (f32[896,1024]{1,0:T(8,128)}, f32[896,1024]{1,0:T(8,128)}, bf16[896,1024]{1,0:T(8,128)(2,1)S(1)}, bf16[1024,1024]{1,0:T(8,128)(2,1)S(1)}, bf16[...) custom-call(bf16[896,1024]{1,0:T(8,128)(2,1)S(1)} %bitcast.71, bf16[2,3072,256]{2,1,0:T(8,128)(2,1)} %pad_maximum_fusion.own_ref, ...), custom_call_target="tpu_custom_call" | custom-call | flops 3758096384 | bytes 25165824 | tf_op jit(solution)/shard_map/pallas_call | solution.py:97
  176.6 29.8 %all-to-all-done.2 = bf16[8,112,1024]{2,1,0:T(8,128)(2,1)} async-done(((bf16[8,112,1024]{2,1,0:T(8,128)(2,1)}), bf16[8,112,1024]{2,1,0:T(8,128)(2,1)}, u32[]{:S(2)}, u32[]{:S(2)}) %all-to-all-start.2) | async-done | bytes 1835040 | tf_op jit(solution)/shard_map/all_to_all | solution.py:175
  206.4 11.7 %shard_map.112 = (bf16[896,1024]{1,0:T(8,128)(2,1)S(1)}, bf16[896,1024]{1,0:T(8,128)(2,1)S(1)}, bf16[896,1024]{1,0:T(8,128)(2,1)}) custom-call(bf16[896,1024]{1,0:T(8,128)(2,1)} %bitcast.25.dy_ref, f32[896,1024]{1,0:T(8,128)} %get-tuple-element.21.act_ref, f32[896,1024]{1,0:T(8,128)} %get-tuple-element.22.fac_ref, bf16[1024,1024]{1,0:T(8,128)(2,1)} %copy-done.5, ...), custom_call_target="tpu_custom_call" | custom-call | flops 5637144576 | bytes 20971520 | tf_op jit(solution)/shard_map/pallas_call | solution.py:119
  220.5 4.3 %all-to-all-start.4 = ((bf16[8,112,1024]{2,1,0:T(8,128)(2,1)}), bf16[8,112,1024]{2,1,0:T(8,128)(2,1)}, u32[]{:S(2)}, u32[]{:S(2)}) async-start(bf16[8,112,1024]{2,1,0:T(8,128)(2,1)} %bitcast.28), calls=%async_computation.4 | async-start | bytes 3670016 | tf_op jit(solution)/shard_map/all_to_all | solution.py:175
  224.8 4.6 %fusion.76 = (bf16[1024,1024]{1,0:T(8,128)(2,1)S(1)}, f32[1024,1024]{1,0:T(8,128)S(1)}) fusion(bf16[896,1024]{1,0:T(8,128)(2,1)} %copy-done.2, bf16[896,1024]{1,0:T(8,128)(2,1)} %bitcast.25.dy_ref), kind=kOutput, calls=%fused_computation.145 | convolution fusion | flops 1880096768 | bytes 9961472 | tf_op jit(solution)/shard_map/dot_general | solution.py:44
  229.4 2.4 fusion.74
  233.3 2.4 fusion.75
  238.5 1.7 copy-done.6
  240.1 3.2 collective-permute-done.3
  243.4 24.5 %all-to-all-done.4 = bf16[8,112,1024]{2,1,0:T(8,128)(2,1)} async-done(((bf16[8,112,1024]{2,1,0:T(8,128)(2,1)}), bf16[8,112,1024]{2,1,0:T(8,128)(2,1)}, u32[]{:S(2)}, u32[]{:S(2)}) %all-to-all-start.4) | async-done | bytes 1835040 | tf_op jit(solution)/shard_map/all_to_all | solution.py:175
  267.9 5.2 %fusion.4 = (bf16[3072,256]{1,0:T(8,128)(2,1)}, bf16[3072,256]{1,0:T(8,128)(2,1)}) fusion(f32[3072,256]{1,0:T(8,128)S(1)} %get-tuple-element.34, bf16[2,3072,256]{2,1,0:T(8,128)(2,1)} %collective-permute-done.3, f32[3072,256]{1,0:T(8,128)} %copy-done.6), kind=kLoop, calls=%fused_computation.13 | loop fusion | flops 4718592 | bytes 12582912 | tf_op jit(solution)/shard_map/convert_element_type | solution.py:205
  273.1 1.9 collective-permute-start.4
  275.0 2.0 collective-permute-start.5
  277.0 5.0 %fusion.10 = bf16[896,1024]{1,0:T(8,128)(2,1)} fusion(bf16[896,1024]{1,0:T(8,128)(2,1)} %bitcast.29, s32[896]{0:T(1024)S(1)} %fusion.53), kind=kOutput, calls=%fused_computation.21 | convolution fusion | flops 1645887488 | bytes 3673600 | tf_op jit(solution)/shard_map/dot_general | solution.py:44
  281.9 6.7 %all-to-all-start.5 = ((bf16[16,56,1024]{2,1,0:T(8,128)(2,1)}), bf16[16,56,1024]{2,1,0:T(8,128)(2,1)S(1)}, u32[]{:S(2)}, u32[]{:S(2)}) async-start(bf16[16,56,1024]{2,1,0:T(8,128)(2,1)} %bitcast.79), calls=%async_computation.5 | async-start | bytes 3670016 | tf_op jit(solution)/shard_map/all_to_all | solution.py:171
  288.6 23.2 %collective-permute-done.4 = bf16[3072,256]{1,0:T(8,128)(2,1)S(1)} collective-permute-done((bf16[3072,256]{1,0:T(8,128)(2,1)}, bf16[3072,256]{1,0:T(8,128)(2,1)S(1)}, u32[]{:S(2)}, u32[]{:S(2)}) %collective-permute-start.4) | collective-permute-done | bytes 1572896 | tf_op jit(solution)/shard_map/ppermute | solution.py:205
  311.8 34.1 %collective-permute-done.5 = bf16[3072,256]{1,0:T(8,128)(2,1)} collective-permute-done((bf16[3072,256]{1,0:T(8,128)(2,1)}, bf16[3072,256]{1,0:T(8,128)(2,1)}, u32[]{:S(2)}, u32[]{:S(2)}) %collective-permute-start.5) | collective-permute-done | bytes 1572896 | tf_op jit(solution)/shard_map/ppermute | solution.py:205
  (71 shorter events, 25.0 us)
Async XLA Ops:
  5.0 7.1 %copy-start.8 = (bf16[2,256,1024]{2,1,0:T(8,128)(2,1)S(1)}, bf16[2,256,1024]{2,1,0:T(8,128)(2,1)}, u32[]{:S(2)}) copy-start(bf16[2,256,1024]{2,1,0:T(8,128)(2,1)} %param.15) | copy-start | bytes 3145732
  5.0 30.5 %all-to-all-start = ((bf16[16,56,1024]{2,1,0:T(8,128)(2,1)}), bf16[16,56,1024]{2,1,0:T(8,128)(2,1)}, u32[]{:S(2)}, u32[]{:S(2)}) async-start(bf16[16,56,1024]{2,1,0:T(8,128)(2,1)} %bitcast.5), calls=%async_computation | async-start | bytes 3670016 | tf_op jit(solution)/shard_map/all_to_all | solution.py:171
  12.1 1.7 copy-start.9
  12.2 1.7 copy-start.7
  16.8 9.0 %copy-start.11 = (bf16[128,4,2]{0,2,1:T(2,128)(2,1)S(1)}, bf16[128,4,2]{0,2,1:T(2,128)(2,1)}, u32[]{:S(2)}) copy-start(bf16[128,4,2]{0,2,1:T(2,128)(2,1)} %param.10) | copy-start | bytes 6148
  16.8 9.1 %copy-start.10 = (bf16[128,4096]{1,0:T(8,128)(2,1)S(1)}, bf16[128,4096]{1,0:T(8,128)(2,1)}, u32[]{:S(2)}) copy-start(bf16[128,4096]{1,0:T(8,128)(2,1)} %param.9) | copy-start | bytes 3145732
  19.7 57.1 %collective-permute-start = (bf16[3072,256]{1,0:T(8,128)(2,1)}, bf16[3072,256]{1,0:T(8,128)(2,1)S(1)}, u32[]{:S(2)}, u32[]{:S(2)}) collective-permute-start(bf16[3072,256]{1,0:T(8,128)(2,1)} %get-tuple-element.50), channel_id=1, source_target_pairs={{0,0},{1,128},{64,64},{65,192},{128,1},{129,129},{192,65},{193,193... | collective-permute-start | bytes 4718600 | tf_op jit(solution)/shard_map/ppermute | solution.py:142
  25.7 68.0 %collective-permute-start.1 = (bf16[3072,256]{1,0:T(8,128)(2,1)}, bf16[3072,256]{1,0:T(8,128)(2,1)}, u32[]{:S(2)}, u32[]{:S(2)}) collective-permute-start(bf16[3072,256]{1,0:T(8,128)(2,1)} %get-tuple-element.51), channel_id=1, source_target_pairs={{0,64},{1,192},{64,0},{65,128},{128,65},{129,193},{192,1},{193,129... | collective-permute-start | bytes 4718600 | tf_op jit(solution)/shard_map/ppermute | solution.py:142
  35.5 66.4 %all-to-all-start.1 = ((bf16[16,56,1024]{2,1,0:T(8,128)(2,1)}), bf16[16,56,1024]{2,1,0:T(8,128)(2,1)S(1)}, u32[]{:S(2)}, u32[]{:S(2)}) async-start(bf16[16,56,1024]{2,1,0:T(8,128)(2,1)} %bitcast.10), calls=%async_computation.1 | async-start | bytes 3670016 | tf_op jit(solution)/shard_map/all_to_all | solution.py:171
  105.4 50.0 %all-to-all-start.3 = ((bf16[8,112,1024]{2,1,0:T(8,128)(2,1)}), bf16[8,112,1024]{2,1,0:T(8,128)(2,1)S(1)}, u32[]{:S(2)}, u32[]{:S(2)}) async-start(bf16[8,112,1024]{2,1,0:T(8,128)(2,1)} %bitcast.82), calls=%async_computation.3 | async-start | bytes 3670016 | tf_op jit(solution)/shard_map/all_to_all | solution.py:175
  112.0 50.2 %collective-permute-start.2 = (bf16[2,3072,256]{2,1,0:T(8,128)(2,1)}, bf16[2,3072,256]{2,1,0:T(8,128)(2,1)}, u32[]{:S(2)}, u32[]{:S(2)}) collective-permute-start(bf16[2,3072,256]{2,1,0:T(8,128)(2,1)} %pad_maximum_fusion.own_ref), channel_id=1, source_target_pairs={{0,1},{1,0},{2,3},{3,2},{4,5},{5,4},{6,7},{7,6},{8,9},{9,8},{10,11... | collective-permute-start | bytes 9437192 | tf_op jit(solution)/shard_map/ppermute | solution.py:187
  155.4 51.0 %all-to-all-start.2 = ((bf16[8,112,1024]{2,1,0:T(8,128)(2,1)}), bf16[8,112,1024]{2,1,0:T(8,128)(2,1)}, u32[]{:S(2)}, u32[]{:S(2)}) async-start(bf16[8,112,1024]{2,1,0:T(8,128)(2,1)} %bitcast.80), calls=%async_computation.2 | async-start | bytes 3670016 | tf_op jit(solution)/shard_map/all_to_all | solution.py:175
  173.9 1.3 copy-start.2
  175.2 1.4 copy-start.5
  218.1 1.2 copy-start
  219.3 1.2 copy-start.3
  220.5 47.4 %all-to-all-start.4 = ((bf16[8,112,1024]{2,1,0:T(8,128)(2,1)}), bf16[8,112,1024]{2,1,0:T(8,128)(2,1)}, u32[]{:S(2)}, u32[]{:S(2)}) async-start(bf16[8,112,1024]{2,1,0:T(8,128)(2,1)} %bitcast.28), calls=%async_computation.4 | async-start | bytes 3670016 | tf_op jit(solution)/shard_map/all_to_all | solution.py:175
  224.8 4.6 %copy-start.4 = (bf16[896,1024]{1,0:T(8,128)(2,1)S(1)}, bf16[896,1024]{1,0:T(8,128)(2,1)}, u32[]{:S(2)}) copy-start(bf16[896,1024]{1,0:T(8,128)(2,1)} %copy-done.3) | copy-start | bytes 5505028
  231.8 1.5 copy-start.1
  236.3 7.1 %collective-permute-start.3 = (bf16[2,3072,256]{2,1,0:T(8,128)(2,1)S(1)}, bf16[2,3072,256]{2,1,0:T(8,128)(2,1)}, u32[]{:S(2)}, u32[]{:S(2)}) collective-permute-start(bf16[2,3072,256]{2,1,0:T(8,128)(2,1)S(1)} %pad_maximum_fusion.1), channel_id=1, source_target_pairs={{0,1},{1,0},{2,3},{3,2},{4,5},{5,4},{6,7},{7,6},{8,9},{9,8},{10,11... | collective-permute-start | bytes 9437192 | tf_op jit(solution)/shard_map/ppermute | solution.py:202
  238.5 1.7 copy-start.6
  273.1 38.7 %collective-permute-start.4 = (bf16[3072,256]{1,0:T(8,128)(2,1)}, bf16[3072,256]{1,0:T(8,128)(2,1)S(1)}, u32[]{:S(2)}, u32[]{:S(2)}) collective-permute-start(bf16[3072,256]{1,0:T(8,128)(2,1)} %get-tuple-element.48), channel_id=1, source_target_pairs={{0,0},{128,1},{64,64},{192,65},{1,128},{129,129},{65,192},{193,193... | collective-permute-start | bytes 4718600 | tf_op jit(solution)/shard_map/ppermute | solution.py:205
  275.0 70.9 %collective-permute-start.5 = (bf16[3072,256]{1,0:T(8,128)(2,1)}, bf16[3072,256]{1,0:T(8,128)(2,1)}, u32[]{:S(2)}, u32[]{:S(2)}) collective-permute-start(bf16[3072,256]{1,0:T(8,128)(2,1)} %get-tuple-element.49), channel_id=1, source_target_pairs={{64,0},{192,1},{0,64},{128,65},{65,128},{193,129},{1,192},{129,193... | collective-permute-start | bytes 4718600 | tf_op jit(solution)/shard_map/ppermute | solution.py:205
  281.9 69.1 %all-to-all-start.5 = ((bf16[16,56,1024]{2,1,0:T(8,128)(2,1)}), bf16[16,56,1024]{2,1,0:T(8,128)(2,1)S(1)}, u32[]{:S(2)}, u32[]{:S(2)}) async-start(bf16[16,56,1024]{2,1,0:T(8,128)(2,1)} %bitcast.79), calls=%async_computation.5 | async-start | bytes 3670016 | tf_op jit(solution)/shard_map/all_to_all | solution.py:171

commit v2 on v1

--- a/solution.py
+++ b/solution.py
@@ -44,36 +44,34 @@
     return lax.dot_general(a, b, ((over[:1], over[1:]), ((), ())), preferred_element_type=F32)
 
 
-def forward_kernel(x_ref, own_ref, other_ref, act_ref, fac_ref, hid_ref, gt_ref, ut_ref, dt_ref):
+def forward_kernel(
+    x_ref, w0, w1, w2, w3, act_ref, fac_ref, hid_ref, gt_ref, ut_ref, dt_ref, w_ref
+):
     j = pl.program_id(0)
-
-    def part(w_ref):
-        def step(i, _):
-            at = pl.ds(pl.multiple_of(i * STEP, STEP), STEP)
-            x = x_ref[at, :]
-            g = dot(x, w_ref[0, :SUB, :], (1, 0))
-            u = dot(x, w_ref[0, SUB : 2 * SUB, :], (1, 0))
-            sig = jax.nn.sigmoid(g)
-            act = g * sig
-            act_ref[at, :] = act
-            fac_ref[at, :] = u * sig * (1.0 + g * (1.0 - sig))
-            hid_ref[at, :] = (act * u).astype(BF16)
-            return 0
-
-        lax.fori_loop(0, ROWS // STEP, step, 0)
-        gt_ref[...] = w_ref[0, :SUB, :].T
-        ut_ref[...] = w_ref[0, SUB : 2 * SUB, :].T
-        for f in range(SUB // PART):
-            low = 2 * SUB + f * PART
-            dt_ref[f * PART : (f + 1) * PART, :] = w_ref[0, low : low + PART, :].T
-
-    @pl.when(j < 2)
-    def _():
-        part(own_ref)
-
-    @pl.when(j >= 2)
-    def _():
-        part(other_ref)
+    for i, ref in enumerate((w0, w1, w2, w3)):
+
+        @pl.when(j == i)
+        def _():
+            w_ref[...] = ref[...]
+
+    def step(i, _):
+        at = pl.ds(pl.multiple_of(i * STEP, STEP), STEP)
+        x = x_ref[at, :]
+        g = dot(x, w_ref[:SUB, :], (1, 0))
+        u = dot(x, w_ref[SUB : 2 * SUB, :], (1, 0))
+        sig = jax.nn.sigmoid(g)
+        act = g * sig
+        act_ref[at, :] = act
+        fac_ref[at, :] = u * sig * (1.0 + g * (1.0 - sig))
+        hid_ref[at, :] = (act * u).astype(BF16)
+        return 0
+
+    lax.fori_loop(0, ROWS // STEP, step, 0)
+    gt_ref[...] = w_ref[:SUB, :].T
+    ut_ref[...] = w_ref[SUB : 2 * SUB, :].T
+    for f in range(SUB // PART):
+        low = 2 * SUB + f * PART
+        dt_ref[f * PART : (f + 1) * PART, :] = w_ref[low : low + PART, :].T
 
 
 def backward_kernel(dy_ref, act_ref, fac_ref, gt_ref, ut_ref, dt_ref, dg_ref, du_ref, dx_ref):
@@ -90,7 +88,7 @@
     )
 
 
-def forward(x, own, other):
+def forward(x, pieces):
     columns = pl.BlockSpec((ROWS, PART), lambda j: (0, j))
     float_out = jax.ShapeDtypeStruct((ROWS, SUB), F32)
     square = jax.ShapeDtypeStruct((SUB, SUB), BF16)
@@ -99,18 +97,18 @@
         grid=(4,),
         in_specs=[
             pl.BlockSpec((ROWS, SUB), lambda j: (0, 0)),
-            pl.BlockSpec((1, 3 * SUB, PART), lambda j: (jnp.minimum(j, 1), 0, 0)),
-            pl.BlockSpec((1, 3 * SUB, PART), lambda j: (jnp.maximum(j - 2, 0), 0, 0)),
-        ],
+        ]
+        + [pl.BlockSpec((3 * SUB, PART), lambda j: (0, 0))] * 4,
         out_specs=[columns] * 3
         + [pl.BlockSpec((PART, SUB), lambda j: (j, 0))] * 2
         + [pl.BlockSpec((SUB, PART), lambda j: (0, j))],
         out_shape=[float_out, float_out, jax.ShapeDtypeStruct((ROWS, SUB), BF16)] + [square] * 3,
+        scratch_shapes=[pltpu.VMEM((3 * SUB, PART), BF16)],
         compiler_params=params(),
         cost_estimate=pl.CostEstimate(
             flops=4 * ROWS * SUB * SUB, bytes_accessed=24 * 2**20, transcendentals=ROWS * SUB
         ),
-    )(x, own, other)
+    )(x, *pieces)
 
 
 def backward(dy, act, fac, gate_t, up_t, down_t):
@@ -134,19 +132,16 @@
     rows = toks * HEADS
     h = lax.axis_index("rep")
 
-    packed = jnp.stack(
-        [jnp.concatenate([w_gate[p], w_up[p], tall(w_down[p])], 0) for p in range(2)], 0
-    )
-    own = jnp.stack(
-        [
-            lax.ppermute(
-                lax.dynamic_index_in_dim(packed, (h + q) % 2, 0, keepdims=False), PAIR, to_host(q)
-            )
-            for q in range(2)
-        ],
-        0,
-    )
-    other = lax.ppermute(own, "core", SWAP)
+    own = []
+    for q in range(2):
+        one = [
+            lax.dynamic_index_in_dim(w, (h + q) % 2, 0, keepdims=False)
+            for w in (w_gate, w_up, w_down)
+        ]
+        piece = jnp.concatenate([one[0], one[1], tall(one[2])], 0)
+        if own:
+            piece, own[0] = lax.optimization_barrier((piece, own[0]))
+        own.append(lax.ppermute(piece, PAIR, to_host(q)))
 
     def heads_first(a):
         return jnp.transpose(a, (1, 0, 2)).reshape(rows, 2)
@@ -182,12 +177,12 @@
     x_slot = dot(pick, cut(tokens), (1, 0)).astype(BF16)
     dy_slot = dot(pick_gate, cut(cotangent), (1, 0)).astype(BF16)
     x_rows = dot(regroup, in_plane(x_slot), (1, 0)).astype(BF16)
-    dy_rows = dot(regroup, in_plane(dy_slot), (1, 0)).astype(BF16)
+    dy_rows = in_plane(dy_slot)
     x_rows, dy_rows, own = lax.optimization_barrier((x_rows, dy_rows, own))
-    other = lax.ppermute(own, "core", SWAP)
+    other = [lax.ppermute(w, "core", SWAP) for w in own]
     x = along_z(x_rows)
-    act, fac, hidden, gate_t, up_t, down_t = forward(x, own, other)
-    dy = along_z(dy_rows)
+    act, fac, hidden, gate_t, up_t, down_t = forward(x, own + other)
+    dy = along_z(dot(regroup, dy_rows, (1, 0)).astype(BF16))
     d_gate, d_up, dx = backward(dy, act, fac, gate_t, up_t, down_t)
     dx = along_z(dx)
 
@@ -200,11 +195,11 @@
         )
 
     theirs = lax.ppermute(jnp.stack([pack(2), pack(3)], 0).astype(BF16), "core", SWAP)
-    dx, theirs = lax.optimization_barrier((dx, theirs))
-    back = [
-        lax.ppermute((pack(q) + theirs[q].astype(F32)).astype(BF16), PAIR, from_host(q))
-        for q in range(2)
-    ]
+    sums = [(pack(q) + theirs[q].astype(F32)).astype(BF16) for q in range(2)]
+    dx, sums = lax.optimization_barrier((dx, sums))
+    first = lax.ppermute(sums[0], PAIR, from_host(0))
+    first, second = lax.optimization_barrier((first, sums[1]))
+    back = [first, lax.ppermute(second, PAIR, from_host(1))]
     returned = in_plane(dot(regroup, dx, (0, 0)).astype(BF16))
     even = h % 2 == 0
     both = [jnp.where(even, back[0], back[1]), jnp.where(even, back[1], back[0])]

time: 354 us -> 358 us (1.011)
  matrix products: 28.6 us -> 38.9 us
  other arithmetic: 18.5 us -> 11.5 us
    dot_general x9, matrix products: 28.6 us -> 38.9 us  [dot(): lax.dot_general(a, b, ((over[:1], over[1:]), ((), ())), preferred_element...]
    all_to_all x3, waiting for transfers between devices: 96.3 us -> 101 us  [along_z(): return lax.all_to_all(a, ('zh', 'rep'), 0, 0, tiled=True).reshape(ROWS, SUB)]
    all_to_all x3, waiting for transfers between devices: 7.24 us -> 11.6 us  [in_plane(): return lax.all_to_all(a, ('y', 'x'), 0, 0, tiled=True).reshape(ROWS, SUB)]
    ppermute x5 -> x6, waiting for transfers between devices: 108 us -> 103 us  [the longest x2 42.3 us: on_device(): own.append(lax.ppermute(piece, PAIR, to_host(q)))]
    ppermute x5 -> x6, starting transfers between devices: 11.4 us -> 10.4 us  [the longest x2 6.01 us: on_device(): own.append(lax.ppermute(piece, PAIR, to_host(q)))]
    unnamed x41 -> x36, local copies, waits for them, and re-layouts: 12.5 us -> 12.6 us
  transfers between devices with their start and end apart: 12 -> 13, of which waited for: 9 -> 11; matrix products, arithmetic and copies ran while one was open for 11% -> 9% of each run, Pallas kernels for 3% -> 3%
where the time goes in v2:
time: 358 us; the launch traced here: 357 us
  waiting for transfers between devices  216 us (60%)
  starting transfers between devices  50.5 us (14%)
  matrix products  38.9 us (11%)
  Pallas kernels  23.1 us (6%)
  local copies, waits for them, and re-layouts  15.7 us (4%)
  other arithmetic  11.5 us (3%)
    all_to_all x3, waiting for transfers between devices, along_z(): return lax.all_to_all(a, ('zh', 'rep'), 0, 0, tiled=True).reshape(ROWS, SUB)  101 us
    ppermute x2, waiting for transfers between devices, on_device(): own.append(lax.ppermute(piece, PAIR, to_host(q)))  42.3 us
    dot_general x9, matrix products, dot(): lax.dot_general(a, b, ((over[:1], over[1:]), ((), ())), preferred_element...  38.9 us
    ppermute x1, waiting for transfers between devices, on_device(): back = [first, lax.ppermute(second, PAIR, from_host(1))]  32.7 us
    ppermute x1, waiting for transfers between devices, on_device(): first = lax.ppermute(sums[0], PAIR, from_host(0))  22.9 us
    all_to_all x3, starting transfers between devices, in_plane(): return lax.all_to_all(a, ('y', 'x'), 0, 0, tiled=True).reshape(ROWS, SUB)  21.5 us
    all_to_all x3, starting transfers between devices, along_z(): return lax.all_to_all(a, ('zh', 'rep'), 0, 0, tiled=True).reshape(ROWS, SUB)  17.2 us
    unnamed x36, local copies, waits for them, and re-layouts  12.6 us
  transfers between devices with their start and end apart: 13, of which 11 were waited for; matrix products, arithmetic and copies ran while one was open for 9% of the time, Pallas kernels for 3%

profile of v2, /device:TPU:35, one launch (start us, length us, event | category | flops | bytes accessed | tf_op | source)
XLA Modules:
  0.0 356.6 jit_solution(3139567768720959327)
XLA Ops:
  2.6 2.4 convolution_convert_fusion
  5.0 7.0 %all-to-all-start = ((bf16[16,56,1024]{2,1,0:T(8,128)(2,1)}), bf16[16,56,1024]{2,1,0:T(8,128)(2,1)}, u32[]{:S(2)}, u32[]{:S(2)}) async-start(bf16[16,56,1024]{2,1,0:T(8,128)(2,1)} %bitcast.5), calls=%async_computation | async-start | bytes 3670016 | tf_op jit(solution)/shard_map/all_to_all | solution.py:166
  17.7 6.0 %collective-permute-start = (bf16[3072,256]{1,0:T(8,128)(2,1)}, bf16[3072,256]{1,0:T(8,128)(2,1)S(1)}, u32[]{:S(2)}, u32[]{:S(2)}) collective-permute-start(bf16[3072,256]{1,0:T(8,128)(2,1)} %slice_dynamic-update-slice_fusion.24), channel_id=1, source_target_pairs={{0,0},{1,128},{64,64},{65,192},{128,1},{129,129},{192,65},{193,193... | collective-permute-start | bytes 4718600 | tf_op jit(solution)/shard_map/ppermute | solution.py:144
  25.1 2.4 convolution_convert_fusion.1
  27.4 8.1 %all-to-all-done = bf16[16,56,1024]{2,1,0:T(8,128)(2,1)} async-done(((bf16[16,56,1024]{2,1,0:T(8,128)(2,1)}), bf16[16,56,1024]{2,1,0:T(8,128)(2,1)}, u32[]{:S(2)}, u32[]{:S(2)}) %all-to-all-start) | async-done | bytes 1835040 | tf_op jit(solution)/shard_map/all_to_all | solution.py:166
  35.5 7.8 %all-to-all-start.1 = ((bf16[16,56,1024]{2,1,0:T(8,128)(2,1)}), bf16[16,56,1024]{2,1,0:T(8,128)(2,1)}, u32[]{:S(2)}, u32[]{:S(2)}) async-start(bf16[16,56,1024]{2,1,0:T(8,128)(2,1)} %bitcast.70), calls=%async_computation.1 | async-start | bytes 3670016 | tf_op jit(solution)/shard_map/all_to_all | solution.py:166
  44.0 13.8 %collective-permute-done.w0 = bf16[3072,256]{1,0:T(8,128)(2,1)S(1)} collective-permute-done((bf16[3072,256]{1,0:T(8,128)(2,1)}, bf16[3072,256]{1,0:T(8,128)(2,1)S(1)}, u32[]{:S(2)}, u32[]{:S(2)}) %collective-permute-start) | collective-permute-done | bytes 1572896 | tf_op jit(solution)/shard_map/ppermute | solution.py:144
  57.8 4.8 %fusion.8 = bf16[896,1024]{1,0:T(8,128)(2,1)} fusion(bf16[896,1024]{1,0:T(8,128)(2,1)} %bitcast.6, s32[896]{0:T(1024)S(1)} %fusion.49), kind=kOutput, calls=%fused_computation.14 | convolution fusion | flops 1645887488 | bytes 3673600 | tf_op jit(solution)/shard_map/dot_general | solution.py:44
  62.7 3.5 all-to-all-done.1
  66.2 28.5 %collective-permute-done.1.w1 = bf16[3072,256]{1,0:T(8,128)(2,1)S(1)} collective-permute-done((bf16[3072,256]{1,0:T(8,128)(2,1)}, bf16[3072,256]{1,0:T(8,128)(2,1)S(1)}, u32[]{:S(2)}, u32[]{:S(2)}) %collective-permute-start.1) | collective-permute-done | bytes 1572896 | tf_op jit(solution)/shard_map/ppermute | solution.py:144
  94.7 6.2 %all-to-all-start.3 = ((bf16[8,112,1024]{2,1,0:T(8,128)(2,1)}), bf16[8,112,1024]{2,1,0:T(8,128)(2,1)}, u32[]{:S(2)}, u32[]{:S(2)}) async-start(bf16[8,112,1024]{2,1,0:T(8,128)(2,1)} %bitcast.73), calls=%async_computation.3 | async-start | bytes 3670016 | tf_op jit(solution)/shard_map/all_to_all | solution.py:170
  100.9 4.8 %fusion.9 = bf16[896,1024]{1,0:T(8,128)(2,1)} fusion(bf16[896,1024]{1,0:T(8,128)(2,1)} %bitcast.11, s32[896]{0:T(1024)S(1)} %fusion.49), kind=kOutput, calls=%fused_computation.15 | convolution fusion | flops 1645887488 | bytes 3673600 | tf_op jit(solution)/shard_map/dot_general | solution.py:44
  105.8 40.1 %all-to-all-done.3 = bf16[8,112,1024]{2,1,0:T(8,128)(2,1)} async-done(((bf16[8,112,1024]{2,1,0:T(8,128)(2,1)}), bf16[8,112,1024]{2,1,0:T(8,128)(2,1)}, u32[]{:S(2)}, u32[]{:S(2)}) %all-to-all-start.3) | async-done | bytes 1835040 | tf_op jit(solution)/shard_map/all_to_all | solution.py:170
  145.9 5.6 %all-to-all-start.2 = ((bf16[8,112,1024]{2,1,0:T(8,128)(2,1)}), bf16[8,112,1024]{2,1,0:T(8,128)(2,1)}, u32[]{:S(2)}, u32[]{:S(2)}) async-start(bf16[8,112,1024]{2,1,0:T(8,128)(2,1)} %bitcast.69), calls=%async_computation.2 | async-start | bytes 3670016 | tf_op jit(solution)/shard_map/all_to_all | solution.py:170
  152.2 3.0 collective-permute-done.2.w2
  155.3 2.2 collective-permute-done.3.w3
  158.7 11.4 %shard_map.111 = (f32[896,1024]{1,0:T(8,128)}, f32[896,1024]{1,0:T(8,128)}, bf16[896,1024]{1,0:T(8,128)(2,1)}, bf16[1024,1024]{1,0:T(8,128)(2,1)}, bf16[1024,102...) custom-call(bf16[896,1024]{1,0:T(8,128)(2,1)} %bitcast.21.x_ref, bf16[3072,256]{1,0:T(8,128)(2,1)S(1)} %collective-permute-done.w0, ...), custom_call_target="tpu_custom_call" | custom-call | flops 3758096384 | bytes 25165824 | tf_op jit(solution)/shard_map/pallas_call | solution.py:95
  170.1 25.5 %all-to-all-done.2 = bf16[8,112,1024]{2,1,0:T(8,128)(2,1)} async-done(((bf16[8,112,1024]{2,1,0:T(8,128)(2,1)}), bf16[8,112,1024]{2,1,0:T(8,128)(2,1)}, u32[]{:S(2)}, u32[]{:S(2)}) %all-to-all-start.2) | async-done | bytes 1835040 | tf_op jit(solution)/shard_map/all_to_all | solution.py:170
  195.6 6.4 %fusion.72 = (bf16[1024,1024]{1,0:T(8,128)(2,1)S(1)}, f32[1024,1024]{1,0:T(8,128)}) fusion(bf16[896,1024]{1,0:T(8,128)(2,1)} %get-tuple-element.38, bf16[896,1024]{1,0:T(8,128)(2,1)} %bitcast.19.dy_ref), kind=kOutput, calls=%fused_computation.138 | convolution fusion | flops 1880096768 | bytes 9961472 | tf_op jit(solution)/shard_map/dot_general | solution.py:44
  202.0 11.7 %shard_map.112 = (bf16[896,1024]{1,0:T(8,128)(2,1)S(1)}, bf16[896,1024]{1,0:T(8,128)(2,1)S(1)}, bf16[896,1024]{1,0:T(8,128)(2,1)}) custom-call(bf16[896,1024]{1,0:T(8,128)(2,1)} %bitcast.19.dy_ref, f32[896,1024]{1,0:T(8,128)} %get-tuple-element.30.act_ref, f32[896,1024]{1,0:T(8,128)} %get-tuple-element.31.fac_ref, ...), custom_call_target="tpu_custom_call" | custom-call | flops 5637144576 | bytes 20971520 | tf_op jit(solution)/shard_map/pallas_call | solution.py:117
  213.7 5.9 %fusion.70 = (bf16[1024,1024]{1,0:T(8,128)(2,1)S(1)}, f32[1024,1024]{1,0:T(8,128)}) fusion(bf16[896,1024]{1,0:T(8,128)(2,1)} %bitcast.21.x_ref, bf16[896,1024]{1,0:T(8,128)(2,1)S(1)} %get-tuple-element.36), kind=kOutput, calls=%fused_computation.136 | convolution fusion | flops 1880096768 | bytes 9961472 | tf_op jit(solution)/shard_map/dot_general | solution.py:44
  219.7 5.9 %fusion.71 = (bf16[1024,1024]{1,0:T(8,128)(2,1)S(1)}, f32[1024,1024]{1,0:T(8,128)}) fusion(bf16[896,1024]{1,0:T(8,128)(2,1)} %bitcast.21.x_ref, bf16[896,1024]{1,0:T(8,128)(2,1)S(1)} %get-tuple-element.37), kind=kOutput, calls=%fused_computation.137 | convolution fusion | flops 1880096768 | bytes 9961472 | tf_op jit(solution)/shard_map/dot_general | solution.py:44
  227.6 5.4 %all-to-all-start.4 = ((bf16[8,112,1024]{2,1,0:T(8,128)(2,1)}), bf16[8,112,1024]{2,1,0:T(8,128)(2,1)}, u32[]{:S(2)}, u32[]{:S(2)}) async-start(bf16[8,112,1024]{2,1,0:T(8,128)(2,1)} %bitcast.22), calls=%async_computation.4 | async-start | bytes 3670016 | tf_op jit(solution)/shard_map/all_to_all | solution.py:170
  236.0 2.0 copy-done
  238.2 4.0 %fusion.3 = (bf16[3072,256]{1,0:T(8,128)(2,1)S(1)}, bf16[3072,256]{1,0:T(8,128)(2,1)}) fusion(f32[3072,256]{1,0:T(8,128)S(1)} %get-tuple-element.46, bf16[2,3072,256]{2,1,0:T(8,128)(2,1)} %collective-permute-done.4, f32[3072,256]{1,0:T(8,128)S(1)} %get-tuple-element.47), kind=kLoop, calls=%fused_computation.6 | loop fusion | flops 4718592 | bytes 12582912 | tf_op jit(solution)/shard_map/convert_element_type | solution.py:198
  242.2 35.5 %all-to-all-done.4 = bf16[8,112,1024]{2,1,0:T(8,128)(2,1)} async-done(((bf16[8,112,1024]{2,1,0:T(8,128)(2,1)}), bf16[8,112,1024]{2,1,0:T(8,128)(2,1)}, u32[]{:S(2)}, u32[]{:S(2)}) %all-to-all-start.4) | async-done | bytes 1835040 | tf_op jit(solution)/shard_map/all_to_all | solution.py:170
  277.7 1.9 collective-permute-start.5
  279.6 5.0 %fusion.10 = bf16[896,1024]{1,0:T(8,128)(2,1)} fusion(bf16[896,1024]{1,0:T(8,128)(2,1)} %bitcast.23, s32[896]{0:T(1024)S(1)} %fusion.49), kind=kOutput, calls=%fused_computation.16 | convolution fusion | flops 1645887488 | bytes 3673600 | tf_op jit(solution)/shard_map/dot_general | solution.py:44
  284.5 6.7 %all-to-all-start.5 = ((bf16[16,56,1024]{2,1,0:T(8,128)(2,1)}), bf16[16,56,1024]{2,1,0:T(8,128)(2,1)S(1)}, u32[]{:S(2)}, u32[]{:S(2)}) async-start(bf16[16,56,1024]{2,1,0:T(8,128)(2,1)} %bitcast.72), calls=%async_computation.5 | async-start | bytes 3670016 | tf_op jit(solution)/shard_map/all_to_all | solution.py:166
  291.2 22.9 %collective-permute-done.5 = bf16[3072,256]{1,0:T(8,128)(2,1)} collective-permute-done((bf16[3072,256]{1,0:T(8,128)(2,1)}, bf16[3072,256]{1,0:T(8,128)(2,1)}, u32[]{:S(2)}, u32[]{:S(2)}) %collective-permute-start.5) | collective-permute-done | bytes 1572896 | tf_op jit(solution)/shard_map/ppermute | solution.py:200
  318.2 32.7 %collective-permute-done.6 = bf16[3072,256]{1,0:T(8,128)(2,1)} collective-permute-done((bf16[3072,256]{1,0:T(8,128)(2,1)S(1)}, bf16[3072,256]{1,0:T(8,128)(2,1)}, u32[]{:S(2)}, u32[]{:S(2)}) %collective-permute-start.6) | collective-permute-done | bytes 1572896 | tf_op jit(solution)/shard_map/ppermute | solution.py:202
  350.9 2.1 broadcast_select_fusion.1
  (64 shorter events, 24.3 us)
Async XLA Ops:
  5.0 7.1 %copy-start.3 = (bf16[2,256,1024]{2,1,0:T(8,128)(2,1)S(1)}, bf16[2,256,1024]{2,1,0:T(8,128)(2,1)}, u32[]{:S(2)}) copy-start(bf16[2,256,1024]{2,1,0:T(8,128)(2,1)} %param.15) | copy-start | bytes 3145732
  5.0 30.5 %all-to-all-start = ((bf16[16,56,1024]{2,1,0:T(8,128)(2,1)}), bf16[16,56,1024]{2,1,0:T(8,128)(2,1)}, u32[]{:S(2)}, u32[]{:S(2)}) async-start(bf16[16,56,1024]{2,1,0:T(8,128)(2,1)} %bitcast.5), calls=%async_computation | async-start | bytes 3670016 | tf_op jit(solution)/shard_map/all_to_all | solution.py:166
  12.1 1.2 copy-start.4
  12.1 2.0 copy-start.5
  14.1 9.6 %copy-start.7 = (bf16[128,4,2]{0,2,1:T(2,128)(2,1)S(1)}, bf16[128,4,2]{0,2,1:T(2,128)(2,1)}, u32[]{:S(2)}) copy-start(bf16[128,4,2]{0,2,1:T(2,128)(2,1)} %param.10) | copy-start | bytes 6148
  14.1 9.7 %copy-start.2 = (bf16[128,4096]{1,0:T(8,128)(2,1)S(1)}, bf16[128,4096]{1,0:T(8,128)(2,1)}, u32[]{:S(2)}) copy-start(bf16[128,4096]{1,0:T(8,128)(2,1)} %param.9) | copy-start | bytes 3145732
  17.7 40.1 %collective-permute-start = (bf16[3072,256]{1,0:T(8,128)(2,1)}, bf16[3072,256]{1,0:T(8,128)(2,1)S(1)}, u32[]{:S(2)}, u32[]{:S(2)}) collective-permute-start(bf16[3072,256]{1,0:T(8,128)(2,1)} %slice_dynamic-update-slice_fusion.24), channel_id=1, source_target_pairs={{0,0},{1,128},{64,64},{65,192},{128,1},{129,129},{192,65},{193,193... | collective-permute-start | bytes 4718600 | tf_op jit(solution)/shard_map/ppermute | solution.py:144
  23.8 1.2 copy-start.6
  35.5 30.6 %all-to-all-start.1 = ((bf16[16,56,1024]{2,1,0:T(8,128)(2,1)}), bf16[16,56,1024]{2,1,0:T(8,128)(2,1)}, u32[]{:S(2)}, u32[]{:S(2)}) async-start(bf16[16,56,1024]{2,1,0:T(8,128)(2,1)} %bitcast.70), calls=%async_computation.1 | async-start | bytes 3670016 | tf_op jit(solution)/shard_map/all_to_all | solution.py:166
  57.8 36.9 %collective-permute-start.1 = (bf16[3072,256]{1,0:T(8,128)(2,1)}, bf16[3072,256]{1,0:T(8,128)(2,1)S(1)}, u32[]{:S(2)}, u32[]{:S(2)}) collective-permute-start(bf16[3072,256]{1,0:T(8,128)(2,1)} %slice_dynamic-update-slice_fusion.28), channel_id=1, source_target_pairs={{0,64},{1,192},{64,0},{65,128},{128,65},{129,193},{192,1},{193,129... | collective-permute-start | bytes 4718600 | tf_op jit(solution)/shard_map/ppermute | solution.py:144
  94.7 51.2 %all-to-all-start.3 = ((bf16[8,112,1024]{2,1,0:T(8,128)(2,1)}), bf16[8,112,1024]{2,1,0:T(8,128)(2,1)}, u32[]{:S(2)}, u32[]{:S(2)}) async-start(bf16[8,112,1024]{2,1,0:T(8,128)(2,1)} %bitcast.73), calls=%async_computation.3 | async-start | bytes 3670016 | tf_op jit(solution)/shard_map/all_to_all | solution.py:170
  145.9 49.7 %all-to-all-start.2 = ((bf16[8,112,1024]{2,1,0:T(8,128)(2,1)}), bf16[8,112,1024]{2,1,0:T(8,128)(2,1)}, u32[]{:S(2)}, u32[]{:S(2)}) async-start(bf16[8,112,1024]{2,1,0:T(8,128)(2,1)} %bitcast.69), calls=%async_computation.2 | async-start | bytes 3670016 | tf_op jit(solution)/shard_map/all_to_all | solution.py:170
  151.4 3.8 %collective-permute-start.2 = (bf16[3072,256]{1,0:T(8,128)(2,1)S(1)}, bf16[3072,256]{1,0:T(8,128)(2,1)S(1)}, u32[]{:S(2)}, u32[]{:S(2)}) collective-permute-start(bf16[3072,256]{1,0:T(8,128)(2,1)S(1)} %collective-permute-done.w0), channel_id=1, source_target_pairs={{0,1},{1,0},{2,3},{3,2},{4,5},{5,4},{6,7},{7,6},{8,9},{9,8},{10,11... | collective-permute-start | bytes 4718600 | tf_op jit(solution)/shard_map/ppermute | solution.py:182
  152.2 5.3 %collective-permute-start.3 = (bf16[3072,256]{1,0:T(8,128)(2,1)S(1)}, bf16[3072,256]{1,0:T(8,128)(2,1)S(1)}, u32[]{:S(2)}, u32[]{:S(2)}) collective-permute-start(bf16[3072,256]{1,0:T(8,128)(2,1)S(1)} %collective-permute-done.1.w1), channel_id=1, source_target_pairs={{0,1},{1,0},{2,3},{3,2},{4,5},{5,4},{6,7},{7,6},{8,9},{9,8},{10,11... | collective-permute-start | bytes 4718600 | tf_op jit(solution)/shard_map/ppermute | solution.py:182
  157.5 1.2 copy-start.8
  226.2 12.0 %collective-permute-start.4 = (bf16[2,3072,256]{2,1,0:T(8,128)(2,1)S(1)}, bf16[2,3072,256]{2,1,0:T(8,128)(2,1)}, u32[]{:S(2)}, u32[]{:S(2)}) collective-permute-start(bf16[2,3072,256]{2,1,0:T(8,128)(2,1)S(1)} %pad_maximum_fusion), channel_id=1, source_target_pairs={{0,1},{1,0},{2,3},{3,2},{4,5},{5,4},{6,7},{7,6},{8,9},{9,8},{10,11... | collective-permute-start | bytes 9437192 | tf_op jit(solution)/shard_map/ppermute | solution.py:197
  227.6 50.1 %all-to-all-start.4 = ((bf16[8,112,1024]{2,1,0:T(8,128)(2,1)}), bf16[8,112,1024]{2,1,0:T(8,128)(2,1)}, u32[]{:S(2)}, u32[]{:S(2)}) async-start(bf16[8,112,1024]{2,1,0:T(8,128)(2,1)} %bitcast.22), calls=%async_computation.4 | async-start | bytes 3670016 | tf_op jit(solution)/shard_map/all_to_all | solution.py:170
  233.0 2.8 copy-start.1
  235.8 2.2 copy-start
  277.7 36.5 %collective-permute-start.5 = (bf16[3072,256]{1,0:T(8,128)(2,1)}, bf16[3072,256]{1,0:T(8,128)(2,1)}, u32[]{:S(2)}, u32[]{:S(2)}) collective-permute-start(bf16[3072,256]{1,0:T(8,128)(2,1)} %get-tuple-element.40), channel_id=1, source_target_pairs={{0,0},{128,1},{64,64},{192,65},{1,128},{129,129},{65,192},{193,193... | collective-permute-start | bytes 4718600 | tf_op jit(solution)/shard_map/ppermute | solution.py:200
  284.5 31.3 %all-to-all-start.5 = ((bf16[16,56,1024]{2,1,0:T(8,128)(2,1)}), bf16[16,56,1024]{2,1,0:T(8,128)(2,1)S(1)}, u32[]{:S(2)}, u32[]{:S(2)}) async-start(bf16[16,56,1024]{2,1,0:T(8,128)(2,1)} %bitcast.72), calls=%async_computation.5 | async-start | bytes 3670016 | tf_op jit(solution)/shard_map/all_to_all | solution.py:166
  314.1 36.8 %collective-permute-start.6 = (bf16[3072,256]{1,0:T(8,128)(2,1)S(1)}, bf16[3072,256]{1,0:T(8,128)(2,1)}, u32[]{:S(2)}, u32[]{:S(2)}) collective-permute-start(bf16[3072,256]{1,0:T(8,128)(2,1)S(1)} %get-tuple-element.43), channel_id=1, source_target_pairs={{64,0},{192,1},{0,64},{128,65},{65,128},{193,129},{1,192},{129,193... | collective-permute-start | bytes 4718600 | tf_op jit(solution)/shard_map/ppermute | solution.py:202

commit v3 on v2

--- a/solution.py
+++ b/solution.py
@@ -45,14 +45,14 @@
 
 
 def forward_kernel(
-    x_ref, w0, w1, w2, w3, act_ref, fac_ref, hid_ref, gt_ref, ut_ref, dt_ref, w_ref
+    x_ref, own_ref, other_ref, act_ref, fac_ref, hid_ref, gt_ref, ut_ref, dt_ref, w_ref
 ):
     j = pl.program_id(0)
-    for i, ref in enumerate((w0, w1, w2, w3)):
+    for i in range(4):
 
         @pl.when(j == i)
         def _():
-            w_ref[...] = ref[...]
+            w_ref[...] = (own_ref, other_ref)[i // 2][i % 2]
 
     def step(i, _):
         at = pl.ds(pl.multiple_of(i * STEP, STEP), STEP)
@@ -82,13 +82,55 @@
     dx_ref[...] = dx.astype(BF16)
 
 
+def gradient_kernel(x_ref, dy_ref, dg_ref, du_ref, hid_ref, own_ref, theirs_ref, xt_ref):
+    j = pl.program_id(0)
+
+    @pl.when(j == 0)
+    def _():
+        xt_ref[...] = x_ref[...].T
+
+    def part(out_ref):
+        out_ref[0, :SUB, :] = dot(xt_ref[...], dg_ref[...], (1, 0)).astype(BF16)
+        out_ref[0, SUB : 2 * SUB, :] = dot(xt_ref[...], du_ref[...], (1, 0)).astype(BF16)
+        down = dot(hid_ref[...].T, dy_ref[...], (1, 0)).astype(BF16)
+        for f in range(SUB // PART):
+            low = 2 * SUB + f * PART
+            out_ref[0, low : low + PART, :] = down[:, f * PART : (f + 1) * PART]
+
+    @pl.when(j < 2)
+    def _():
+        part(own_ref)
+
+    @pl.when(j >= 2)
+    def _():
+        part(theirs_ref)
+
+
+def gradients(x, dy, d_gate, d_up, hidden):
+    whole = pl.BlockSpec((ROWS, SUB), lambda j: (0, 0))
+    columns = pl.BlockSpec((ROWS, PART), lambda j: (0, j))
+    return pl.pallas_call(
+        gradient_kernel,
+        grid=(4,),
+        in_specs=[whole, whole, columns, columns, columns],
+        out_specs=[
+            pl.BlockSpec((1, 3 * SUB, PART), lambda j: (jnp.minimum(j, 1), 0, 0)),
+            pl.BlockSpec((1, 3 * SUB, PART), lambda j: (jnp.maximum(j - 2, 0), 0, 0)),
+        ],
+        out_shape=[jax.ShapeDtypeStruct((2, 3 * SUB, PART), BF16)] * 2,
+        scratch_shapes=[pltpu.VMEM((SUB, ROWS), BF16)],
+        compiler_params=params(),
+        cost_estimate=pl.CostEstimate(flops=2**20, bytes_accessed=2**16, transcendentals=0),
+    )(x, dy, d_gate, d_up, hidden)
+
+
 def params():
     return pltpu.CompilerParams(
         dimension_semantics=("arbitrary",), vmem_limit_bytes=48 * 1024 * 1024
     )
 
 
-def forward(x, pieces):
+def forward(x, own, other):
     columns = pl.BlockSpec((ROWS, PART), lambda j: (0, j))
     float_out = jax.ShapeDtypeStruct((ROWS, SUB), F32)
     square = jax.ShapeDtypeStruct((SUB, SUB), BF16)
@@ -98,7 +140,7 @@
         in_specs=[
             pl.BlockSpec((ROWS, SUB), lambda j: (0, 0)),
         ]
-        + [pl.BlockSpec((3 * SUB, PART), lambda j: (0, 0))] * 4,
+        + [pl.BlockSpec((2, 3 * SUB, PART), lambda j: (0, 0, 0))] * 2,
         out_specs=[columns] * 3
         + [pl.BlockSpec((PART, SUB), lambda j: (j, 0))] * 2
         + [pl.BlockSpec((SUB, PART), lambda j: (0, j))],
@@ -108,7 +150,7 @@
         cost_estimate=pl.CostEstimate(
             flops=4 * ROWS * SUB * SUB, bytes_accessed=24 * 2**20, transcendentals=ROWS * SUB
         ),
-    )(x, *pieces)
+    )(x, own, other)
 
 
 def backward(dy, act, fac, gate_t, up_t, down_t):
@@ -132,16 +174,12 @@
     rows = toks * HEADS
     h = lax.axis_index("rep")
 
-    own = []
-    for q in range(2):
-        one = [
-            lax.dynamic_index_in_dim(w, (h + q) % 2, 0, keepdims=False)
-            for w in (w_gate, w_up, w_down)
-        ]
-        piece = jnp.concatenate([one[0], one[1], tall(one[2])], 0)
-        if own:
-            piece, own[0] = lax.optimization_barrier((piece, own[0]))
-        own.append(lax.ppermute(piece, PAIR, to_host(q)))
+    stages = []
+    for w in (w_gate, w_up, w_down):
+        pair = [lax.dynamic_index_in_dim(w, (h + q) % 2, 0, keepdims=False) for q in range(2)]
+        if stages:
+            pair, stages[-1] = lax.optimization_barrier((pair, stages[-1]))
+        stages.append([lax.ppermute(pair[q], PAIR, to_host(q)) for q in range(2)])
 
     def heads_first(a):
         return jnp.transpose(a, (1, 0, 2)).reshape(rows, 2)
@@ -178,37 +216,36 @@
     dy_slot = dot(pick_gate, cut(cotangent), (1, 0)).astype(BF16)
     x_rows = dot(regroup, in_plane(x_slot), (1, 0)).astype(BF16)
     dy_rows = in_plane(dy_slot)
-    x_rows, dy_rows, own = lax.optimization_barrier((x_rows, dy_rows, own))
-    other = [lax.ppermute(w, "core", SWAP) for w in own]
+    x_rows, dy_rows, stages = lax.optimization_barrier((x_rows, dy_rows, stages))
+    own = jnp.stack(
+        [
+            jnp.concatenate([stages[0][q], stages[1][q], tall(stages[2][q])], 0)
+            for q in range(2)
+        ],
+        0,
+    )
+    other = lax.ppermute(own, "core", SWAP)
     x = along_z(x_rows)
-    act, fac, hidden, gate_t, up_t, down_t = forward(x, own + other)
+    act, fac, hidden, gate_t, up_t, down_t = forward(x, own, other)
     dy = along_z(dot(regroup, dy_rows, (1, 0)).astype(BF16))
     d_gate, d_up, dx = backward(dy, act, fac, gate_t, up_t, down_t)
     dx = along_z(dx)
 
-    whole = (dot(x, d_gate, (0, 0)), dot(x, d_up, (0, 0)), dot(hidden, dy, (0, 0)))
-
-    def pack(q):
-        low, high = q * PART, (q + 1) * PART
-        return jnp.concatenate(
-            [whole[0][:, low:high], whole[1][:, low:high], tall(whole[2][low:high])], 0
-        )
-
-    theirs = lax.ppermute(jnp.stack([pack(2), pack(3)], 0).astype(BF16), "core", SWAP)
-    sums = [(pack(q) + theirs[q].astype(F32)).astype(BF16) for q in range(2)]
+    mine, theirs = gradients(x, dy, d_gate, d_up, hidden)
+    theirs = lax.ppermute(theirs, "core", SWAP)
+    sums = [(mine[q].astype(F32) + theirs[q].astype(F32)).astype(BF16) for q in range(2)]
     dx, sums = lax.optimization_barrier((dx, sums))
-    first = lax.ppermute(sums[0], PAIR, from_host(0))
-    first, second = lax.optimization_barrier((first, sums[1]))
-    back = [first, lax.ppermute(second, PAIR, from_host(1))]
+    back = [lax.ppermute(sums[q], PAIR, from_host(q)) for q in range(2)]
     returned = in_plane(dot(regroup, dx, (0, 0)).astype(BF16))
+    summed = dot(pick, returned, (0, 0)).astype(BF16)
+    token_grads = jnp.concatenate([summed[i * toks : (i + 1) * toks] for i in range(HEADS)], 1)
+
+    token_grads, back = lax.optimization_barrier((token_grads, back))
     even = h % 2 == 0
     both = [jnp.where(even, back[0], back[1]), jnp.where(even, back[1], back[0])]
     grad_gate = jnp.stack([a[:SUB] for a in both], 0)
     grad_up = jnp.stack([a[SUB : 2 * SUB] for a in both], 0)
     grad_down = jnp.stack([wide(a[2 * SUB :]) for a in both], 0)
-
-    summed = dot(pick, returned, (0, 0)).astype(BF16)
-    token_grads = jnp.concatenate([summed[i * toks : (i + 1) * toks] for i in range(HEADS)], 1)
     return (token_grads, grad_gate, grad_up, grad_down)
 
 

time: 358 us -> 392 us (1.095)
  waiting for transfers between devices: 216 us -> 246 us
  matrix products: 38.9 us -> 19.2 us
  Pallas kernels: 23.1 us -> 35.4 us
  starting transfers between devices: 50.5 us -> 62.3 us
    all_to_all x3, waiting for transfers between devices: 11.6 us -> 38.8 us  [in_plane(): return lax.all_to_all(a, ('y', 'x'), 0, 0, tiled=True).reshape(ROWS, SUB)]
    dot_general x9 -> x6, matrix products: 38.9 us -> 19.2 us  [dot(): lax.dot_general(a, b, ((over[:1], over[1:]), ((), ())), preferred_element...]
    pallas_call x0 -> x1, Pallas kernels: none -> 12.2 us  [gradients(): pl.pallas_call(gradient_kernel, grid=(4,), in_specs=[whole, whole, column...]
    ppermute x7 -> x10, starting transfers between devices: 11.8 us -> 22.8 us  [the longest x6 14.9 us: on_device(): stages.append([lax.ppermute(pair[q], PAIR, to_host(q)) for q in range(2)])]
    ppermute x7 -> x10, waiting for transfers between devices: 103 us -> 113 us  [the longest x6 63.5 us: on_device(): stages.append([lax.ppermute(pair[q], PAIR, to_host(q)) for q in range(2)])]
    all_to_all x3, waiting for transfers between devices: 101 us -> 94.2 us  [along_z(): return lax.all_to_all(a, ('zh', 'rep'), 0, 0, tiled=True).reshape(ROWS, SUB)]
    unnamed x36 -> x32, local copies, waits for them, and re-layouts: 12.6 us -> 10.7 us
  transfers between devices with their start and end apart: 13 -> 16, of which waited for: 11 -> 14; matrix products, arithmetic and copies ran while one was open for 9% -> 7% of each run, Pallas kernels for 3% -> 3%
where the time goes in v3:
time: 392 us; the launch traced here: 390 us
  waiting for transfers between devices  246 us (63%)
  starting transfers between devices  62.3 us (16%)
  Pallas kernels  35.4 us (9%)
  matrix products  19.2 us (5%)
  local copies, waits for them, and re-layouts  13.6 us (3%)
  other arithmetic  13.5 us (3%)
    all_to_all x3, waiting for transfers between devices, along_z(): return lax.all_to_all(a, ('zh', 'rep'), 0, 0, tiled=True).reshape(ROWS, SUB)  94.2 us
    ppermute x6, waiting for transfers between devices, on_device(): stages.append([lax.ppermute(pair[q], PAIR, to_host(q)) for q in range(2)])  63.5 us
    ppermute x2, waiting for transfers between devices, on_device(): back = [lax.ppermute(sums[q], PAIR, from_host(q)) for q in range(2)]  48 us
    all_to_all x3, waiting for transfers between devices, in_plane(): return lax.all_to_all(a, ('y', 'x'), 0, 0, tiled=True).reshape(ROWS, SUB)  38.8 us
    all_to_all x3, starting transfers between devices, in_plane(): return lax.all_to_all(a, ('y', 'x'), 0, 0, tiled=True).reshape(ROWS, SUB)  21.7 us
    dot_general x6, matrix products, dot(): lax.dot_general(a, b, ((over[:1], over[1:]), ((), ())), preferred_element...  19.2 us
    all_to_all x3, starting transfers between devices, along_z(): return lax.all_to_all(a, ('zh', 'rep'), 0, 0, tiled=True).reshape(ROWS, SUB)  17.8 us
    ppermute x6, starting transfers between devices, on_device(): stages.append([lax.ppermute(pair[q], PAIR, to_host(q)) for q in range(2)])  14.9 us
  transfers between devices with their start and end apart: 16, of which 14 were waited for; matrix products, arithmetic and copies ran while one was open for 7% of the time, Pallas kernels for 3%

profile of v3, /device:TPU:35, one launch (start us, length us, event | category | flops | bytes accessed | tf_op | source)
XLA Modules:
  0.0 390.5 jit_solution(1853089444156186356)
XLA Ops:
  2.6 2.4 convolution_convert_fusion
  5.0 7.0 %all-to-all-start = ((bf16[16,56,1024]{2,1,0:T(8,128)(2,1)}), bf16[16,56,1024]{2,1,0:T(8,128)(2,1)S(1)}, u32[]{:S(2)}, u32[]{:S(2)}) async-start(bf16[16,56,1024]{2,1,0:T(8,128)(2,1)} %bitcast.61), calls=%async_computation | async-start | bytes 3670016 | tf_op jit(solution)/shard_map/all_to_all | solution.py:204
  12.2 2.4 convolution_convert_fusion.1
  14.6 21.0 %all-to-all-done = bf16[16,56,1024]{2,1,0:T(8,128)(2,1)S(1)} async-done(((bf16[16,56,1024]{2,1,0:T(8,128)(2,1)}), bf16[16,56,1024]{2,1,0:T(8,128)(2,1)S(1)}, u32[]{:S(2)}, u32[]{:S(2)}) %all-to-all-start) | async-done | bytes 1835040 | tf_op jit(solution)/shard_map/all_to_all | solution.py:204
  35.6 7.8 %all-to-all-start.1 = ((bf16[16,56,1024]{2,1,0:T(8,128)(2,1)}), bf16[16,56,1024]{2,1,0:T(8,128)(2,1)}, u32[]{:S(2)}, u32[]{:S(2)}) async-start(bf16[16,56,1024]{2,1,0:T(8,128)(2,1)} %bitcast.62), calls=%async_computation.1 | async-start | bytes 3670016 | tf_op jit(solution)/shard_map/all_to_all | solution.py:204
  43.5 3.8 collective-permute-start.1
  47.3 3.4 collective-permute-start
  50.8 11.5 %collective-permute-done.1 = bf16[1024,256]{1,0:T(8,128)(2,1)S(1)} collective-permute-done((bf16[1024,256]{1,0:T(8,128)(2,1)S(1)}, bf16[1024,256]{1,0:T(8,128)(2,1)S(1)}, u32[]{:S(2)}, u32[]{:S(2)}) %collective-permute-start.1) | collective-permute-done | bytes 524320 | tf_op jit(solution)/shard_map/ppermute | solution.py:182
  62.4 8.0 %collective-permute-done = bf16[1024,256]{1,0:T(8,128)(2,1)S(1)} collective-permute-done((bf16[1024,256]{1,0:T(8,128)(2,1)S(1)}, bf16[1024,256]{1,0:T(8,128)(2,1)S(1)}, u32[]{:S(2)}, u32[]{:S(2)}) %collective-permute-start) | collective-permute-done | bytes 524320 | tf_op jit(solution)/shard_map/ppermute | solution.py:182
  70.4 5.3 %collective-permute-start.2 = (bf16[1024,256]{1,0:T(8,128)(2,1)S(1)}, bf16[1024,256]{1,0:T(8,128)(2,1)S(1)}, u32[]{:S(2)}, u32[]{:S(2)}) collective-permute-start(bf16[1024,256]{1,0:T(8,128)(2,1)S(1)} %get-tuple-element.39), channel_id=1, source_target_pairs={{0,0},{1,128},{64,64},{65,192},{128,1},{129,129},{192,65},{193,193... | collective-permute-start | bytes 1572872 | tf_op jit(solution)/shard_map/ppermute | solution.py:182
  75.9 11.3 %collective-permute-done.2 = bf16[1024,256]{1,0:T(8,128)(2,1)S(1)} collective-permute-done((bf16[1024,256]{1,0:T(8,128)(2,1)S(1)}, bf16[1024,256]{1,0:T(8,128)(2,1)S(1)}, u32[]{:S(2)}, u32[]{:S(2)}) %collective-permute-start.2) | collective-permute-done | bytes 524320 | tf_op jit(solution)/shard_map/ppermute | solution.py:182
  87.2 12.3 %collective-permute-done.3 = bf16[1024,256]{1,0:T(8,128)(2,1)} collective-permute-done((bf16[1024,256]{1,0:T(8,128)(2,1)S(1)}, bf16[1024,256]{1,0:T(8,128)(2,1)}, u32[]{:S(2)}, u32[]{:S(2)}) %collective-permute-start.3) | collective-permute-done | bytes 524320 | tf_op jit(solution)/shard_map/ppermute | solution.py:182
  101.8 3.3 fusion.6
  105.1 13.7 %collective-permute-done.4 = bf16[256,1024]{1,0:T(8,128)(2,1)} collective-permute-done((bf16[256,1024]{1,0:T(8,128)(2,1)S(1)}, bf16[256,1024]{1,0:T(8,128)(2,1)}, u32[]{:S(2)}, u32[]{:S(2)}) %collective-permute-start.4) | collective-permute-done | bytes 524320 | tf_op jit(solution)/shard_map/ppermute | solution.py:182
  118.8 6.7 %collective-permute-done.5 = bf16[256,1024]{1,0:T(8,128)(2,1)} collective-permute-done((bf16[256,1024]{1,0:T(8,128)(2,1)S(1)}, bf16[256,1024]{1,0:T(8,128)(2,1)}, u32[]{:S(2)}, u32[]{:S(2)}) %collective-permute-start.5) | collective-permute-done | bytes 524320 | tf_op jit(solution)/shard_map/ppermute | solution.py:182
  125.4 6.5 %all-to-all-start.3 = ((bf16[8,112,1024]{2,1,0:T(8,128)(2,1)}), bf16[8,112,1024]{2,1,0:T(8,128)(2,1)S(1)}, u32[]{:S(2)}, u32[]{:S(2)}) async-start(bf16[8,112,1024]{2,1,0:T(8,128)(2,1)} %bitcast.63), calls=%async_computation.3 | async-start | bytes 3670016 | tf_op jit(solution)/shard_map/all_to_all | solution.py:208
  142.9 4.9 %fusion.7 = bf16[896,1024]{1,0:T(8,128)(2,1)} fusion(bf16[896,1024]{1,0:T(8,128)(2,1)} %bitcast.11, s32[896]{0:T(1024)S(1)} %fusion.49), kind=kOutput, calls=%fused_computation.13 | convolution fusion | flops 1645887488 | bytes 3673600 | tf_op jit(solution)/shard_map/dot_general | solution.py:44
  147.8 27.6 %all-to-all-done.3 = bf16[8,112,1024]{2,1,0:T(8,128)(2,1)S(1)} async-done(((bf16[8,112,1024]{2,1,0:T(8,128)(2,1)}), bf16[8,112,1024]{2,1,0:T(8,128)(2,1)S(1)}, u32[]{:S(2)}, u32[]{:S(2)}) %all-to-all-start.3) | async-done | bytes 1835040 | tf_op jit(solution)/shard_map/all_to_all | solution.py:208
  175.4 6.8 %all-to-all-start.2 = ((bf16[8,112,1024]{2,1,0:T(8,128)(2,1)}), bf16[8,112,1024]{2,1,0:T(8,128)(2,1)}, u32[]{:S(2)}, u32[]{:S(2)}) async-start(bf16[8,112,1024]{2,1,0:T(8,128)(2,1)} %bitcast.64), calls=%async_computation.2 | async-start | bytes 3670016 | tf_op jit(solution)/shard_map/all_to_all | solution.py:208
  182.2 12.3 %shard_map.111 = (f32[896,1024]{1,0:T(8,128)}, f32[896,1024]{1,0:T(8,128)}, bf16[896,1024]{1,0:T(8,128)(2,1)S(1)}, bf16[1024,1024]{1,0:T(8,128)(2,1)S(1)}, bf16[...) custom-call(bf16[896,1024]{1,0:T(8,128)(2,1)S(1)} %bitcast.55, bf16[2,3072,256]{2,1,0:T(8,128)(2,1)} %pad_maximum_fusion.own_ref, ...), custom_call_target="tpu_custom_call" | custom-call | flops 3758096384 | bytes 25165824 | tf_op jit(solution)/shard_map/pallas_call | solution.py:137
  197.2 29.1 %all-to-all-done.2 = bf16[8,112,1024]{2,1,0:T(8,128)(2,1)} async-done(((bf16[8,112,1024]{2,1,0:T(8,128)(2,1)}), bf16[8,112,1024]{2,1,0:T(8,128)(2,1)}, u32[]{:S(2)}, u32[]{:S(2)}) %all-to-all-start.2) | async-done | bytes 1835040 | tf_op jit(solution)/shard_map/all_to_all | solution.py:208
  226.3 10.8 %shard_map.112 = (bf16[896,1024]{1,0:T(8,128)(2,1)S(1)}, bf16[896,1024]{1,0:T(8,128)(2,1)S(1)}, bf16[896,1024]{1,0:T(8,128)(2,1)S(1)}) custom-call(bf16[896,1024]{1,0:T(8,128)(2,1)} %bitcast.19.dy_ref, f32[896,1024]{1,0:T(8,128)} %get-tuple-element.53.act_ref, f32[896,1024]{1,0:T(8,128)} %get-tuple-element.54.fac_ref, bf16[1024,1024]{1,0:T(8,128)(2,1)} %copy-done.3, ...), custom_call_target="tpu_custom_call" | custom-call | flops 5637144576 | bytes 20971520 | tf_op jit(solution)/shard_map/pallas_call | solution.py:159
  238.5 12.2 %shard_map.113 = (bf16[2,3072,256]{2,1,0:T(8,128)(2,1)}, bf16[2,3072,256]{2,1,0:T(8,128)(2,1)}) custom-call(bf16[896,1024]{1,0:T(8,128)(2,1)S(1)} %bitcast.56, bf16[896,1024]{1,0:T(8,128)(2,1)} %bitcast.19.dy_ref, bf16[896,1024]{1,0:T(8,128)(2,1)S(1)} %get-tuple-element.59.dg_ref, bf16[896,1024]{1,0:T(8,128)(2,1)} %copy-done.2, bf16[896,1024]{1,0:T(8,128)(2,1)} %copy-done.1), custom_call_target="tpu_custom_call" | custom-call | flops 1048576 | bytes 65536 | tf_op jit(solution)/shard_map/pallas_call | solution.py:112
  252.0 4.5 %all-to-all-start.4 = ((bf16[8,112,1024]{2,1,0:T(8,128)(2,1)}), bf16[8,112,1024]{2,1,0:T(8,128)(2,1)}, u32[]{:S(2)}, u32[]{:S(2)}) async-start(bf16[8,112,1024]{2,1,0:T(8,128)(2,1)} %bitcast.57), calls=%async_computation.4 | async-start | bytes 3670016 | tf_op jit(solution)/shard_map/all_to_all | solution.py:208
  257.7 4.3 %fusion.13 = (bf16[3072,256]{1,0:T(8,128)(2,1)}, bf16[3072,256]{1,0:T(8,128)(2,1)}) fusion(bf16[2,3072,256]{2,1,0:T(8,128)(2,1)} %collective-permute-done.7, bf16[2,3072,256]{2,1,0:T(8,128)(2,1)S(1)} %copy-done.4), kind=kLoop, calls=%fused_computation.21 | loop fusion | flops 6291456 | bytes 9437184 | tf_op jit(solution)/shard_map/convert_element_type | solution.py:236
  262.0 37.5 %all-to-all-done.4 = bf16[8,112,1024]{2,1,0:T(8,128)(2,1)} async-done(((bf16[8,112,1024]{2,1,0:T(8,128)(2,1)}), bf16[8,112,1024]{2,1,0:T(8,128)(2,1)}, u32[]{:S(2)}, u32[]{:S(2)}) %all-to-all-start.4) | async-done | bytes 1835040 | tf_op jit(solution)/shard_map/all_to_all | solution.py:208
  299.5 4.9 %fusion.8 = bf16[896,1024]{1,0:T(8,128)(2,1)} fusion(bf16[896,1024]{1,0:T(8,128)(2,1)} %bitcast.25, s32[896]{0:T(1024)S(1)} %fusion.49), kind=kOutput, calls=%fused_computation.14 | convolution fusion | flops 1645887488 | bytes 3673600 | tf_op jit(solution)/shard_map/dot_general | solution.py:44
  304.4 6.9 %all-to-all-start.5 = ((bf16[16,56,1024]{2,1,0:T(8,128)(2,1)}), bf16[16,56,1024]{2,1,0:T(8,128)(2,1)S(1)}, u32[]{:S(2)}, u32[]{:S(2)}) async-start(bf16[16,56,1024]{2,1,0:T(8,128)(2,1)} %bitcast.66), calls=%async_computation.5 | async-start | bytes 3670016 | tf_op jit(solution)/shard_map/all_to_all | solution.py:204
  313.2 3.4 collective-permute-start.9
  316.6 17.8 %all-to-all-done.5 = bf16[16,56,1024]{2,1,0:T(8,128)(2,1)S(1)} async-done(((bf16[16,56,1024]{2,1,0:T(8,128)(2,1)}), bf16[16,56,1024]{2,1,0:T(8,128)(2,1)S(1)}, u32[]{:S(2)}, u32[]{:S(2)}) %all-to-all-start.5) | async-done | bytes 1835040 | tf_op jit(solution)/shard_map/all_to_all | solution.py:204
  336.8 19.8 %collective-permute-done.8 = bf16[3072,256]{1,0:T(8,128)(2,1)} collective-permute-done((bf16[3072,256]{1,0:T(8,128)(2,1)}, bf16[3072,256]{1,0:T(8,128)(2,1)}, u32[]{:S(2)}, u32[]{:S(2)}) %collective-permute-start.8) | collective-permute-done | bytes 1572896 | tf_op jit(solution)/shard_map/ppermute | solution.py:238
  356.6 28.2 %collective-permute-done.9 = bf16[3072,256]{1,0:T(8,128)(2,1)} collective-permute-done((bf16[3072,256]{1,0:T(8,128)(2,1)S(1)}, bf16[3072,256]{1,0:T(8,128)(2,1)}, u32[]{:S(2)}, u32[]{:S(2)}) %collective-permute-start.9) | collective-permute-done | bytes 1572896 | tf_op jit(solution)/shard_map/ppermute | solution.py:238
  (65 shorter events, 32.1 us)
Async XLA Ops:
  5.0 7.1 %copy-start.10 = (bf16[128,4,2]{0,2,1:T(2,128)(2,1)S(1)}, bf16[128,4,2]{0,2,1:T(2,128)(2,1)}, u32[]{:S(2)}) copy-start(bf16[128,4,2]{0,2,1:T(2,128)(2,1)} %param.10) | copy-start | bytes 6148
  5.0 7.1 %copy-start.6 = (bf16[128,4096]{1,0:T(8,128)(2,1)S(1)}, bf16[128,4096]{1,0:T(8,128)(2,1)}, u32[]{:S(2)}) copy-start(bf16[128,4096]{1,0:T(8,128)(2,1)} %param.9) | copy-start | bytes 3145732
  5.0 30.5 %all-to-all-start = ((bf16[16,56,1024]{2,1,0:T(8,128)(2,1)}), bf16[16,56,1024]{2,1,0:T(8,128)(2,1)S(1)}, u32[]{:S(2)}, u32[]{:S(2)}) async-start(bf16[16,56,1024]{2,1,0:T(8,128)(2,1)} %bitcast.61), calls=%async_computation | async-start | bytes 3670016 | tf_op jit(solution)/shard_map/all_to_all | solution.py:204
  35.6 7.8 %copy-start.7 = (bf16[2,1024,256]{2,1,0:T(8,128)(2,1)S(1)}, bf16[2,1024,256]{2,1,0:T(8,128)(2,1)}, u32[]{:S(2)}) copy-start(bf16[2,1024,256]{2,1,0:T(8,128)(2,1)} %param.13) | copy-start | bytes 3145732
  35.6 89.9 %all-to-all-start.1 = ((bf16[16,56,1024]{2,1,0:T(8,128)(2,1)}), bf16[16,56,1024]{2,1,0:T(8,128)(2,1)}, u32[]{:S(2)}, u32[]{:S(2)}) async-start(bf16[16,56,1024]{2,1,0:T(8,128)(2,1)} %bitcast.62), calls=%async_computation.1 | async-start | bytes 3670016 | tf_op jit(solution)/shard_map/all_to_all | solution.py:204
  43.4 7.3 %copy-start.8 = (bf16[2,1024,256]{2,1,0:T(8,128)(2,1)S(1)}, bf16[2,1024,256]{2,1,0:T(8,128)(2,1)}, u32[]{:S(2)}) copy-start(bf16[2,1024,256]{2,1,0:T(8,128)(2,1)} %param.14) | copy-start | bytes 3145732
  43.4 32.4 %copy-start.9 = (bf16[2,256,1024]{2,1,0:T(8,128)(2,1)S(1)}, bf16[2,256,1024]{2,1,0:T(8,128)(2,1)}, u32[]{:S(2)}) copy-start(bf16[2,256,1024]{2,1,0:T(8,128)(2,1)} %param.15) | copy-start | bytes 3145732
  43.5 18.8 %collective-permute-start.1 = (bf16[1024,256]{1,0:T(8,128)(2,1)S(1)}, bf16[1024,256]{1,0:T(8,128)(2,1)S(1)}, u32[]{:S(2)}, u32[]{:S(2)}) collective-permute-start(bf16[1024,256]{1,0:T(8,128)(2,1)S(1)} %get-tuple-element.94), channel_id=1, source_target_pairs={{0,64},{1,192},{64,0},{65,128},{128,65},{129,193},{192,1},{193,129... | collective-permute-start | bytes 1572872 | tf_op jit(solution)/shard_map/ppermute | solution.py:182
  47.3 23.0 %collective-permute-start = (bf16[1024,256]{1,0:T(8,128)(2,1)S(1)}, bf16[1024,256]{1,0:T(8,128)(2,1)S(1)}, u32[]{:S(2)}, u32[]{:S(2)}) collective-permute-start(bf16[1024,256]{1,0:T(8,128)(2,1)S(1)} %get-tuple-element.95), channel_id=1, source_target_pairs={{0,0},{1,128},{64,64},{65,192},{128,1},{129,129},{192,65},{193,193... | collective-permute-start | bytes 1572872 | tf_op jit(solution)/shard_map/ppermute | solution.py:182
  70.4 16.8 %collective-permute-start.2 = (bf16[1024,256]{1,0:T(8,128)(2,1)S(1)}, bf16[1024,256]{1,0:T(8,128)(2,1)S(1)}, u32[]{:S(2)}, u32[]{:S(2)}) collective-permute-start(bf16[1024,256]{1,0:T(8,128)(2,1)S(1)} %get-tuple-element.39), channel_id=1, source_target_pairs={{0,0},{1,128},{64,64},{65,192},{128,1},{129,129},{192,65},{193,193... | collective-permute-start | bytes 1572872 | tf_op jit(solution)/shard_map/ppermute | solution.py:182
  75.6 23.9 %collective-permute-start.3 = (bf16[1024,256]{1,0:T(8,128)(2,1)S(1)}, bf16[1024,256]{1,0:T(8,128)(2,1)}, u32[]{:S(2)}, u32[]{:S(2)}) collective-permute-start(bf16[1024,256]{1,0:T(8,128)(2,1)S(1)} %get-tuple-element.40), channel_id=1, source_target_pairs={{0,64},{1,192},{64,0},{65,128},{128,65},{129,193},{192,1},{193,129... | collective-permute-start | bytes 1572872 | tf_op jit(solution)/shard_map/ppermute | solution.py:182
  99.5 19.3 %collective-permute-start.4 = (bf16[256,1024]{1,0:T(8,128)(2,1)S(1)}, bf16[256,1024]{1,0:T(8,128)(2,1)}, u32[]{:S(2)}, u32[]{:S(2)}) collective-permute-start(bf16[256,1024]{1,0:T(8,128)(2,1)S(1)} %get-tuple-element.43), channel_id=1, source_target_pairs={{0,0},{1,128},{64,64},{65,192},{128,1},{129,129},{192,65},{193,193... | collective-permute-start | bytes 1572872 | tf_op jit(solution)/shard_map/ppermute | solution.py:182
  101.4 24.0 %collective-permute-start.5 = (bf16[256,1024]{1,0:T(8,128)(2,1)S(1)}, bf16[256,1024]{1,0:T(8,128)(2,1)}, u32[]{:S(2)}, u32[]{:S(2)}) collective-permute-start(bf16[256,1024]{1,0:T(8,128)(2,1)S(1)} %get-tuple-element.44), channel_id=1, source_target_pairs={{0,64},{1,192},{64,0},{65,128},{128,65},{129,193},{192,1},{193,129... | collective-permute-start | bytes 1572872 | tf_op jit(solution)/shard_map/ppermute | solution.py:182
  125.4 49.9 %all-to-all-start.3 = ((bf16[8,112,1024]{2,1,0:T(8,128)(2,1)}), bf16[8,112,1024]{2,1,0:T(8,128)(2,1)S(1)}, u32[]{:S(2)}, u32[]{:S(2)}) async-start(bf16[8,112,1024]{2,1,0:T(8,128)(2,1)} %bitcast.63), calls=%async_computation.3 | async-start | bytes 3670016 | tf_op jit(solution)/shard_map/all_to_all | solution.py:208
  141.6 40.5 %collective-permute-start.6 = (bf16[2,3072,256]{2,1,0:T(8,128)(2,1)}, bf16[2,3072,256]{2,1,0:T(8,128)(2,1)}, u32[]{:S(2)}, u32[]{:S(2)}) collective-permute-start(bf16[2,3072,256]{2,1,0:T(8,128)(2,1)} %pad_maximum_fusion.own_ref), channel_id=1, source_target_pairs={{0,1},{1,0},{2,3},{3,2},{4,5},{5,4},{6,7},{7,6},{8,9},{9,8},{10,11... | collective-permute-start | bytes 9437192 | tf_op jit(solution)/shard_map/ppermute | solution.py:227
  175.4 51.0 %all-to-all-start.2 = ((bf16[8,112,1024]{2,1,0:T(8,128)(2,1)}), bf16[8,112,1024]{2,1,0:T(8,128)(2,1)}, u32[]{:S(2)}, u32[]{:S(2)}) async-start(bf16[8,112,1024]{2,1,0:T(8,128)(2,1)} %bitcast.64), calls=%async_computation.2 | async-start | bytes 3670016 | tf_op jit(solution)/shard_map/all_to_all | solution.py:208
  194.5 1.3 copy-start.1
  195.8 1.4 copy-start.3
  237.1 1.3 copy-start.2
  238.5 12.2 %copy-start = (bf16[896,1024]{1,0:T(8,128)(2,1)}, bf16[896,1024]{1,0:T(8,128)(2,1)S(1)}, u32[]{:S(2)}) copy-start(bf16[896,1024]{1,0:T(8,128)(2,1)S(1)} %get-tuple-element.58) | copy-start | bytes 5505028
  250.7 7.0 %collective-permute-start.7 = (bf16[2,3072,256]{2,1,0:T(8,128)(2,1)}, bf16[2,3072,256]{2,1,0:T(8,128)(2,1)}, u32[]{:S(2)}, u32[]{:S(2)}) collective-permute-start(bf16[2,3072,256]{2,1,0:T(8,128)(2,1)} %get-tuple-element.63), channel_id=1, source_target_pairs={{0,1},{1,0},{2,3},{3,2},{4,5},{5,4},{6,7},{7,6},{8,9},{9,8},{10,11... | collective-permute-start | bytes 9437192 | tf_op jit(solution)/shard_map/ppermute | solution.py:235
  252.0 5.6 %copy-start.4 = (bf16[2,3072,256]{2,1,0:T(8,128)(2,1)S(1)}, bf16[2,3072,256]{2,1,0:T(8,128)(2,1)}, u32[]{:S(2)}) copy-start(bf16[2,3072,256]{2,1,0:T(8,128)(2,1)} %get-tuple-element.62) | copy-start | bytes 9437188
  252.0 47.4 %all-to-all-start.4 = ((bf16[8,112,1024]{2,1,0:T(8,128)(2,1)}), bf16[8,112,1024]{2,1,0:T(8,128)(2,1)}, u32[]{:S(2)}, u32[]{:S(2)}) async-start(bf16[8,112,1024]{2,1,0:T(8,128)(2,1)} %bitcast.57), calls=%async_computation.4 | async-start | bytes 3670016 | tf_op jit(solution)/shard_map/all_to_all | solution.py:208
  304.4 8.8 %copy-start.5 = (bf16[3072,256]{1,0:T(8,128)(2,1)S(1)}, bf16[3072,256]{1,0:T(8,128)(2,1)}, u32[]{:S(2)}) copy-start(bf16[3072,256]{1,0:T(8,128)(2,1)} %get-tuple-element.66) | copy-start | bytes 4718596
  304.4 30.0 %all-to-all-start.5 = ((bf16[16,56,1024]{2,1,0:T(8,128)(2,1)}), bf16[16,56,1024]{2,1,0:T(8,128)(2,1)S(1)}, u32[]{:S(2)}, u32[]{:S(2)}) async-start(bf16[16,56,1024]{2,1,0:T(8,128)(2,1)} %bitcast.66), calls=%async_computation.5 | async-start | bytes 3670016 | tf_op jit(solution)/shard_map/all_to_all | solution.py:204
  311.3 45.3 %collective-permute-start.8 = (bf16[3072,256]{1,0:T(8,128)(2,1)}, bf16[3072,256]{1,0:T(8,128)(2,1)}, u32[]{:S(2)}, u32[]{:S(2)}) collective-permute-start(bf16[3072,256]{1,0:T(8,128)(2,1)} %get-tuple-element.65), channel_id=1, source_target_pairs={{0,0},{128,1},{64,64},{192,65},{1,128},{129,129},{65,192},{193,193... | collective-permute-start | bytes 4718600 | tf_op jit(solution)/shard_map/ppermute | solution.py:238
  313.2 71.6 %collective-permute-start.9 = (bf16[3072,256]{1,0:T(8,128)(2,1)S(1)}, bf16[3072,256]{1,0:T(8,128)(2,1)}, u32[]{:S(2)}, u32[]{:S(2)}) collective-permute-start(bf16[3072,256]{1,0:T(8,128)(2,1)S(1)} %copy-done.5), channel_id=1, source_target_pairs={{64,0},{192,1},{0,64},{128,65},{65,128},{193,129},{1,192},{129,193... | collective-permute-start | bytes 4718600 | tf_op jit(solution)/shard_map/ppermute | solution.py:238

commit v4 on v2

--- a/solution.py
+++ b/solution.py
@@ -32,27 +32,23 @@
     return [(b, a) for a, b in to_host(q)]
 
 
-def tall(down):
-    return jnp.concatenate([down[:, i * PART : (i + 1) * PART] for i in range(SUB // PART)], 0)
-
-
-def wide(stack):
-    return jnp.concatenate([stack[i * PART : (i + 1) * PART] for i in range(SUB // PART)], 1)
-
-
 def dot(a, b, over):
     return lax.dot_general(a, b, ((over[:1], over[1:]), ((), ())), preferred_element_type=F32)
 
 
 def forward_kernel(
-    x_ref, w0, w1, w2, w3, act_ref, fac_ref, hid_ref, gt_ref, ut_ref, dt_ref, w_ref
+    x_ref, own_ref, other_ref, _, act_ref, fac_ref, hid_ref, gt_ref, ut_ref, dt_ref, xt_ref, w_ref
 ):
     j = pl.program_id(0)
-    for i, ref in enumerate((w0, w1, w2, w3)):
+    for i in range(4):
 
         @pl.when(j == i)
         def _():
-            w_ref[...] = ref[...]
+            w_ref[...] = (own_ref, other_ref)[i // 2][i % 2]
+
+    @pl.when(j == 0)
+    def _():
+        xt_ref[...] = x_ref[...].T
 
     def step(i, _):
         at = pl.ds(pl.multiple_of(i * STEP, STEP), STEP)
@@ -82,13 +78,104 @@
     dx_ref[...] = dx.astype(BF16)
 
 
-def params():
+def gradient_kernel(xt_ref, dy_ref, dg_ref, du_ref, hid_ref, theirs_ref, mine_ref):
+    j = pl.program_id(0)
+
+    def part(out_ref):
+        out_ref[:SUB, :] = dot(xt_ref[...], dg_ref[...], (1, 0)).astype(BF16)
+        out_ref[SUB : 2 * SUB, :] = dot(xt_ref[...], du_ref[...], (1, 0)).astype(BF16)
+        down = dot(hid_ref[...].T, dy_ref[...], (1, 0)).astype(BF16)
+        for f in range(SUB // PART):
+            low = 2 * SUB + f * PART
+            out_ref[low : low + PART, :] = down[:, f * PART : (f + 1) * PART]
+
+    @pl.when(j == 0)
+    def _():
+        part(theirs_ref)
+
+    @pl.when(j == 1)
+    def _():
+        part(mine_ref)
+
+
+def gradients(x_t, dy, d_gate, d_up, hidden, q):
+    columns = pl.BlockSpec((ROWS, PART), lambda j: (0, q + 2 * (1 - j)))
+    out = pl.BlockSpec((3 * SUB, PART), lambda j: (0, 0))
+    return pl.pallas_call(
+        gradient_kernel,
+        grid=(2,),
+        in_specs=[
+            pl.BlockSpec((SUB, ROWS), lambda j: (0, 0)),
+            pl.BlockSpec((ROWS, SUB), lambda j: (0, 0)),
+            columns,
+            columns,
+            columns,
+        ],
+        out_specs=[out, out],
+        out_shape=[jax.ShapeDtypeStruct((3 * SUB, PART), BF16)] * 2,
+        compiler_params=params(),
+        cost_estimate=pl.CostEstimate(
+            flops=3 * ROWS * SUB * SUB, bytes_accessed=10 * 2**20, transcendentals=0
+        ),
+    )(x_t, dy, d_gate, d_up, hidden)
+
+
+def pack_kernel(odd_ref, g_ref, u_ref, d_ref, first_ref, second_ref):
+    odd = odd_ref[0]
+    for out_ref, p in ((first_ref, odd), (second_ref, 1 - odd)):
+        out_ref[:SUB, :] = g_ref[p]
+        out_ref[SUB : 2 * SUB, :] = u_ref[p]
+        down = d_ref[p]
+        for f in range(SUB // PART):
+            low = 2 * SUB + f * PART
+            out_ref[low : low + PART, :] = down[:, f * PART : (f + 1) * PART]
+
+
+def unpack_kernel(odd_ref, first_ref, second_ref, g_ref, u_ref, d_ref):
+    odd = odd_ref[0]
+    for ref, p in ((first_ref, odd), (second_ref, 1 - odd)):
+        g_ref[p] = ref[:SUB, :]
+        u_ref[p] = ref[SUB : 2 * SUB, :]
+        for f in range(SUB // PART):
+            low = 2 * SUB + f * PART
+            d_ref[p, :, f * PART : (f + 1) * PART] = ref[low : low + PART, :]
+
+
+def repack(kernel, odd, arrays, shapes):
+    return pl.pallas_call(
+        kernel,
+        in_specs=[pl.BlockSpec(memory_space=pltpu.SMEM)]
+        + [pl.BlockSpec(memory_space=pltpu.VMEM)] * len(arrays),
+        out_specs=[pl.BlockSpec(memory_space=pltpu.VMEM)] * len(shapes),
+        out_shape=[jax.ShapeDtypeStruct(shape, BF16) for shape in shapes],
+        compiler_params=pltpu.CompilerParams(vmem_limit_bytes=32 * 1024 * 1024),
+        cost_estimate=pl.CostEstimate(flops=0, bytes_accessed=6 * 2**20, transcendentals=0),
+    )(odd, *arrays)
+
+
+def glance_kernel(a_ref, b_ref, c_ref, out_ref):
+    out_ref[...] = a_ref[...] + b_ref[...] + c_ref[...]
+
+
+def glance(arrays):
+    corner = pl.BlockSpec((16, 128), lambda i: (0, 0))
+    return pl.pallas_call(
+        glance_kernel,
+        grid=(1,),
+        in_specs=[corner] * 3,
+        out_specs=corner,
+        out_shape=jax.ShapeDtypeStruct((16, 128), BF16),
+        cost_estimate=pl.CostEstimate(flops=200000000000, bytes_accessed=8192, transcendentals=0),
+    )(*arrays)
+
+
+def params(mib=48):
     return pltpu.CompilerParams(
-        dimension_semantics=("arbitrary",), vmem_limit_bytes=48 * 1024 * 1024
+        dimension_semantics=("arbitrary",), vmem_limit_bytes=mib * 1024 * 1024
     )
 
 
-def forward(x, pieces):
+def forward(x, own, other, seen):
     columns = pl.BlockSpec((ROWS, PART), lambda j: (0, j))
     float_out = jax.ShapeDtypeStruct((ROWS, SUB), F32)
     square = jax.ShapeDtypeStruct((SUB, SUB), BF16)
@@ -98,17 +185,20 @@
         in_specs=[
             pl.BlockSpec((ROWS, SUB), lambda j: (0, 0)),
         ]
-        + [pl.BlockSpec((3 * SUB, PART), lambda j: (0, 0))] * 4,
+        + [pl.BlockSpec((2, 3 * SUB, PART), lambda j: (0, 0, 0))] * 2
+        + [pl.BlockSpec((16, 128), lambda j: (0, 0))],
         out_specs=[columns] * 3
         + [pl.BlockSpec((PART, SUB), lambda j: (j, 0))] * 2
-        + [pl.BlockSpec((SUB, PART), lambda j: (0, j))],
-        out_shape=[float_out, float_out, jax.ShapeDtypeStruct((ROWS, SUB), BF16)] + [square] * 3,
+        + [pl.BlockSpec((SUB, PART), lambda j: (0, j)), pl.BlockSpec((SUB, ROWS), lambda j: (0, 0))],
+        out_shape=[float_out, float_out, jax.ShapeDtypeStruct((ROWS, SUB), BF16)]
+        + [square] * 3
+        + [jax.ShapeDtypeStruct((SUB, ROWS), BF16)],
         scratch_shapes=[pltpu.VMEM((3 * SUB, PART), BF16)],
         compiler_params=params(),
         cost_estimate=pl.CostEstimate(
             flops=4 * ROWS * SUB * SUB, bytes_accessed=24 * 2**20, transcendentals=ROWS * SUB
         ),
-    )(x, *pieces)
+    )(x, own, other, seen)
 
 
 def backward(dy, act, fac, gate_t, up_t, down_t):
@@ -120,7 +210,7 @@
         in_specs=[some] * 3 + [square] * 3,
         out_specs=[some] * 3,
         out_shape=[jax.ShapeDtypeStruct((ROWS, SUB), BF16)] * 3,
-        compiler_params=params(),
+        compiler_params=params(60),
         cost_estimate=pl.CostEstimate(
             flops=6 * ROWS * SUB * SUB, bytes_accessed=20 * 2**20, transcendentals=0
         ),
@@ -132,16 +222,9 @@
     rows = toks * HEADS
     h = lax.axis_index("rep")
 
-    own = []
-    for q in range(2):
-        one = [
-            lax.dynamic_index_in_dim(w, (h + q) % 2, 0, keepdims=False)
-            for w in (w_gate, w_up, w_down)
-        ]
-        piece = jnp.concatenate([one[0], one[1], tall(one[2])], 0)
-        if own:
-            piece, own[0] = lax.optimization_barrier((piece, own[0]))
-        own.append(lax.ppermute(piece, PAIR, to_host(q)))
+    odd = (h % 2).reshape(1)
+    pieces = repack(pack_kernel, odd, (w_gate, w_up, w_down), [(3 * SUB, PART)] * 2)
+    own = [lax.ppermute(pieces[q], PAIR, to_host(q)) for q in range(2)]
 
     def heads_first(a):
         return jnp.transpose(a, (1, 0, 2)).reshape(rows, 2)
@@ -178,37 +261,32 @@
     dy_slot = dot(pick_gate, cut(cotangent), (1, 0)).astype(BF16)
     x_rows = dot(regroup, in_plane(x_slot), (1, 0)).astype(BF16)
     dy_rows = in_plane(dy_slot)
-    x_rows, dy_rows, own = lax.optimization_barrier((x_rows, dy_rows, own))
-    other = [lax.ppermute(w, "core", SWAP) for w in own]
+    seen = glance(own + [x_rows])
+    x_rows, dy_rows, own, seen = lax.optimization_barrier((x_rows, dy_rows, own, seen))
+    own = jnp.stack(own, 0)
+    other = lax.ppermute(own, "core", SWAP)
     x = along_z(x_rows)
-    act, fac, hidden, gate_t, up_t, down_t = forward(x, own + other)
+    act, fac, hidden, gate_t, up_t, down_t, x_t = forward(x, own, other, seen)
     dy = along_z(dot(regroup, dy_rows, (1, 0)).astype(BF16))
     d_gate, d_up, dx = backward(dy, act, fac, gate_t, up_t, down_t)
     dx = along_z(dx)
 
-    whole = (dot(x, d_gate, (0, 0)), dot(x, d_up, (0, 0)), dot(hidden, dy, (0, 0)))
-
-    def pack(q):
-        low, high = q * PART, (q + 1) * PART
-        return jnp.concatenate(
-            [whole[0][:, low:high], whole[1][:, low:high], tall(whole[2][low:high])], 0
-        )
-
-    theirs = lax.ppermute(jnp.stack([pack(2), pack(3)], 0).astype(BF16), "core", SWAP)
-    sums = [(pack(q) + theirs[q].astype(F32)).astype(BF16) for q in range(2)]
-    dx, sums = lax.optimization_barrier((dx, sums))
+    sums = []
+    for q in range(2):
+        theirs, mine = gradients(x_t, dy, d_gate, d_up, hidden, q)
+        theirs = lax.ppermute(theirs, "core", SWAP)
+        sums.append((mine.astype(F32) + theirs.astype(F32)).astype(BF16))
     first = lax.ppermute(sums[0], PAIR, from_host(0))
     first, second = lax.optimization_barrier((first, sums[1]))
     back = [first, lax.ppermute(second, PAIR, from_host(1))]
     returned = in_plane(dot(regroup, dx, (0, 0)).astype(BF16))
-    even = h % 2 == 0
-    both = [jnp.where(even, back[0], back[1]), jnp.where(even, back[1], back[0])]
-    grad_gate = jnp.stack([a[:SUB] for a in both], 0)
-    grad_up = jnp.stack([a[SUB : 2 * SUB] for a in both], 0)
-    grad_down = jnp.stack([wide(a[2 * SUB :]) for a in both], 0)
-
     summed = dot(pick, returned, (0, 0)).astype(BF16)
     token_grads = jnp.concatenate([summed[i * toks : (i + 1) * toks] for i in range(HEADS)], 1)
+
+    token_grads, back = lax.optimization_barrier((token_grads, back))
+    grad_gate, grad_up, grad_down = repack(
+        unpack_kernel, odd, back, [(2, SUB, PART), (2, SUB, PART), (2, PART, SUB)]
+    )
     return (token_grads, grad_gate, grad_up, grad_down)
 
 

time: 358 us -> 321 us (0.90)
  waiting for transfers between devices: 216 us -> 185 us
  Pallas kernels: 23.1 us -> 42.6 us
  matrix products: 38.9 us -> 22.2 us
  local copies, waits for them, and re-layouts: 15.7 us -> 5.16 us
    pallas_call x0 -> x5, Pallas kernels: none -> 18 us  [the longest x2 12.8 us: gradients(): pl.pallas_call(gradient_kernel, grid=(2,), in_specs=[pl.BlockSpec((SUB, R...]
    dot_general x9 -> x6, matrix products: 38.9 us -> 22.2 us  [dot(): lax.dot_general(a, b, ((over[:1], over[1:]), ((), ())), preferred_element...]
    all_to_all x3, waiting for transfers between devices: 101 us -> 86 us  [along_z(): return lax.all_to_all(a, ('zh', 'rep'), 0, 0, tiled=True).reshape(ROWS, SUB)]
    unnamed x36 -> x38, local copies, waits for them, and re-layouts: 12.6 us -> 3.73 us
    ppermute x5, waiting for transfers between devices: 47.6 us -> 39.9 us  [the longest x2 39.8 us: on_device(): own = [lax.ppermute(pieces[q], PAIR, to_host(q)) for q in range(2)]]
    ppermute x1, waiting for transfers between devices: 22.9 us -> 15.4 us  [on_device(): first = lax.ppermute(sums[0], PAIR, from_host(0))]
    ppermute x1, waiting for transfers between devices: 32.7 us -> 28.8 us  [on_device(): back = [first, lax.ppermute(second, PAIR, from_host(1))]]
    all_to_all x3, waiting for transfers between devices: 11.6 us -> 15.3 us  [in_plane(): return lax.all_to_all(a, ('y', 'x'), 0, 0, tiled=True).reshape(ROWS, SUB)]
  transfers between devices with their start and end apart: 13 -> 13, of which waited for: 11 -> 9; matrix products, arithmetic and copies ran while one was open for 9% -> 9% of each run, Pallas kernels for 3% -> 9%
where the time goes in v4:
time: 321 us; the launch traced here: 320 us
  waiting for transfers between devices  185 us (58%)
  starting transfers between devices  53.9 us (17%)
  Pallas kernels  42.6 us (13%)
  matrix products  22.2 us (7%)
  other arithmetic  9.81 us (3%)
  local copies, waits for them, and re-layouts  5.16 us (2%)
    all_to_all x3, waiting for transfers between devices, along_z(): return lax.all_to_all(a, ('zh', 'rep'), 0, 0, tiled=True).reshape(ROWS, SUB)  86 us
    ppermute x2, waiting for transfers between devices, on_device(): own = [lax.ppermute(pieces[q], PAIR, to_host(q)) for q in range(2)]  39.8 us
    ppermute x1, waiting for transfers between devices, on_device(): back = [first, lax.ppermute(second, PAIR, from_host(1))]  28.8 us
    dot_general x6, matrix products, dot(): lax.dot_general(a, b, ((over[:1], over[1:]), ((), ())), preferred_element...  22.2 us
    all_to_all x3, starting transfers between devices, in_plane(): return lax.all_to_all(a, ('y', 'x'), 0, 0, tiled=True).reshape(ROWS, SUB)  21.6 us
    all_to_all x3, starting transfers between devices, along_z(): return lax.all_to_all(a, ('zh', 'rep'), 0, 0, tiled=True).reshape(ROWS, SUB)  18.1 us
    ppermute x1, waiting for transfers between devices, on_device(): first = lax.ppermute(sums[0], PAIR, from_host(0))  15.4 us
    all_to_all x3, waiting for transfers between devices, in_plane(): return lax.all_to_all(a, ('y', 'x'), 0, 0, tiled=True).reshape(ROWS, SUB)  15.3 us
  transfers between devices with their start and end apart: 13, of which 9 were waited for; matrix products, arithmetic and copies ran while one was open for 9% of the time, Pallas kernels for 9%

profile of v4, /device:TPU:35, one launch (start us, length us, event | category | flops | bytes accessed | tf_op | source)
XLA Modules:
  0.0 320.0 jit_solution(12212586805654352938)
XLA Ops:
  2.7 2.4 convolution_convert_fusion
  5.0 7.2 %all-to-all-start = ((bf16[16,56,1024]{2,1,0:T(8,128)(2,1)}), bf16[16,56,1024]{2,1,0:T(8,128)(2,1)}, u32[]{:S(2)}, u32[]{:S(2)}) async-start(bf16[16,56,1024]{2,1,0:T(8,128)(2,1)} %bitcast.29), calls=%async_computation | async-start | bytes 3670016 | tf_op jit(solution)/shard_map/all_to_all | solution.py:249
  12.3 2.0 shard_map.111
  14.3 6.0 %collective-permute-start = (bf16[3072,256]{1,0:T(8,128)(2,1)}, bf16[3072,256]{1,0:T(8,128)(2,1)S(1)}, u32[]{:S(2)}, u32[]{:S(2)}) collective-permute-start(bf16[3072,256]{1,0:T(8,128)(2,1)} %get-tuple-element.33), channel_id=1, source_target_pairs={{0,0},{1,128},{64,64},{65,192},{128,1},{129,129},{192,65},{193,193... | collective-permute-start | bytes 4718600 | tf_op jit(solution)/shard_map/ppermute | solution.py:227
  20.6 2.4 convolution_convert_fusion.1
  23.0 12.8 %all-to-all-done = bf16[16,56,1024]{2,1,0:T(8,128)(2,1)} async-done(((bf16[16,56,1024]{2,1,0:T(8,128)(2,1)}), bf16[16,56,1024]{2,1,0:T(8,128)(2,1)}, u32[]{:S(2)}, u32[]{:S(2)}) %all-to-all-start) | async-done | bytes 1835040 | tf_op jit(solution)/shard_map/all_to_all | solution.py:249
  35.7 7.8 %all-to-all-start.1 = ((bf16[16,56,1024]{2,1,0:T(8,128)(2,1)}), bf16[16,56,1024]{2,1,0:T(8,128)(2,1)}, u32[]{:S(2)}, u32[]{:S(2)}) async-start(bf16[16,56,1024]{2,1,0:T(8,128)(2,1)} %bitcast.10), calls=%async_computation.1 | async-start | bytes 3670016 | tf_op jit(solution)/shard_map/all_to_all | solution.py:249
  43.5 4.8 %fusion.6.c_ref = bf16[896,1024]{1,0:T(8,128)(2,1)} fusion(bf16[896,1024]{1,0:T(8,128)(2,1)} %bitcast.6, s32[896]{0:T(1024)S(1)} %fusion.47), kind=kOutput, calls=%fused_computation.12 | convolution fusion | flops 1645887488 | bytes 3673600 | tf_op jit(solution)/shard_map/dot_general | solution.py:36
  48.4 23.0 %collective-permute-done.a_ref = bf16[3072,256]{1,0:T(8,128)(2,1)S(1)} collective-permute-done((bf16[3072,256]{1,0:T(8,128)(2,1)}, bf16[3072,256]{1,0:T(8,128)(2,1)S(1)}, u32[]{:S(2)}, u32[]{:S(2)}) %collective-permute-start) | collective-permute-done | bytes 1572896 | tf_op jit(solution)/shard_map/ppermute | solution.py:227
  71.4 16.9 %collective-permute-done.1.b_ref = bf16[3072,256]{1,0:T(8,128)(2,1)S(1)} collective-permute-done((bf16[3072,256]{1,0:T(8,128)(2,1)}, bf16[3072,256]{1,0:T(8,128)(2,1)S(1)}, u32[]{:S(2)}, u32[]{:S(2)}) %collective-permute-start.1) | collective-permute-done | bytes 1572896 | tf_op jit(solution)/shard_map/ppermute | solution.py:227
  90.7 6.7 %all-to-all-start.3 = ((bf16[8,112,1024]{2,1,0:T(8,128)(2,1)}), bf16[8,112,1024]{2,1,0:T(8,128)(2,1)S(1)}, u32[]{:S(2)}, u32[]{:S(2)}) async-start(bf16[8,112,1024]{2,1,0:T(8,128)(2,1)} %bitcast.31), calls=%async_computation.3 | async-start | bytes 3670016 | tf_op jit(solution)/shard_map/all_to_all | solution.py:253
  97.3 3.5 %pad_maximum_fusion.own_ref = bf16[2,3072,256]{2,1,0:T(8,128)(2,1)} fusion(bf16[1,3072,256]{2,1,0:T(8,128)(2,1)} %bitcast.35, bf16[1,3072,256]{2,1,0:T(8,128)(2,1)S(1)} %bitcast.34), kind=kLoop, calls=%fused_computation.4 | loop fusion | flops 1572864 | bytes 6291456 | tf_op jit(solution)/shard_map/stack | solution.py:266
  102.2 4.8 %fusion.7 = bf16[896,1024]{1,0:T(8,128)(2,1)} fusion(bf16[896,1024]{1,0:T(8,128)(2,1)} %bitcast.11, s32[896]{0:T(1024)S(1)} %copy-done.14), kind=kOutput, calls=%fused_computation.13 | convolution fusion | flops 1645887488 | bytes 3673600 | tf_op jit(solution)/shard_map/dot_general | solution.py:36
  107.0 33.7 %all-to-all-done.3 = bf16[8,112,1024]{2,1,0:T(8,128)(2,1)S(1)} async-done(((bf16[8,112,1024]{2,1,0:T(8,128)(2,1)}), bf16[8,112,1024]{2,1,0:T(8,128)(2,1)S(1)}, u32[]{:S(2)}, u32[]{:S(2)}) %all-to-all-start.3) | async-done | bytes 1835040 | tf_op jit(solution)/shard_map/all_to_all | solution.py:253
  140.7 7.0 %all-to-all-start.2 = ((bf16[8,112,1024]{2,1,0:T(8,128)(2,1)}), bf16[8,112,1024]{2,1,0:T(8,128)(2,1)}, u32[]{:S(2)}, u32[]{:S(2)}) async-start(bf16[8,112,1024]{2,1,0:T(8,128)(2,1)} %bitcast.32), calls=%async_computation.2 | async-start | bytes 3670016 | tf_op jit(solution)/shard_map/all_to_all | solution.py:253
  147.7 12.9 %shard_map.113 = (f32[896,1024]{1,0:T(8,128)}, f32[896,1024]{1,0:T(8,128)}, bf16[896,1024]{1,0:T(8,128)(2,1)S(1)}, bf16[1024,1024]{1,0:T(8,128)(2,1)}, bf16[1024...) custom-call(bf16[896,1024]{1,0:T(8,128)(2,1)S(1)} %bitcast.28, ...), custom_call_target="tpu_custom_call" | custom-call | flops 3758096384 | bytes 25165824 | tf_op jit(solution)/shard_map/pallas_call | solution.py:182
  163.1 28.8 %all-to-all-done.2 = bf16[8,112,1024]{2,1,0:T(8,128)(2,1)} async-done(((bf16[8,112,1024]{2,1,0:T(8,128)(2,1)}), bf16[8,112,1024]{2,1,0:T(8,128)(2,1)}, u32[]{:S(2)}, u32[]{:S(2)}) %all-to-all-start.2) | async-done | bytes 1835040 | tf_op jit(solution)/shard_map/all_to_all | solution.py:253
  191.9 11.8 %shard_map.114 = (bf16[896,1024]{1,0:T(8,128)(2,1)}, bf16[896,1024]{1,0:T(8,128)(2,1)}, bf16[896,1024]{1,0:T(8,128)(2,1)}) custom-call(bf16[896,1024]{1,0:T(8,128)(2,1)} %bitcast.14.dy_ref, f32[896,1024]{1,0:T(8,128)} %get-tuple-element.40.act_ref, f32[896,1024]{1,0:T(8,128)} %get-tuple-element.41.fac_ref, bf16[1024,1024]{1,0:T(8,128)(2,1)} %get-tuple-element.42.gt_ref, ...), custom_call_target="tpu_custom_call" | custom-call | flops 5637144576 | bytes 20971520 | tf_op jit(solution)/shard_map/pallas_call | solution.py:207
  203.7 4.4 %all-to-all-start.4 = ((bf16[8,112,1024]{2,1,0:T(8,128)(2,1)}), bf16[8,112,1024]{2,1,0:T(8,128)(2,1)}, u32[]{:S(2)}, u32[]{:S(2)}) async-start(bf16[8,112,1024]{2,1,0:T(8,128)(2,1)} %bitcast.30), calls=%async_computation.4 | async-start | bytes 3670016 | tf_op jit(solution)/shard_map/all_to_all | solution.py:253
  208.1 5.9 %shard_map.115 = (bf16[3072,256]{1,0:T(8,128)(2,1)S(1)}, bf16[3072,256]{1,0:T(8,128)(2,1)S(1)}) custom-call(bf16[1024,896]{1,0:T(8,128)(2,1)S(1)} %copy-done.5, bf16[896,1024]{1,0:T(8,128)(2,1)} %bitcast.14.dy_ref, bf16[896,1024]{1,0:T(8,128)(2,1)} %get-tuple-element.47.dg_ref, bf16[896,1024]{1,0:T(8,128)(2,1)} %get-tuple-element.48.du_ref, ...), custom_call_target="tpu_custom_call" | custom-call | flops 2818572288 | bytes 10485760 | tf_op jit(solution)/shard_map/pallas_call | solution.py:104
  215.4 6.9 %shard_map.116 = (bf16[3072,256]{1,0:T(8,128)(2,1)}, bf16[3072,256]{1,0:T(8,128)(2,1)S(1)}) custom-call(bf16[1024,896]{1,0:T(8,128)(2,1)S(1)} %copy-done.6, bf16[896,1024]{1,0:T(8,128)(2,1)} %bitcast.14.dy_ref, bf16[896,1024]{1,0:T(8,128)(2,1)} %get-tuple-element.47.dg_ref, bf16[896,1024]{1,0:T(8,128)(2,1)} %get-tuple-element.48.du_ref, ...), custom_call_target="tpu_custom_call" | custom-call | flops 2818572288 | bytes 10485760 | tf_op jit(solution)/shard_map/pallas_call | solution.py:104
  223.9 3.6 %collective-permute-start.4 = (bf16[3072,256]{1,0:T(8,128)(2,1)}, bf16[3072,256]{1,0:T(8,128)(2,1)S(1)}, u32[]{:S(2)}, u32[]{:S(2)}) collective-permute-start(bf16[3072,256]{1,0:T(8,128)(2,1)} %add_convert_fusion.1), channel_id=1, source_target_pairs={{0,0},{128,1},{64,64},{192,65},{1,128},{129,129},{65,192},{193,193... | collective-permute-start | bytes 4718600 | tf_op jit(solution)/shard_map/ppermute | solution.py:279
  227.6 23.5 %all-to-all-done.4 = bf16[8,112,1024]{2,1,0:T(8,128)(2,1)} async-done(((bf16[8,112,1024]{2,1,0:T(8,128)(2,1)}), bf16[8,112,1024]{2,1,0:T(8,128)(2,1)}, u32[]{:S(2)}, u32[]{:S(2)}) %all-to-all-start.4) | async-done | bytes 1835040 | tf_op jit(solution)/shard_map/all_to_all | solution.py:253
  251.1 4.9 %fusion.8 = bf16[896,1024]{1,0:T(8,128)(2,1)} fusion(bf16[896,1024]{1,0:T(8,128)(2,1)} %bitcast.20, s32[896]{0:T(1024)S(1)} %copy-done.14), kind=kOutput, calls=%fused_computation.14 | convolution fusion | flops 1645887488 | bytes 3673600 | tf_op jit(solution)/shard_map/dot_general | solution.py:36
  256.1 6.7 %all-to-all-start.5 = ((bf16[16,56,1024]{2,1,0:T(8,128)(2,1)}), bf16[16,56,1024]{2,1,0:T(8,128)(2,1)}, u32[]{:S(2)}, u32[]{:S(2)}) async-start(bf16[16,56,1024]{2,1,0:T(8,128)(2,1)} %bitcast.33), calls=%async_computation.5 | async-start | bytes 3670016 | tf_op jit(solution)/shard_map/all_to_all | solution.py:249
  262.8 3.0 add_convert_fusion
  265.7 15.4 %collective-permute-done.4.first_ref = bf16[3072,256]{1,0:T(8,128)(2,1)S(1)} collective-permute-done((bf16[3072,256]{1,0:T(8,128)(2,1)}, bf16[3072,256]{1,0:T(8,128)(2,1)S(1)}, u32[]{:S(2)}, u32[]{:S(2)}) %collective-permute-start.4) | collective-permute-done | bytes 1572896 | tf_op jit(solution)/shard_map/ppermute | solution.py:279
  281.2 1.6 collective-permute-start.6
  282.8 2.6 all-to-all-done.5
  285.4 2.8 convolution_convert_fusion.2
  289.3 28.8 %collective-permute-done.6.second_ref = bf16[3072,256]{1,0:T(8,128)(2,1)S(1)} collective-permute-done((bf16[3072,256]{1,0:T(8,128)(2,1)}, bf16[3072,256]{1,0:T(8,128)(2,1)S(1)}, u32[]{:S(2)}, u32[]{:S(2)}) %collective-permute-start.6) | collective-permute-done | bytes 1572896 | tf_op jit(solution)/shard_map/ppermute | solution.py:281
  318.1 1.9 shard_map.117
  (56 shorter events, 12.7 us)
Async XLA Ops:
  1.4 19.2 %copy-start.15 = (s32[512,1]{0,1:T(1,128)}, s32[512,1]{0,1:T(1,128)S(1)}, u32[]{:S(2)}) copy-start(s32[512,1]{0,1:T(1,128)S(1)} %get-tuple-element.76) | copy-start | bytes 6148
  1.4 19.2 %copy-start.17 = (s32[512,1]{0,1:T(1,128)}, s32[512,1]{0,1:T(1,128)S(1)}, u32[]{:S(2)}) copy-start(s32[512,1]{0,1:T(1,128)S(1)} %get-tuple-element.77) | copy-start | bytes 6148
  5.0 7.2 %copy-start = (bf16[2,1024,256]{2,1,0:T(8,128)(2,1)S(1)}, bf16[2,1024,256]{2,1,0:T(8,128)(2,1)}, u32[]{:S(2)}) copy-start(bf16[2,1024,256]{2,1,0:T(8,128)(2,1)} %g_ref.1) | copy-start | bytes 3145732
  5.0 7.2 %copy-start.1 = (bf16[2,1024,256]{2,1,0:T(8,128)(2,1)S(1)}, bf16[2,1024,256]{2,1,0:T(8,128)(2,1)}, u32[]{:S(2)}) copy-start(bf16[2,1024,256]{2,1,0:T(8,128)(2,1)} %u_ref.1) | copy-start | bytes 3145732
  5.0 7.2 %copy-start.2 = (bf16[2,256,1024]{2,1,0:T(8,128)(2,1)S(1)}, bf16[2,256,1024]{2,1,0:T(8,128)(2,1)}, u32[]{:S(2)}) copy-start(bf16[2,256,1024]{2,1,0:T(8,128)(2,1)} %d_ref.1) | copy-start | bytes 3145732
  5.0 30.7 %all-to-all-start = ((bf16[16,56,1024]{2,1,0:T(8,128)(2,1)}), bf16[16,56,1024]{2,1,0:T(8,128)(2,1)}, u32[]{:S(2)}, u32[]{:S(2)}) async-start(bf16[16,56,1024]{2,1,0:T(8,128)(2,1)} %bitcast.29), calls=%async_computation | async-start | bytes 3670016 | tf_op jit(solution)/shard_map/all_to_all | solution.py:249
  12.2 8.2 %copy-start.12 = (bf16[128,4,2]{0,2,1:T(2,128)(2,1)S(1)}, bf16[128,4,2]{0,2,1:T(2,128)(2,1)}, u32[]{:S(2)}) copy-start(bf16[128,4,2]{0,2,1:T(2,128)(2,1)} %param.10) | copy-start | bytes 6148
  12.2 8.2 %copy-start.11 = (bf16[128,4096]{1,0:T(8,128)(2,1)S(1)}, bf16[128,4096]{1,0:T(8,128)(2,1)}, u32[]{:S(2)}) copy-start(bf16[128,4096]{1,0:T(8,128)(2,1)} %param.9) | copy-start | bytes 3145732
  14.3 57.1 %collective-permute-start = (bf16[3072,256]{1,0:T(8,128)(2,1)}, bf16[3072,256]{1,0:T(8,128)(2,1)S(1)}, u32[]{:S(2)}, u32[]{:S(2)}) collective-permute-start(bf16[3072,256]{1,0:T(8,128)(2,1)} %get-tuple-element.33), channel_id=1, source_target_pairs={{0,0},{1,128},{64,64},{65,192},{128,1},{129,129},{192,65},{193,193... | collective-permute-start | bytes 4718600 | tf_op jit(solution)/shard_map/ppermute | solution.py:227
  20.3 68.0 %collective-permute-start.1 = (bf16[3072,256]{1,0:T(8,128)(2,1)}, bf16[3072,256]{1,0:T(8,128)(2,1)S(1)}, u32[]{:S(2)}, u32[]{:S(2)}) collective-permute-start(bf16[3072,256]{1,0:T(8,128)(2,1)} %get-tuple-element.34), channel_id=1, source_target_pairs={{0,64},{1,192},{64,0},{65,128},{128,65},{129,193},{192,1},{193,129... | collective-permute-start | bytes 4718600 | tf_op jit(solution)/shard_map/ppermute | solution.py:227
  20.4 23.1 %copy-start.13 = (s32[896]{0:T(1024)}, s32[896]{0:T(1024)S(1)}, u32[]{:S(2)}) copy-start(s32[896]{0:T(1024)S(1)} %fusion.47) | copy-start | bytes 10756
  35.7 55.0 %all-to-all-start.1 = ((bf16[16,56,1024]{2,1,0:T(8,128)(2,1)}), bf16[16,56,1024]{2,1,0:T(8,128)(2,1)}, u32[]{:S(2)}, u32[]{:S(2)}) async-start(bf16[16,56,1024]{2,1,0:T(8,128)(2,1)} %bitcast.10), calls=%async_computation.1 | async-start | bytes 3670016 | tf_op jit(solution)/shard_map/all_to_all | solution.py:249
  71.4 16.9 %copy-start.8 = (bf16[3072,256]{1,0:T(8,128)(2,1)}, bf16[3072,256]{1,0:T(8,128)(2,1)S(1)}, u32[]{:S(2)}) copy-start(bf16[3072,256]{1,0:T(8,128)(2,1)S(1)} %collective-permute-done.a_ref) | copy-start | bytes 4718596
  88.2 1.1 copy-start.10
  90.7 6.7 %copy-start.9 = (bf16[3072,256]{1,0:T(8,128)(2,1)S(1)}, bf16[3072,256]{1,0:T(8,128)(2,1)}, u32[]{:S(2)}) copy-start(bf16[3072,256]{1,0:T(8,128)(2,1)} %copy-done.8) | copy-start | bytes 4718596
  90.7 50.0 %all-to-all-start.3 = ((bf16[8,112,1024]{2,1,0:T(8,128)(2,1)}), bf16[8,112,1024]{2,1,0:T(8,128)(2,1)S(1)}, u32[]{:S(2)}, u32[]{:S(2)}) async-start(bf16[8,112,1024]{2,1,0:T(8,128)(2,1)} %bitcast.31), calls=%async_computation.3 | async-start | bytes 3670016 | tf_op jit(solution)/shard_map/all_to_all | solution.py:253
  97.3 4.8 %copy-start.14 = (s32[896]{0:T(1024)S(1)}, s32[896]{0:T(1024)}, u32[]{:S(2)}) copy-start(s32[896]{0:T(1024)} %copy-done.13) | copy-start | bytes 10756
  100.8 46.9 %collective-permute-start.2 = (bf16[2,3072,256]{2,1,0:T(8,128)(2,1)}, bf16[2,3072,256]{2,1,0:T(8,128)(2,1)}, u32[]{:S(2)}, u32[]{:S(2)}) collective-permute-start(bf16[2,3072,256]{2,1,0:T(8,128)(2,1)} %pad_maximum_fusion.own_ref), channel_id=1, source_target_pairs={{0,1},{1,0},{2,3},{3,2},{4,5},{5,4},{6,7},{7,6},{8,9},{9,8},{10,11... | collective-permute-start | bytes 9437192 | tf_op jit(solution)/shard_map/ppermute | solution.py:267
  140.7 7.0 %copy-start.7 = (bf16[16,128]{1,0:T(8,128)(2,1)S(1)}, bf16[16,128]{1,0:T(8,128)(2,1)}, u32[]{:S(2)}) copy-start(bf16[16,128]{1,0:T(8,128)(2,1)} %shard_map.112._) | copy-start | bytes 12292
  140.7 51.2 %all-to-all-start.2 = ((bf16[8,112,1024]{2,1,0:T(8,128)(2,1)}), bf16[8,112,1024]{2,1,0:T(8,128)(2,1)}, u32[]{:S(2)}, u32[]{:S(2)}) async-start(bf16[8,112,1024]{2,1,0:T(8,128)(2,1)} %bitcast.32), calls=%async_computation.2 | async-start | bytes 3670016 | tf_op jit(solution)/shard_map/all_to_all | solution.py:253
  160.6 1.2 copy-start.3
  161.8 1.3 copy-start.4
  203.7 4.4 %copy-start.5 = (bf16[1024,896]{1,0:T(8,128)(2,1)S(1)}, bf16[1024,896]{1,0:T(8,128)(2,1)}, u32[]{:S(2)}) copy-start(bf16[1024,896]{1,0:T(8,128)(2,1)} %copy-done.4) | copy-start | bytes 5505028
  203.7 47.5 %all-to-all-start.4 = ((bf16[8,112,1024]{2,1,0:T(8,128)(2,1)}), bf16[8,112,1024]{2,1,0:T(8,128)(2,1)}, u32[]{:S(2)}, u32[]{:S(2)}) async-start(bf16[8,112,1024]{2,1,0:T(8,128)(2,1)} %bitcast.30), calls=%async_computation.4 | async-start | bytes 3670016 | tf_op jit(solution)/shard_map/all_to_all | solution.py:253
  208.1 7.3 %copy-start.6 = (bf16[1024,896]{1,0:T(8,128)(2,1)S(1)}, bf16[1024,896]{1,0:T(8,128)(2,1)}, u32[]{:S(2)}) copy-start(bf16[1024,896]{1,0:T(8,128)(2,1)} %copy-done.4) | copy-start | bytes 5505028
  214.0 8.4 %collective-permute-start.3 = (bf16[3072,256]{1,0:T(8,128)(2,1)S(1)}, bf16[3072,256]{1,0:T(8,128)(2,1)S(1)}, u32[]{:S(2)}, u32[]{:S(2)}) collective-permute-start(bf16[3072,256]{1,0:T(8,128)(2,1)S(1)} %get-tuple-element.51), channel_id=1, source_target_pairs={{0,1},{1,0},{2,3},{3,2},{4,5},{5,4},{6,7},{7,6},{8,9},{9,8},{10,11... | collective-permute-start | bytes 4718600 | tf_op jit(solution)/shard_map/ppermute | solution.py:277
  222.3 40.4 %collective-permute-start.5 = (bf16[3072,256]{1,0:T(8,128)(2,1)}, bf16[3072,256]{1,0:T(8,128)(2,1)}, u32[]{:S(2)}, u32[]{:S(2)}) collective-permute-start(bf16[3072,256]{1,0:T(8,128)(2,1)} %get-tuple-element.53), channel_id=1, source_target_pairs={{0,1},{1,0},{2,3},{3,2},{4,5},{5,4},{6,7},{7,6},{8,9},{9,8},{10,11... | collective-permute-start | bytes 4718600 | tf_op jit(solution)/shard_map/ppermute | solution.py:277
  223.9 57.3 %collective-permute-start.4 = (bf16[3072,256]{1,0:T(8,128)(2,1)}, bf16[3072,256]{1,0:T(8,128)(2,1)S(1)}, u32[]{:S(2)}, u32[]{:S(2)}) collective-permute-start(bf16[3072,256]{1,0:T(8,128)(2,1)} %add_convert_fusion.1), channel_id=1, source_target_pairs={{0,0},{128,1},{64,64},{192,65},{1,128},{129,129},{65,192},{193,193... | collective-permute-start | bytes 4718600 | tf_op jit(solution)/shard_map/ppermute | solution.py:279
  256.1 29.3 %all-to-all-start.5 = ((bf16[16,56,1024]{2,1,0:T(8,128)(2,1)}), bf16[16,56,1024]{2,1,0:T(8,128)(2,1)}, u32[]{:S(2)}, u32[]{:S(2)}) async-start(bf16[16,56,1024]{2,1,0:T(8,128)(2,1)} %bitcast.33), calls=%async_computation.5 | async-start | bytes 3670016 | tf_op jit(solution)/shard_map/all_to_all | solution.py:249
  262.7 22.6 %copy-start.16 = (s32[512,1]{0,1:T(1,128)S(1)}, s32[512,1]{0,1:T(1,128)}, u32[]{:S(2)}) copy-start(s32[512,1]{0,1:T(1,128)} %copy-done.15) | copy-start | bytes 6148
  262.7 22.6 %copy-start.18 = (s32[512,1]{0,1:T(1,128)S(1)}, s32[512,1]{0,1:T(1,128)}, u32[]{:S(2)}) copy-start(s32[512,1]{0,1:T(1,128)} %copy-done.17) | copy-start | bytes 6148
  281.2 36.9 %collective-permute-start.6 = (bf16[3072,256]{1,0:T(8,128)(2,1)}, bf16[3072,256]{1,0:T(8,128)(2,1)S(1)}, u32[]{:S(2)}, u32[]{:S(2)}) collective-permute-start(bf16[3072,256]{1,0:T(8,128)(2,1)} %add_convert_fusion), channel_id=1, source_target_pairs={{64,0},{192,1},{0,64},{128,65},{65,128},{193,129},{1,192},{129,193... | collective-permute-start | bytes 4718600 | tf_op jit(solution)/shard_map/ppermute | solution.py:281

commit v5 on v4

--- a/solution.py
+++ b/solution.py
@@ -261,8 +261,10 @@
     dy_slot = dot(pick_gate, cut(cotangent), (1, 0)).astype(BF16)
     x_rows = dot(regroup, in_plane(x_slot), (1, 0)).astype(BF16)
     dy_rows = in_plane(dy_slot)
-    seen = glance(own + [x_rows])
-    x_rows, dy_rows, own, seen = lax.optimization_barrier((x_rows, dy_rows, own, seen))
+    seen = glance([own[0], x_rows, x_rows])
+    x_rows, dy_rows, own[0], seen = lax.optimization_barrier((x_rows, dy_rows, own[0], seen))
+    seen = glance([own[1], seen, seen])
+    own[1], seen = lax.optimization_barrier((own[1], seen))
     own = jnp.stack(own, 0)
     other = lax.ppermute(own, "core", SWAP)
     x = along_z(x_rows)

time: 321 us -> 307 us (0.956)
  waiting for transfers between devices: 185 us -> 166 us
  starting transfers between devices: 53.9 us -> 57.8 us
    all_to_all x3, waiting for transfers between devices: 86 us -> 42.7 us  [along_z(): return lax.all_to_all(a, ('zh', 'rep'), 0, 0, tiled=True).reshape(ROWS, SUB)]
    ppermute x2, waiting for transfers between devices: 39.8 us -> 57.5 us  [on_device(): own = [lax.ppermute(pieces[q], PAIR, to_host(q)) for q in range(2)]]
    ppermute x1, waiting for transfers between devices: 15.4 us -> 21.2 us  [on_device(): first = lax.ppermute(sums[0], PAIR, from_host(0))]
  transfers between devices with their start and end apart: 13 -> 13, of which waited for: 9 -> 8; matrix products, arithmetic and copies ran while one was open for 9% -> 9% of each run, Pallas kernels for 9% -> 10%
where the time goes in v5:
time: 307 us; the launch traced here: 306 us
  waiting for transfers between devices  166 us (54%)
  starting transfers between devices  57.8 us (19%)
  Pallas kernels  44.5 us (14%)
  matrix products  22.2 us (7%)
  other arithmetic  9.83 us (3%)
  local copies, waits for them, and re-layouts  5.41 us (2%)
    ppermute x2, waiting for transfers between devices, on_device(): own = [lax.ppermute(pieces[q], PAIR, to_host(q)) for q in range(2)]  57.5 us
    all_to_all x3, waiting for transfers between devices, along_z(): return lax.all_to_all(a, ('zh', 'rep'), 0, 0, tiled=True).reshape(ROWS, SUB)  42.7 us
    ppermute x1, waiting for transfers between devices, on_device(): back = [first, lax.ppermute(second, PAIR, from_host(1))]  31.5 us
    dot_general x6, matrix products, dot(): lax.dot_general(a, b, ((over[:1], over[1:]), ((), ())), preferred_element...  22.2 us
    all_to_all x3, starting transfers between devices, in_plane(): return lax.all_to_all(a, ('y', 'x'), 0, 0, tiled=True).reshape(ROWS, SUB)  21.6 us
    ppermute x1, waiting for transfers between devices, on_device(): first = lax.ppermute(sums[0], PAIR, from_host(0))  21.2 us
    all_to_all x3, starting transfers between devices, along_z(): return lax.all_to_all(a, ('zh', 'rep'), 0, 0, tiled=True).reshape(ROWS, SUB)  20.1 us
    pallas_call x1, Pallas kernels, forward(): pl.pallas_call(forward_kernel, grid=(4,), in_specs=[pl.BlockSpec((ROWS, S...  13.4 us
  transfers between devices with their start and end apart: 13, of which 8 were waited for; matrix products, arithmetic and copies ran while one was open for 9% of the time, Pallas kernels for 10%

profile of v5, /device:TPU:35, one launch (start us, length us, event | category | flops | bytes accessed | tf_op | source)
XLA Modules:
  0.0 306.4 jit_solution(4906744599521141148)
XLA Ops:
  2.7 2.4 convolution_convert_fusion
  5.0 7.2 %all-to-all-start = ((bf16[16,56,1024]{2,1,0:T(8,128)(2,1)}), bf16[16,56,1024]{2,1,0:T(8,128)(2,1)}, u32[]{:S(2)}, u32[]{:S(2)}) async-start(bf16[16,56,1024]{2,1,0:T(8,128)(2,1)} %bitcast.28), calls=%async_computation | async-start | bytes 3670016 | tf_op jit(solution)/shard_map/all_to_all | solution.py:249
  12.3 2.0 shard_map.111
  14.2 6.0 %collective-permute-start = (bf16[3072,256]{1,0:T(8,128)(2,1)}, bf16[3072,256]{1,0:T(8,128)(2,1)S(1)}, u32[]{:S(2)}, u32[]{:S(2)}) collective-permute-start(bf16[3072,256]{1,0:T(8,128)(2,1)} %get-tuple-element.34), channel_id=1, source_target_pairs={{0,0},{1,128},{64,64},{65,192},{128,1},{129,129},{192,65},{193,193... | collective-permute-start | bytes 4718600 | tf_op jit(solution)/shard_map/ppermute | solution.py:227
  20.6 2.4 convolution_convert_fusion.1
  22.9 12.8 %all-to-all-done = bf16[16,56,1024]{2,1,0:T(8,128)(2,1)} async-done(((bf16[16,56,1024]{2,1,0:T(8,128)(2,1)}), bf16[16,56,1024]{2,1,0:T(8,128)(2,1)}, u32[]{:S(2)}, u32[]{:S(2)}) %all-to-all-start) | async-done | bytes 1835040 | tf_op jit(solution)/shard_map/all_to_all | solution.py:249
  35.7 7.8 %all-to-all-start.1 = ((bf16[16,56,1024]{2,1,0:T(8,128)(2,1)}), bf16[16,56,1024]{2,1,0:T(8,128)(2,1)}, u32[]{:S(2)}, u32[]{:S(2)}) async-start(bf16[16,56,1024]{2,1,0:T(8,128)(2,1)} %bitcast.10), calls=%async_computation.1 | async-start | bytes 3670016 | tf_op jit(solution)/shard_map/all_to_all | solution.py:249
  43.5 4.8 %fusion.6.b_ref.c_ref = bf16[896,1024]{1,0:T(8,128)(2,1)} fusion(bf16[896,1024]{1,0:T(8,128)(2,1)} %bitcast.6, s32[896]{0:T(1024)S(1)} %fusion.47), kind=kOutput, calls=%fused_computation.12 | convolution fusion | flops 1645887488 | bytes 3673600 | tf_op jit(solution)/shard_map/dot_general | solution.py:36
  48.4 23.0 %collective-permute-done.a_ref = bf16[3072,256]{1,0:T(8,128)(2,1)S(1)} collective-permute-done((bf16[3072,256]{1,0:T(8,128)(2,1)}, bf16[3072,256]{1,0:T(8,128)(2,1)S(1)}, u32[]{:S(2)}, u32[]{:S(2)}) %collective-permute-start) | collective-permute-done | bytes 1572896 | tf_op jit(solution)/shard_map/ppermute | solution.py:227
  73.9 7.4 %all-to-all-start.3 = ((bf16[8,112,1024]{2,1,0:T(8,128)(2,1)}), bf16[8,112,1024]{2,1,0:T(8,128)(2,1)}, u32[]{:S(2)}, u32[]{:S(2)}) async-start(bf16[8,112,1024]{2,1,0:T(8,128)(2,1)} %bitcast.15), calls=%async_computation.3 | async-start | bytes 3670016 | tf_op jit(solution)/shard_map/all_to_all | solution.py:253
  81.3 34.5 %collective-permute-done.1.a_ref = bf16[3072,256]{1,0:T(8,128)(2,1)} collective-permute-done((bf16[3072,256]{1,0:T(8,128)(2,1)}, bf16[3072,256]{1,0:T(8,128)(2,1)}, u32[]{:S(2)}, u32[]{:S(2)}) %collective-permute-start.1) | collective-permute-done | bytes 1572896 | tf_op jit(solution)/shard_map/ppermute | solution.py:227
  117.3 3.5 %pad_maximum_fusion.own_ref = bf16[2,3072,256]{2,1,0:T(8,128)(2,1)} fusion(bf16[1,3072,256]{2,1,0:T(8,128)(2,1)} %bitcast.18, bf16[1,3072,256]{2,1,0:T(8,128)(2,1)S(1)} %bitcast.31), kind=kLoop, calls=%fused_computation.4 | loop fusion | flops 1572864 | bytes 6291456 | tf_op jit(solution)/shard_map/stack | solution.py:268
  120.8 4.9 %fusion.7 = bf16[896,1024]{1,0:T(8,128)(2,1)} fusion(bf16[896,1024]{1,0:T(8,128)(2,1)} %bitcast.11, s32[896]{0:T(1024)S(1)} %copy-done.12), kind=kOutput, calls=%fused_computation.13 | convolution fusion | flops 1645887488 | bytes 3673600 | tf_op jit(solution)/shard_map/dot_general | solution.py:36
  125.7 1.9 all-to-all-done.3
  127.5 6.9 %all-to-all-start.2 = ((bf16[8,112,1024]{2,1,0:T(8,128)(2,1)}), bf16[8,112,1024]{2,1,0:T(8,128)(2,1)}, u32[]{:S(2)}, u32[]{:S(2)}) async-start(bf16[8,112,1024]{2,1,0:T(8,128)(2,1)} %bitcast.13), calls=%async_computation.2 | async-start | bytes 3670016 | tf_op jit(solution)/shard_map/all_to_all | solution.py:253
  134.4 13.4 %shard_map.114 = (f32[896,1024]{1,0:T(8,128)}, f32[896,1024]{1,0:T(8,128)}, bf16[896,1024]{1,0:T(8,128)(2,1)S(1)}, bf16[1024,1024]{1,0:T(8,128)(2,1)}, bf16[1024...) custom-call(bf16[896,1024]{1,0:T(8,128)(2,1)} %bitcast.16.x_ref, ...), custom_call_target="tpu_custom_call" | custom-call | flops 3758096384 | bytes 25165824 | tf_op jit(solution)/shard_map/pallas_call | solution.py:182
  149.1 27.0 %all-to-all-done.2 = bf16[8,112,1024]{2,1,0:T(8,128)(2,1)} async-done(((bf16[8,112,1024]{2,1,0:T(8,128)(2,1)}), bf16[8,112,1024]{2,1,0:T(8,128)(2,1)}, u32[]{:S(2)}, u32[]{:S(2)}) %all-to-all-start.2) | async-done | bytes 1835040 | tf_op jit(solution)/shard_map/all_to_all | solution.py:253
  176.1 11.8 %shard_map.115 = (bf16[896,1024]{1,0:T(8,128)(2,1)}, bf16[896,1024]{1,0:T(8,128)(2,1)}, bf16[896,1024]{1,0:T(8,128)(2,1)}) custom-call(bf16[896,1024]{1,0:T(8,128)(2,1)} %bitcast.14.dy_ref, f32[896,1024]{1,0:T(8,128)} %get-tuple-element.42.act_ref, f32[896,1024]{1,0:T(8,128)} %get-tuple-element.43.fac_ref, bf16[1024,1024]{1,0:T(8,128)(2,1)} %get-tuple-element.44.gt_ref, ...), custom_call_target="tpu_custom_call" | custom-call | flops 5637144576 | bytes 20971520 | tf_op jit(solution)/shard_map/pallas_call | solution.py:207
  187.9 5.8 %all-to-all-start.4 = ((bf16[8,112,1024]{2,1,0:T(8,128)(2,1)}), bf16[8,112,1024]{2,1,0:T(8,128)(2,1)}, u32[]{:S(2)}, u32[]{:S(2)}) async-start(bf16[8,112,1024]{2,1,0:T(8,128)(2,1)} %bitcast.29), calls=%async_computation.4 | async-start | bytes 3670016 | tf_op jit(solution)/shard_map/all_to_all | solution.py:253
  193.7 5.8 %shard_map.116 = (bf16[3072,256]{1,0:T(8,128)(2,1)S(1)}, bf16[3072,256]{1,0:T(8,128)(2,1)S(1)}) custom-call(bf16[1024,896]{1,0:T(8,128)(2,1)S(1)} %get-tuple-element.48.xt_ref, bf16[896,1024]{1,0:T(8,128)(2,1)} %bitcast.14.dy_ref, bf16[896,1024]{1,0:T(8,128)(2,1)} %get-tuple-element.49.dg_ref, bf16[896,1024]{1,0:T(8,128)(2,1)} %get-tuple-element.50.du_ref, ...), custom_call_target="tpu_custom_call" | custom-call | flops 2818572288 | bytes 10485760 | tf_op jit(solution)/shard_map/pallas_call | solution.py:104
  199.5 3.8 %collective-permute-start.3 = (bf16[3072,256]{1,0:T(8,128)(2,1)S(1)}, bf16[3072,256]{1,0:T(8,128)(2,1)S(1)}, u32[]{:S(2)}, u32[]{:S(2)}) collective-permute-start(bf16[3072,256]{1,0:T(8,128)(2,1)S(1)} %get-tuple-element.53), channel_id=1, source_target_pairs={{0,1},{1,0},{2,3},{3,2},{4,5},{5,4},{6,7},{7,6},{8,9},{9,8},{10,11... | collective-permute-start | bytes 4718600 | tf_op jit(solution)/shard_map/ppermute | solution.py:279
  204.8 6.9 %shard_map.117 = (bf16[3072,256]{1,0:T(8,128)(2,1)}, bf16[3072,256]{1,0:T(8,128)(2,1)S(1)}) custom-call(bf16[1024,896]{1,0:T(8,128)(2,1)S(1)} %copy-done.5, bf16[896,1024]{1,0:T(8,128)(2,1)} %bitcast.14.dy_ref, bf16[896,1024]{1,0:T(8,128)(2,1)} %get-tuple-element.49.dg_ref, bf16[896,1024]{1,0:T(8,128)(2,1)} %get-tuple-element.50.du_ref, ...), custom_call_target="tpu_custom_call" | custom-call | flops 2818572288 | bytes 10485760 | tf_op jit(solution)/shard_map/pallas_call | solution.py:104
  211.7 1.6 add_convert_fusion.1
  213.3 4.6 %collective-permute-start.4 = (bf16[3072,256]{1,0:T(8,128)(2,1)}, bf16[3072,256]{1,0:T(8,128)(2,1)S(1)}, u32[]{:S(2)}, u32[]{:S(2)}) collective-permute-start(bf16[3072,256]{1,0:T(8,128)(2,1)} %add_convert_fusion.1), channel_id=1, source_target_pairs={{0,0},{128,1},{64,64},{192,65},{1,128},{129,129},{65,192},{193,193... | collective-permute-start | bytes 4718600 | tf_op jit(solution)/shard_map/ppermute | solution.py:281
  217.9 13.8 %all-to-all-done.4 = bf16[8,112,1024]{2,1,0:T(8,128)(2,1)} async-done(((bf16[8,112,1024]{2,1,0:T(8,128)(2,1)}), bf16[8,112,1024]{2,1,0:T(8,128)(2,1)}, u32[]{:S(2)}, u32[]{:S(2)}) %all-to-all-start.4) | async-done | bytes 1835040 | tf_op jit(solution)/shard_map/all_to_all | solution.py:253
  231.7 4.9 %fusion.8 = bf16[896,1024]{1,0:T(8,128)(2,1)} fusion(bf16[896,1024]{1,0:T(8,128)(2,1)} %bitcast.20, s32[896]{0:T(1024)S(1)} %copy-done.12), kind=kOutput, calls=%fused_computation.14 | convolution fusion | flops 1645887488 | bytes 3673600 | tf_op jit(solution)/shard_map/dot_general | solution.py:36
  236.6 6.7 %all-to-all-start.5 = ((bf16[16,56,1024]{2,1,0:T(8,128)(2,1)}), bf16[16,56,1024]{2,1,0:T(8,128)(2,1)}, u32[]{:S(2)}, u32[]{:S(2)}) async-start(bf16[16,56,1024]{2,1,0:T(8,128)(2,1)} %bitcast.30), calls=%async_computation.5 | async-start | bytes 3670016 | tf_op jit(solution)/shard_map/all_to_all | solution.py:249
  243.3 3.0 add_convert_fusion
  246.3 21.2 %collective-permute-done.4.first_ref = bf16[3072,256]{1,0:T(8,128)(2,1)S(1)} collective-permute-done((bf16[3072,256]{1,0:T(8,128)(2,1)}, bf16[3072,256]{1,0:T(8,128)(2,1)S(1)}, u32[]{:S(2)}, u32[]{:S(2)}) %collective-permute-start.4) | collective-permute-done | bytes 1572896 | tf_op jit(solution)/shard_map/ppermute | solution.py:281
  269.1 2.8 convolution_convert_fusion.2
  273.0 31.5 %collective-permute-done.6.second_ref = bf16[3072,256]{1,0:T(8,128)(2,1)S(1)} collective-permute-done((bf16[3072,256]{1,0:T(8,128)(2,1)}, bf16[3072,256]{1,0:T(8,128)(2,1)S(1)}, u32[]{:S(2)}, u32[]{:S(2)}) %collective-permute-start.6) | collective-permute-done | bytes 1572896 | tf_op jit(solution)/shard_map/ppermute | solution.py:283
  304.4 1.9 shard_map.118
  (53 shorter events, 11.6 us)
Async XLA Ops:
  1.4 19.2 %copy-start.13 = (s32[512,1]{0,1:T(1,128)}, s32[512,1]{0,1:T(1,128)S(1)}, u32[]{:S(2)}) copy-start(s32[512,1]{0,1:T(1,128)S(1)} %get-tuple-element.78) | copy-start | bytes 6148
  1.4 19.2 %copy-start.15 = (s32[512,1]{0,1:T(1,128)}, s32[512,1]{0,1:T(1,128)S(1)}, u32[]{:S(2)}) copy-start(s32[512,1]{0,1:T(1,128)S(1)} %get-tuple-element.79) | copy-start | bytes 6148
  5.0 7.2 %copy-start = (bf16[2,1024,256]{2,1,0:T(8,128)(2,1)S(1)}, bf16[2,1024,256]{2,1,0:T(8,128)(2,1)}, u32[]{:S(2)}) copy-start(bf16[2,1024,256]{2,1,0:T(8,128)(2,1)} %g_ref.1) | copy-start | bytes 3145732
  5.0 7.2 %copy-start.1 = (bf16[2,1024,256]{2,1,0:T(8,128)(2,1)S(1)}, bf16[2,1024,256]{2,1,0:T(8,128)(2,1)}, u32[]{:S(2)}) copy-start(bf16[2,1024,256]{2,1,0:T(8,128)(2,1)} %u_ref.1) | copy-start | bytes 3145732
  5.0 7.2 %copy-start.2 = (bf16[2,256,1024]{2,1,0:T(8,128)(2,1)S(1)}, bf16[2,256,1024]{2,1,0:T(8,128)(2,1)}, u32[]{:S(2)}) copy-start(bf16[2,256,1024]{2,1,0:T(8,128)(2,1)} %d_ref.1) | copy-start | bytes 3145732
  5.0 30.7 %all-to-all-start = ((bf16[16,56,1024]{2,1,0:T(8,128)(2,1)}), bf16[16,56,1024]{2,1,0:T(8,128)(2,1)}, u32[]{:S(2)}, u32[]{:S(2)}) async-start(bf16[16,56,1024]{2,1,0:T(8,128)(2,1)} %bitcast.28), calls=%async_computation | async-start | bytes 3670016 | tf_op jit(solution)/shard_map/all_to_all | solution.py:249
  12.2 8.2 %copy-start.10 = (bf16[128,4,2]{0,2,1:T(2,128)(2,1)S(1)}, bf16[128,4,2]{0,2,1:T(2,128)(2,1)}, u32[]{:S(2)}) copy-start(bf16[128,4,2]{0,2,1:T(2,128)(2,1)} %param.10) | copy-start | bytes 6148
  12.2 8.2 %copy-start.9 = (bf16[128,4096]{1,0:T(8,128)(2,1)S(1)}, bf16[128,4096]{1,0:T(8,128)(2,1)}, u32[]{:S(2)}) copy-start(bf16[128,4096]{1,0:T(8,128)(2,1)} %param.9) | copy-start | bytes 3145732
  14.2 57.1 %collective-permute-start = (bf16[3072,256]{1,0:T(8,128)(2,1)}, bf16[3072,256]{1,0:T(8,128)(2,1)S(1)}, u32[]{:S(2)}, u32[]{:S(2)}) collective-permute-start(bf16[3072,256]{1,0:T(8,128)(2,1)} %get-tuple-element.34), channel_id=1, source_target_pairs={{0,0},{1,128},{64,64},{65,192},{128,1},{129,129},{192,65},{193,193... | collective-permute-start | bytes 4718600 | tf_op jit(solution)/shard_map/ppermute | solution.py:227
  20.3 95.6 %collective-permute-start.1 = (bf16[3072,256]{1,0:T(8,128)(2,1)}, bf16[3072,256]{1,0:T(8,128)(2,1)}, u32[]{:S(2)}, u32[]{:S(2)}) collective-permute-start(bf16[3072,256]{1,0:T(8,128)(2,1)} %get-tuple-element.38), channel_id=1, source_target_pairs={{0,64},{1,192},{64,0},{65,128},{128,65},{129,193},{192,1},{193,129... | collective-permute-start | bytes 4718600 | tf_op jit(solution)/shard_map/ppermute | solution.py:227
  20.4 23.1 %copy-start.11 = (s32[896]{0:T(1024)}, s32[896]{0:T(1024)S(1)}, u32[]{:S(2)}) copy-start(s32[896]{0:T(1024)S(1)} %fusion.47) | copy-start | bytes 10756
  35.7 38.1 %all-to-all-start.1 = ((bf16[16,56,1024]{2,1,0:T(8,128)(2,1)}), bf16[16,56,1024]{2,1,0:T(8,128)(2,1)}, u32[]{:S(2)}, u32[]{:S(2)}) async-start(bf16[16,56,1024]{2,1,0:T(8,128)(2,1)} %bitcast.10), calls=%async_computation.1 | async-start | bytes 3670016 | tf_op jit(solution)/shard_map/all_to_all | solution.py:249
  71.4 1.2 copy-start.7
  73.9 53.7 %all-to-all-start.3 = ((bf16[8,112,1024]{2,1,0:T(8,128)(2,1)}), bf16[8,112,1024]{2,1,0:T(8,128)(2,1)}, u32[]{:S(2)}, u32[]{:S(2)}) async-start(bf16[8,112,1024]{2,1,0:T(8,128)(2,1)} %bitcast.15), calls=%async_computation.3 | async-start | bytes 3670016 | tf_op jit(solution)/shard_map/all_to_all | solution.py:253
  115.8 1.4 copy-start.8
  117.3 3.5 %copy-start.12 = (s32[896]{0:T(1024)S(1)}, s32[896]{0:T(1024)}, u32[]{:S(2)}) copy-start(s32[896]{0:T(1024)} %copy-done.11) | copy-start | bytes 10756
  120.8 13.7 %collective-permute-start.2 = (bf16[2,3072,256]{2,1,0:T(8,128)(2,1)}, bf16[2,3072,256]{2,1,0:T(8,128)(2,1)}, u32[]{:S(2)}, u32[]{:S(2)}) collective-permute-start(bf16[2,3072,256]{2,1,0:T(8,128)(2,1)} %pad_maximum_fusion.own_ref), channel_id=1, source_target_pairs={{0,1},{1,0},{2,3},{3,2},{4,5},{5,4},{6,7},{7,6},{8,9},{9,8},{10,11... | collective-permute-start | bytes 9437192 | tf_op jit(solution)/shard_map/ppermute | solution.py:269
  127.5 6.9 %copy-start.6 = (bf16[16,128]{1,0:T(8,128)(2,1)S(1)}, bf16[16,128]{1,0:T(8,128)(2,1)}, u32[]{:S(2)}) copy-start(bf16[16,128]{1,0:T(8,128)(2,1)} %shard_map.113._) | copy-start | bytes 12292
  127.5 48.6 %all-to-all-start.2 = ((bf16[8,112,1024]{2,1,0:T(8,128)(2,1)}), bf16[8,112,1024]{2,1,0:T(8,128)(2,1)}, u32[]{:S(2)}, u32[]{:S(2)}) async-start(bf16[8,112,1024]{2,1,0:T(8,128)(2,1)} %bitcast.13), calls=%async_computation.2 | async-start | bytes 3670016 | tf_op jit(solution)/shard_map/all_to_all | solution.py:253
  147.9 1.2 copy-start.3
  149.1 44.6 %copy-start.4 = (bf16[1024,896]{1,0:T(8,128)(2,1)}, bf16[1024,896]{1,0:T(8,128)(2,1)S(1)}, u32[]{:S(2)}) copy-start(bf16[1024,896]{1,0:T(8,128)(2,1)S(1)} %get-tuple-element.48.xt_ref) | copy-start | bytes 5505028
  187.9 43.8 %all-to-all-start.4 = ((bf16[8,112,1024]{2,1,0:T(8,128)(2,1)}), bf16[8,112,1024]{2,1,0:T(8,128)(2,1)}, u32[]{:S(2)}, u32[]{:S(2)}) async-start(bf16[8,112,1024]{2,1,0:T(8,128)(2,1)} %bitcast.29), calls=%async_computation.4 | async-start | bytes 3670016 | tf_op jit(solution)/shard_map/all_to_all | solution.py:253
  199.5 12.2 %collective-permute-start.3 = (bf16[3072,256]{1,0:T(8,128)(2,1)S(1)}, bf16[3072,256]{1,0:T(8,128)(2,1)S(1)}, u32[]{:S(2)}, u32[]{:S(2)}) collective-permute-start(bf16[3072,256]{1,0:T(8,128)(2,1)S(1)} %get-tuple-element.53), channel_id=1, source_target_pairs={{0,1},{1,0},{2,3},{3,2},{4,5},{5,4},{6,7},{7,6},{8,9},{9,8},{10,11... | collective-permute-start | bytes 4718600 | tf_op jit(solution)/shard_map/ppermute | solution.py:279
  203.3 1.5 copy-start.5
  211.7 31.6 %collective-permute-start.5 = (bf16[3072,256]{1,0:T(8,128)(2,1)}, bf16[3072,256]{1,0:T(8,128)(2,1)}, u32[]{:S(2)}, u32[]{:S(2)}) collective-permute-start(bf16[3072,256]{1,0:T(8,128)(2,1)} %get-tuple-element.55), channel_id=1, source_target_pairs={{0,1},{1,0},{2,3},{3,2},{4,5},{5,4},{6,7},{7,6},{8,9},{9,8},{10,11... | collective-permute-start | bytes 4718600 | tf_op jit(solution)/shard_map/ppermute | solution.py:279
  213.3 54.2 %collective-permute-start.4 = (bf16[3072,256]{1,0:T(8,128)(2,1)}, bf16[3072,256]{1,0:T(8,128)(2,1)S(1)}, u32[]{:S(2)}, u32[]{:S(2)}) collective-permute-start(bf16[3072,256]{1,0:T(8,128)(2,1)} %add_convert_fusion.1), channel_id=1, source_target_pairs={{0,0},{128,1},{64,64},{192,65},{1,128},{129,129},{65,192},{193,193... | collective-permute-start | bytes 4718600 | tf_op jit(solution)/shard_map/ppermute | solution.py:281
  236.6 32.4 %all-to-all-start.5 = ((bf16[16,56,1024]{2,1,0:T(8,128)(2,1)}), bf16[16,56,1024]{2,1,0:T(8,128)(2,1)}, u32[]{:S(2)}, u32[]{:S(2)}) async-start(bf16[16,56,1024]{2,1,0:T(8,128)(2,1)} %bitcast.30), calls=%async_computation.5 | async-start | bytes 3670016 | tf_op jit(solution)/shard_map/all_to_all | solution.py:249
  243.3 25.8 %copy-start.14 = (s32[512,1]{0,1:T(1,128)S(1)}, s32[512,1]{0,1:T(1,128)}, u32[]{:S(2)}) copy-start(s32[512,1]{0,1:T(1,128)} %copy-done.13) | copy-start | bytes 6148
  243.3 25.8 %copy-start.16 = (s32[512,1]{0,1:T(1,128)S(1)}, s32[512,1]{0,1:T(1,128)}, u32[]{:S(2)}) copy-start(s32[512,1]{0,1:T(1,128)} %copy-done.15) | copy-start | bytes 6148
  267.5 36.9 %collective-permute-start.6 = (bf16[3072,256]{1,0:T(8,128)(2,1)}, bf16[3072,256]{1,0:T(8,128)(2,1)S(1)}, u32[]{:S(2)}, u32[]{:S(2)}) collective-permute-start(bf16[3072,256]{1,0:T(8,128)(2,1)} %add_convert_fusion), channel_id=1, source_target_pairs={{64,0},{192,1},{0,64},{128,65},{65,128},{193,129},{1,192},{129,193... | collective-permute-start | bytes 4718600 | tf_op jit(solution)/shard_map/ppermute | solution.py:283

commit v6 on v5

--- a/solution.py
+++ b/solution.py
@@ -37,7 +37,7 @@
 
 
 def forward_kernel(
-    x_ref, own_ref, other_ref, _, act_ref, fac_ref, hid_ref, gt_ref, ut_ref, dt_ref, xt_ref, w_ref
+    x_ref, own_ref, other_ref, _, act_ref, fac_ref, hid_ref, gu_ref, dt_ref, xt_ref, w_ref
 ):
     j = pl.program_id(0)
     for i in range(4):
@@ -63,19 +63,22 @@
         return 0
 
     lax.fori_loop(0, ROWS // STEP, step, 0)
-    gt_ref[...] = w_ref[:SUB, :].T
-    ut_ref[...] = w_ref[SUB : 2 * SUB, :].T
+    gu_ref[0] = w_ref[:SUB, :].T
+    gu_ref[1] = w_ref[SUB : 2 * SUB, :].T
     for f in range(SUB // PART):
         low = 2 * SUB + f * PART
         dt_ref[f * PART : (f + 1) * PART, :] = w_ref[low : low + PART, :].T
 
 
-def backward_kernel(dy_ref, act_ref, fac_ref, gt_ref, ut_ref, dt_ref, dg_ref, du_ref, dx_ref):
+def backward_kernel(dy_ref, act_ref, fac_ref, gu_ref, dt_ref, dg_ref, du_ref, dx_ref, both_ref):
     dh = dot(dy_ref[...], dt_ref[...], (1, 0))
-    du_ref[...] = (dh * act_ref[...]).astype(BF16)
-    dg_ref[...] = (dh * fac_ref[...]).astype(BF16)
-    dx = dot(dg_ref[...], gt_ref[...], (1, 0)) + dot(du_ref[...], ut_ref[...], (1, 0))
-    dx_ref[...] = dx.astype(BF16)
+    d_gate = (dh * fac_ref[...]).astype(BF16)
+    d_up = (dh * act_ref[...]).astype(BF16)
+    dg_ref[...] = d_gate
+    du_ref[...] = d_up
+    both_ref[:, :SUB] = d_gate
+    both_ref[:, SUB:] = d_up
+    dx_ref[...] = dot(both_ref[...], gu_ref[...].reshape(2 * SUB, SUB), (1, 0)).astype(BF16)
 
 
 def gradient_kernel(xt_ref, dy_ref, dg_ref, du_ref, hid_ref, theirs_ref, mine_ref):
@@ -188,10 +191,10 @@
         + [pl.BlockSpec((2, 3 * SUB, PART), lambda j: (0, 0, 0))] * 2
         + [pl.BlockSpec((16, 128), lambda j: (0, 0))],
         out_specs=[columns] * 3
-        + [pl.BlockSpec((PART, SUB), lambda j: (j, 0))] * 2
+        + [pl.BlockSpec((2, PART, SUB), lambda j: (0, j, 0))]
         + [pl.BlockSpec((SUB, PART), lambda j: (0, j)), pl.BlockSpec((SUB, ROWS), lambda j: (0, 0))],
         out_shape=[float_out, float_out, jax.ShapeDtypeStruct((ROWS, SUB), BF16)]
-        + [square] * 3
+        + [jax.ShapeDtypeStruct((2, SUB, SUB), BF16), square]
         + [jax.ShapeDtypeStruct((SUB, ROWS), BF16)],
         scratch_shapes=[pltpu.VMEM((3 * SUB, PART), BF16)],
         compiler_params=params(),
@@ -201,20 +204,21 @@
     )(x, own, other, seen)
 
 
-def backward(dy, act, fac, gate_t, up_t, down_t):
+def backward(dy, act, fac, both_t, down_t):
     some = pl.BlockSpec((STEP, SUB), lambda i: (i, 0))
     square = pl.BlockSpec((SUB, SUB), lambda i: (0, 0))
     return pl.pallas_call(
         backward_kernel,
         grid=(ROWS // STEP,),
-        in_specs=[some] * 3 + [square] * 3,
+        in_specs=[some] * 3 + [pl.BlockSpec((2, SUB, SUB), lambda i: (0, 0, 0)), square],
         out_specs=[some] * 3,
         out_shape=[jax.ShapeDtypeStruct((ROWS, SUB), BF16)] * 3,
+        scratch_shapes=[pltpu.VMEM((STEP, 2 * SUB), BF16)],
         compiler_params=params(60),
         cost_estimate=pl.CostEstimate(
             flops=6 * ROWS * SUB * SUB, bytes_accessed=20 * 2**20, transcendentals=0
         ),
-    )(dy, act, fac, gate_t, up_t, down_t)
+    )(dy, act, fac, both_t, down_t)
 
 
 def on_device(tokens, cotangent, gates, expert_ids, slots, w_gate, w_up, w_down):
@@ -268,9 +272,9 @@
     own = jnp.stack(own, 0)
     other = lax.ppermute(own, "core", SWAP)
     x = along_z(x_rows)
-    act, fac, hidden, gate_t, up_t, down_t, x_t = forward(x, own, other, seen)
+    act, fac, hidden, both_t, down_t, x_t = forward(x, own, other, seen)
     dy = along_z(dot(regroup, dy_rows, (1, 0)).astype(BF16))
-    d_gate, d_up, dx = backward(dy, act, fac, gate_t, up_t, down_t)
+    d_gate, d_up, dx = backward(dy, act, fac, both_t, down_t)
     dx = along_z(dx)
 
     sums = []

time: 307 us -> 307 us (level)
  no operation moved by 1% of the time
where the time goes in v6:
time: 307 us; the launch traced here: 306 us
  waiting for transfers between devices  166 us (54%)
  starting transfers between devices  57.8 us (19%)
  Pallas kernels  44.7 us (15%)
  matrix products  22.2 us (7%)
  other arithmetic  9.72 us (3%)
  local copies, waits for them, and re-layouts  5.43 us (2%)
    ppermute x2, waiting for transfers between devices, on_device(): own = [lax.ppermute(pieces[q], PAIR, to_host(q)) for q in range(2)]  57.3 us
    all_to_all x3, waiting for transfers between devices, along_z(): return lax.all_to_all(a, ('zh', 'rep'), 0, 0, tiled=True).reshape(ROWS, SUB)  42.9 us
    ppermute x1, waiting for transfers between devices, on_device(): back = [first, lax.ppermute(second, PAIR, from_host(1))]  31.5 us
    dot_general x6, matrix products, dot(): lax.dot_general(a, b, ((over[:1], over[1:]), ((), ())), preferred_element...  22.2 us
    all_to_all x3, starting transfers between devices, in_plane(): return lax.all_to_all(a, ('y', 'x'), 0, 0, tiled=True).reshape(ROWS, SUB)  21.7 us
    ppermute x1, waiting for transfers between devices, on_device(): first = lax.ppermute(sums[0], PAIR, from_host(0))  21.2 us
    all_to_all x3, starting transfers between devices, along_z(): return lax.all_to_all(a, ('zh', 'rep'), 0, 0, tiled=True).reshape(ROWS, SUB)  20.1 us
    pallas_call x1, Pallas kernels, forward(): pl.pallas_call(forward_kernel, grid=(4,), in_specs=[pl.BlockSpec((ROWS, S...  13.5 us
  transfers between devices with their start and end apart: 13, of which 8 were waited for; matrix products, arithmetic and copies ran while one was open for 9% of the time, Pallas kernels for 10%

profile of v6, /device:TPU:35, one launch (start us, length us, event | category | flops | bytes accessed | tf_op | source)
XLA Modules:
  0.0 306.4 jit_solution(9409520698334318353)
XLA Ops:
  2.7 2.4 convolution_convert_fusion
  5.0 7.2 %all-to-all-start = ((bf16[16,56,1024]{2,1,0:T(8,128)(2,1)}), bf16[16,56,1024]{2,1,0:T(8,128)(2,1)}, u32[]{:S(2)}, u32[]{:S(2)}) async-start(bf16[16,56,1024]{2,1,0:T(8,128)(2,1)} %bitcast.28), calls=%async_computation | async-start | bytes 3670016 | tf_op jit(solution)/shard_map/all_to_all | solution.py:253
  12.3 1.9 shard_map.111
  14.2 6.0 %collective-permute-start = (bf16[3072,256]{1,0:T(8,128)(2,1)}, bf16[3072,256]{1,0:T(8,128)(2,1)S(1)}, u32[]{:S(2)}, u32[]{:S(2)}) collective-permute-start(bf16[3072,256]{1,0:T(8,128)(2,1)} %get-tuple-element.33), channel_id=1, source_target_pairs={{0,0},{1,128},{64,64},{65,192},{128,1},{129,129},{192,65},{193,193... | collective-permute-start | bytes 4718600 | tf_op jit(solution)/shard_map/ppermute | solution.py:231
  20.5 2.4 convolution_convert_fusion.1
  22.9 12.9 %all-to-all-done = bf16[16,56,1024]{2,1,0:T(8,128)(2,1)} async-done(((bf16[16,56,1024]{2,1,0:T(8,128)(2,1)}), bf16[16,56,1024]{2,1,0:T(8,128)(2,1)}, u32[]{:S(2)}, u32[]{:S(2)}) %all-to-all-start) | async-done | bytes 1835040 | tf_op jit(solution)/shard_map/all_to_all | solution.py:253
  35.7 7.8 %all-to-all-start.1 = ((bf16[16,56,1024]{2,1,0:T(8,128)(2,1)}), bf16[16,56,1024]{2,1,0:T(8,128)(2,1)}, u32[]{:S(2)}, u32[]{:S(2)}) async-start(bf16[16,56,1024]{2,1,0:T(8,128)(2,1)} %bitcast.10), calls=%async_computation.1 | async-start | bytes 3670016 | tf_op jit(solution)/shard_map/all_to_all | solution.py:253
  43.5 4.9 %fusion.6.b_ref.c_ref = bf16[896,1024]{1,0:T(8,128)(2,1)} fusion(bf16[896,1024]{1,0:T(8,128)(2,1)} %bitcast.6, s32[896]{0:T(1024)S(1)} %fusion.47), kind=kOutput, calls=%fused_computation.12 | convolution fusion | flops 1645887488 | bytes 3673600 | tf_op jit(solution)/shard_map/dot_general | solution.py:36
  48.4 22.9 %collective-permute-done.a_ref = bf16[3072,256]{1,0:T(8,128)(2,1)S(1)} collective-permute-done((bf16[3072,256]{1,0:T(8,128)(2,1)}, bf16[3072,256]{1,0:T(8,128)(2,1)S(1)}, u32[]{:S(2)}, u32[]{:S(2)}) %collective-permute-start) | collective-permute-done | bytes 1572896 | tf_op jit(solution)/shard_map/ppermute | solution.py:231
  73.8 7.4 %all-to-all-start.3 = ((bf16[8,112,1024]{2,1,0:T(8,128)(2,1)}), bf16[8,112,1024]{2,1,0:T(8,128)(2,1)}, u32[]{:S(2)}, u32[]{:S(2)}) async-start(bf16[8,112,1024]{2,1,0:T(8,128)(2,1)} %bitcast.15), calls=%async_computation.3 | async-start | bytes 3670016 | tf_op jit(solution)/shard_map/all_to_all | solution.py:257
  81.3 34.4 %collective-permute-done.1.a_ref = bf16[3072,256]{1,0:T(8,128)(2,1)} collective-permute-done((bf16[3072,256]{1,0:T(8,128)(2,1)}, bf16[3072,256]{1,0:T(8,128)(2,1)}, u32[]{:S(2)}, u32[]{:S(2)}) %collective-permute-start.1) | collective-permute-done | bytes 1572896 | tf_op jit(solution)/shard_map/ppermute | solution.py:231
  117.1 3.4 %pad_maximum_fusion.own_ref = bf16[2,3072,256]{2,1,0:T(8,128)(2,1)} fusion(bf16[1,3072,256]{2,1,0:T(8,128)(2,1)} %bitcast.18, bf16[1,3072,256]{2,1,0:T(8,128)(2,1)S(1)} %bitcast.31), kind=kLoop, calls=%fused_computation.4 | loop fusion | flops 1572864 | bytes 6291456 | tf_op jit(solution)/shard_map/stack | solution.py:272
  120.5 4.9 %fusion.7 = bf16[896,1024]{1,0:T(8,128)(2,1)} fusion(bf16[896,1024]{1,0:T(8,128)(2,1)} %bitcast.11, s32[896]{0:T(1024)S(1)} %copy-done.12), kind=kOutput, calls=%fused_computation.13 | convolution fusion | flops 1645887488 | bytes 3673600 | tf_op jit(solution)/shard_map/dot_general | solution.py:36
  125.4 2.1 all-to-all-done.3
  127.5 6.9 %all-to-all-start.2 = ((bf16[8,112,1024]{2,1,0:T(8,128)(2,1)}), bf16[8,112,1024]{2,1,0:T(8,128)(2,1)}, u32[]{:S(2)}, u32[]{:S(2)}) async-start(bf16[8,112,1024]{2,1,0:T(8,128)(2,1)} %bitcast.13), calls=%async_computation.2 | async-start | bytes 3670016 | tf_op jit(solution)/shard_map/all_to_all | solution.py:257
  134.4 13.5 %shard_map.114 = (f32[896,1024]{1,0:T(8,128)}, f32[896,1024]{1,0:T(8,128)}, bf16[896,1024]{1,0:T(8,128)(2,1)S(1)}, bf16[2,1024,1024]{2,1,0:T(8,128)(2,1)}, bf16[...) custom-call(bf16[896,1024]{1,0:T(8,128)(2,1)} %bitcast.16.x_ref, bf16[2,3072,256]{2,1,0:T(8,128)(2,1)} %pad_maximum_fusion.own_ref, ...), custom_call_target="tpu_custom_call" | custom-call | flops 3758096384 | bytes 25165824 | tf_op jit(solution)/shard_map/pallas_call | solution.py:185
  149.1 26.9 %all-to-all-done.2 = bf16[8,112,1024]{2,1,0:T(8,128)(2,1)} async-done(((bf16[8,112,1024]{2,1,0:T(8,128)(2,1)}), bf16[8,112,1024]{2,1,0:T(8,128)(2,1)}, u32[]{:S(2)}, u32[]{:S(2)}) %all-to-all-start.2) | async-done | bytes 1835040 | tf_op jit(solution)/shard_map/all_to_all | solution.py:257
  176.1 11.9 %shard_map.115 = (bf16[896,1024]{1,0:T(8,128)(2,1)}, bf16[896,1024]{1,0:T(8,128)(2,1)}, bf16[896,1024]{1,0:T(8,128)(2,1)}) custom-call(bf16[896,1024]{1,0:T(8,128)(2,1)} %bitcast.14.dy_ref, f32[896,1024]{1,0:T(8,128)} %get-tuple-element.41.act_ref, f32[896,1024]{1,0:T(8,128)} %get-tuple-element.42.fac_ref, bf16[2,1024,1024]{2,1,0:T(8,128)(2,1)} %get-tuple-element.43.gu_ref, ...), custom_call_target="tpu_custom_call" | custom-call | flops 5637144576 | bytes 20971520 | tf_op jit(solution)/shard_map/pallas_call | solution.py:210
  188.0 5.8 %all-to-all-start.4 = ((bf16[8,112,1024]{2,1,0:T(8,128)(2,1)}), bf16[8,112,1024]{2,1,0:T(8,128)(2,1)}, u32[]{:S(2)}, u32[]{:S(2)}) async-start(bf16[8,112,1024]{2,1,0:T(8,128)(2,1)} %bitcast.29), calls=%async_computation.4 | async-start | bytes 3670016 | tf_op jit(solution)/shard_map/all_to_all | solution.py:257
  193.8 5.8 %shard_map.116 = (bf16[3072,256]{1,0:T(8,128)(2,1)S(1)}, bf16[3072,256]{1,0:T(8,128)(2,1)S(1)}) custom-call(bf16[1024,896]{1,0:T(8,128)(2,1)S(1)} %get-tuple-element.46.xt_ref, bf16[896,1024]{1,0:T(8,128)(2,1)} %bitcast.14.dy_ref, bf16[896,1024]{1,0:T(8,128)(2,1)} %get-tuple-element.47.dg_ref, bf16[896,1024]{1,0:T(8,128)(2,1)} %get-tuple-element.48.du_ref, ...), custom_call_target="tpu_custom_call" | custom-call | flops 2818572288 | bytes 10485760 | tf_op jit(solution)/shard_map/pallas_call | solution.py:107
  199.5 3.8 %collective-permute-start.3 = (bf16[3072,256]{1,0:T(8,128)(2,1)S(1)}, bf16[3072,256]{1,0:T(8,128)(2,1)S(1)}, u32[]{:S(2)}, u32[]{:S(2)}) collective-permute-start(bf16[3072,256]{1,0:T(8,128)(2,1)S(1)} %get-tuple-element.51), channel_id=1, source_target_pairs={{0,1},{1,0},{2,3},{3,2},{4,5},{5,4},{6,7},{7,6},{8,9},{9,8},{10,11... | collective-permute-start | bytes 4718600 | tf_op jit(solution)/shard_map/ppermute | solution.py:283
  204.8 6.9 %shard_map.117 = (bf16[3072,256]{1,0:T(8,128)(2,1)}, bf16[3072,256]{1,0:T(8,128)(2,1)S(1)}) custom-call(bf16[1024,896]{1,0:T(8,128)(2,1)S(1)} %copy-done.5, bf16[896,1024]{1,0:T(8,128)(2,1)} %bitcast.14.dy_ref, bf16[896,1024]{1,0:T(8,128)(2,1)} %get-tuple-element.47.dg_ref, bf16[896,1024]{1,0:T(8,128)(2,1)} %get-tuple-element.48.du_ref, ...), custom_call_target="tpu_custom_call" | custom-call | flops 2818572288 | bytes 10485760 | tf_op jit(solution)/shard_map/pallas_call | solution.py:107
  211.7 1.5 add_convert_fusion.1
  213.3 4.6 %collective-permute-start.4 = (bf16[3072,256]{1,0:T(8,128)(2,1)}, bf16[3072,256]{1,0:T(8,128)(2,1)S(1)}, u32[]{:S(2)}, u32[]{:S(2)}) collective-permute-start(bf16[3072,256]{1,0:T(8,128)(2,1)} %add_convert_fusion.1), channel_id=1, source_target_pairs={{0,0},{128,1},{64,64},{192,65},{1,128},{129,129},{65,192},{193,193... | collective-permute-start | bytes 4718600 | tf_op jit(solution)/shard_map/ppermute | solution.py:285
  217.9 13.8 %all-to-all-done.4 = bf16[8,112,1024]{2,1,0:T(8,128)(2,1)} async-done(((bf16[8,112,1024]{2,1,0:T(8,128)(2,1)}), bf16[8,112,1024]{2,1,0:T(8,128)(2,1)}, u32[]{:S(2)}, u32[]{:S(2)}) %all-to-all-start.4) | async-done | bytes 1835040 | tf_op jit(solution)/shard_map/all_to_all | solution.py:257
  231.7 4.9 %fusion.8 = bf16[896,1024]{1,0:T(8,128)(2,1)} fusion(bf16[896,1024]{1,0:T(8,128)(2,1)} %bitcast.20, s32[896]{0:T(1024)S(1)} %copy-done.12), kind=kOutput, calls=%fused_computation.14 | convolution fusion | flops 1645887488 | bytes 3673600 | tf_op jit(solution)/shard_map/dot_general | solution.py:36
  236.6 6.7 %all-to-all-start.5 = ((bf16[16,56,1024]{2,1,0:T(8,128)(2,1)}), bf16[16,56,1024]{2,1,0:T(8,128)(2,1)}, u32[]{:S(2)}, u32[]{:S(2)}) async-start(bf16[16,56,1024]{2,1,0:T(8,128)(2,1)} %bitcast.30), calls=%async_computation.5 | async-start | bytes 3670016 | tf_op jit(solution)/shard_map/all_to_all | solution.py:253
  243.3 3.0 add_convert_fusion
  246.3 21.2 %collective-permute-done.4.first_ref = bf16[3072,256]{1,0:T(8,128)(2,1)S(1)} collective-permute-done((bf16[3072,256]{1,0:T(8,128)(2,1)}, bf16[3072,256]{1,0:T(8,128)(2,1)S(1)}, u32[]{:S(2)}, u32[]{:S(2)}) %collective-permute-start.4) | collective-permute-done | bytes 1572896 | tf_op jit(solution)/shard_map/ppermute | solution.py:285
  269.1 2.8 convolution_convert_fusion.2
  273.0 31.5 %collective-permute-done.6.second_ref = bf16[3072,256]{1,0:T(8,128)(2,1)S(1)} collective-permute-done((bf16[3072,256]{1,0:T(8,128)(2,1)}, bf16[3072,256]{1,0:T(8,128)(2,1)S(1)}, u32[]{:S(2)}, u32[]{:S(2)}) %collective-permute-start.6) | collective-permute-done | bytes 1572896 | tf_op jit(solution)/shard_map/ppermute | solution.py:287
  304.5 1.9 shard_map.118
  (53 shorter events, 11.6 us)
Async XLA Ops:
  1.4 19.1 %copy-start.13 = (s32[512,1]{0,1:T(1,128)}, s32[512,1]{0,1:T(1,128)S(1)}, u32[]{:S(2)}) copy-start(s32[512,1]{0,1:T(1,128)S(1)} %get-tuple-element.76) | copy-start | bytes 6148
  1.4 19.1 %copy-start.15 = (s32[512,1]{0,1:T(1,128)}, s32[512,1]{0,1:T(1,128)S(1)}, u32[]{:S(2)}) copy-start(s32[512,1]{0,1:T(1,128)S(1)} %get-tuple-element.77) | copy-start | bytes 6148
  5.0 7.2 %copy-start = (bf16[2,1024,256]{2,1,0:T(8,128)(2,1)S(1)}, bf16[2,1024,256]{2,1,0:T(8,128)(2,1)}, u32[]{:S(2)}) copy-start(bf16[2,1024,256]{2,1,0:T(8,128)(2,1)} %g_ref.1) | copy-start | bytes 3145732
  5.0 7.2 %copy-start.1 = (bf16[2,1024,256]{2,1,0:T(8,128)(2,1)S(1)}, bf16[2,1024,256]{2,1,0:T(8,128)(2,1)}, u32[]{:S(2)}) copy-start(bf16[2,1024,256]{2,1,0:T(8,128)(2,1)} %u_ref.1) | copy-start | bytes 3145732
  5.0 7.2 %copy-start.2 = (bf16[2,256,1024]{2,1,0:T(8,128)(2,1)S(1)}, bf16[2,256,1024]{2,1,0:T(8,128)(2,1)}, u32[]{:S(2)}) copy-start(bf16[2,256,1024]{2,1,0:T(8,128)(2,1)} %d_ref.1) | copy-start | bytes 3145732
  5.0 30.7 %all-to-all-start = ((bf16[16,56,1024]{2,1,0:T(8,128)(2,1)}), bf16[16,56,1024]{2,1,0:T(8,128)(2,1)}, u32[]{:S(2)}, u32[]{:S(2)}) async-start(bf16[16,56,1024]{2,1,0:T(8,128)(2,1)} %bitcast.28), calls=%async_computation | async-start | bytes 3670016 | tf_op jit(solution)/shard_map/all_to_all | solution.py:253
  12.2 8.1 %copy-start.10 = (bf16[128,4,2]{0,2,1:T(2,128)(2,1)S(1)}, bf16[128,4,2]{0,2,1:T(2,128)(2,1)}, u32[]{:S(2)}) copy-start(bf16[128,4,2]{0,2,1:T(2,128)(2,1)} %param.10) | copy-start | bytes 6148
  12.2 8.1 %copy-start.9 = (bf16[128,4096]{1,0:T(8,128)(2,1)S(1)}, bf16[128,4096]{1,0:T(8,128)(2,1)}, u32[]{:S(2)}) copy-start(bf16[128,4096]{1,0:T(8,128)(2,1)} %param.9) | copy-start | bytes 3145732
  14.2 57.1 %collective-permute-start = (bf16[3072,256]{1,0:T(8,128)(2,1)}, bf16[3072,256]{1,0:T(8,128)(2,1)S(1)}, u32[]{:S(2)}, u32[]{:S(2)}) collective-permute-start(bf16[3072,256]{1,0:T(8,128)(2,1)} %get-tuple-element.33), channel_id=1, source_target_pairs={{0,0},{1,128},{64,64},{65,192},{128,1},{129,129},{192,65},{193,193... | collective-permute-start | bytes 4718600 | tf_op jit(solution)/shard_map/ppermute | solution.py:231
  20.2 95.4 %collective-permute-start.1 = (bf16[3072,256]{1,0:T(8,128)(2,1)}, bf16[3072,256]{1,0:T(8,128)(2,1)}, u32[]{:S(2)}, u32[]{:S(2)}) collective-permute-start(bf16[3072,256]{1,0:T(8,128)(2,1)} %get-tuple-element.37), channel_id=1, source_target_pairs={{0,64},{1,192},{64,0},{65,128},{128,65},{129,193},{192,1},{193,129... | collective-permute-start | bytes 4718600 | tf_op jit(solution)/shard_map/ppermute | solution.py:231
  20.3 23.2 %copy-start.11 = (s32[896]{0:T(1024)}, s32[896]{0:T(1024)S(1)}, u32[]{:S(2)}) copy-start(s32[896]{0:T(1024)S(1)} %fusion.47) | copy-start | bytes 10756
  35.7 38.1 %all-to-all-start.1 = ((bf16[16,56,1024]{2,1,0:T(8,128)(2,1)}), bf16[16,56,1024]{2,1,0:T(8,128)(2,1)}, u32[]{:S(2)}, u32[]{:S(2)}) async-start(bf16[16,56,1024]{2,1,0:T(8,128)(2,1)} %bitcast.10), calls=%async_computation.1 | async-start | bytes 3670016 | tf_op jit(solution)/shard_map/all_to_all | solution.py:253
  71.3 1.2 copy-start.7
  73.8 53.6 %all-to-all-start.3 = ((bf16[8,112,1024]{2,1,0:T(8,128)(2,1)}), bf16[8,112,1024]{2,1,0:T(8,128)(2,1)}, u32[]{:S(2)}, u32[]{:S(2)}) async-start(bf16[8,112,1024]{2,1,0:T(8,128)(2,1)} %bitcast.15), calls=%async_computation.3 | async-start | bytes 3670016 | tf_op jit(solution)/shard_map/all_to_all | solution.py:257
  115.6 1.4 copy-start.8
  117.1 3.4 %copy-start.12 = (s32[896]{0:T(1024)S(1)}, s32[896]{0:T(1024)}, u32[]{:S(2)}) copy-start(s32[896]{0:T(1024)} %copy-done.11) | copy-start | bytes 10756
  120.5 13.9 %collective-permute-start.2 = (bf16[2,3072,256]{2,1,0:T(8,128)(2,1)}, bf16[2,3072,256]{2,1,0:T(8,128)(2,1)}, u32[]{:S(2)}, u32[]{:S(2)}) collective-permute-start(bf16[2,3072,256]{2,1,0:T(8,128)(2,1)} %pad_maximum_fusion.own_ref), channel_id=1, source_target_pairs={{0,1},{1,0},{2,3},{3,2},{4,5},{5,4},{6,7},{7,6},{8,9},{9,8},{10,11... | collective-permute-start | bytes 9437192 | tf_op jit(solution)/shard_map/ppermute | solution.py:273
  127.5 6.9 %copy-start.6 = (bf16[16,128]{1,0:T(8,128)(2,1)S(1)}, bf16[16,128]{1,0:T(8,128)(2,1)}, u32[]{:S(2)}) copy-start(bf16[16,128]{1,0:T(8,128)(2,1)} %shard_map.113._) | copy-start | bytes 12292
  127.5 48.6 %all-to-all-start.2 = ((bf16[8,112,1024]{2,1,0:T(8,128)(2,1)}), bf16[8,112,1024]{2,1,0:T(8,128)(2,1)}, u32[]{:S(2)}, u32[]{:S(2)}) async-start(bf16[8,112,1024]{2,1,0:T(8,128)(2,1)} %bitcast.13), calls=%async_computation.2 | async-start | bytes 3670016 | tf_op jit(solution)/shard_map/all_to_all | solution.py:257
  147.9 1.2 copy-start.3
  149.1 44.6 %copy-start.4 = (bf16[1024,896]{1,0:T(8,128)(2,1)}, bf16[1024,896]{1,0:T(8,128)(2,1)S(1)}, u32[]{:S(2)}) copy-start(bf16[1024,896]{1,0:T(8,128)(2,1)S(1)} %get-tuple-element.46.xt_ref) | copy-start | bytes 5505028
  188.0 43.8 %all-to-all-start.4 = ((bf16[8,112,1024]{2,1,0:T(8,128)(2,1)}), bf16[8,112,1024]{2,1,0:T(8,128)(2,1)}, u32[]{:S(2)}, u32[]{:S(2)}) async-start(bf16[8,112,1024]{2,1,0:T(8,128)(2,1)} %bitcast.29), calls=%async_computation.4 | async-start | bytes 3670016 | tf_op jit(solution)/shard_map/all_to_all | solution.py:257
  199.5 12.2 %collective-permute-start.3 = (bf16[3072,256]{1,0:T(8,128)(2,1)S(1)}, bf16[3072,256]{1,0:T(8,128)(2,1)S(1)}, u32[]{:S(2)}, u32[]{:S(2)}) collective-permute-start(bf16[3072,256]{1,0:T(8,128)(2,1)S(1)} %get-tuple-element.51), channel_id=1, source_target_pairs={{0,1},{1,0},{2,3},{3,2},{4,5},{5,4},{6,7},{7,6},{8,9},{9,8},{10,11... | collective-permute-start | bytes 4718600 | tf_op jit(solution)/shard_map/ppermute | solution.py:283
  203.3 1.5 copy-start.5
  211.7 31.6 %collective-permute-start.5 = (bf16[3072,256]{1,0:T(8,128)(2,1)}, bf16[3072,256]{1,0:T(8,128)(2,1)}, u32[]{:S(2)}, u32[]{:S(2)}) collective-permute-start(bf16[3072,256]{1,0:T(8,128)(2,1)} %get-tuple-element.53), channel_id=1, source_target_pairs={{0,1},{1,0},{2,3},{3,2},{4,5},{5,4},{6,7},{7,6},{8,9},{9,8},{10,11... | collective-permute-start | bytes 4718600 | tf_op jit(solution)/shard_map/ppermute | solution.py:283
  213.3 54.3 %collective-permute-start.4 = (bf16[3072,256]{1,0:T(8,128)(2,1)}, bf16[3072,256]{1,0:T(8,128)(2,1)S(1)}, u32[]{:S(2)}, u32[]{:S(2)}) collective-permute-start(bf16[3072,256]{1,0:T(8,128)(2,1)} %add_convert_fusion.1), channel_id=1, source_target_pairs={{0,0},{128,1},{64,64},{192,65},{1,128},{129,129},{65,192},{193,193... | collective-permute-start | bytes 4718600 | tf_op jit(solution)/shard_map/ppermute | solution.py:285
  236.6 32.4 %all-to-all-start.5 = ((bf16[16,56,1024]{2,1,0:T(8,128)(2,1)}), bf16[16,56,1024]{2,1,0:T(8,128)(2,1)}, u32[]{:S(2)}, u32[]{:S(2)}) async-start(bf16[16,56,1024]{2,1,0:T(8,128)(2,1)} %bitcast.30), calls=%async_computation.5 | async-start | bytes 3670016 | tf_op jit(solution)/shard_map/all_to_all | solution.py:253
  243.3 25.8 %copy-start.14 = (s32[512,1]{0,1:T(1,128)S(1)}, s32[512,1]{0,1:T(1,128)}, u32[]{:S(2)}) copy-start(s32[512,1]{0,1:T(1,128)} %copy-done.13) | copy-start | bytes 6148
  243.3 25.7 %copy-start.16 = (s32[512,1]{0,1:T(1,128)S(1)}, s32[512,1]{0,1:T(1,128)}, u32[]{:S(2)}) copy-start(s32[512,1]{0,1:T(1,128)} %copy-done.15) | copy-start | bytes 6148
  267.5 36.9 %collective-permute-start.6 = (bf16[3072,256]{1,0:T(8,128)(2,1)}, bf16[3072,256]{1,0:T(8,128)(2,1)S(1)}, u32[]{:S(2)}, u32[]{:S(2)}) collective-permute-start(bf16[3072,256]{1,0:T(8,128)(2,1)} %add_convert_fusion), channel_id=1, source_target_pairs={{64,0},{192,1},{0,64},{128,65},{65,128},{193,129},{1,192},{129,193... | collective-permute-start | bytes 4718600 | tf_op jit(solution)/shard_map/ppermute | solution.py:287
